TPU v7x, 32 devices: a whole 2x2x4 slice. The times are simulated.
32 devices in a mesh: gx: 8 (over z, y), gy: 4 (over x, core).
Axes of the slice: x: 2, y: 2, z: 4, core: 2. Of those that a mesh axis runs over, the one named last changes fastest.
Arguments:
- prediction: float32 [64, 64, 256], P('gx', 'gy'), may hold values from 0 to 1
- vessel_mask: int32 [64, 64, 256], P('gx', 'gy'), may hold values from 0 to 1
Outputs:
- grad_pred: float32 [64, 64, 256], P('gx', 'gy')
- loss: float32 [], replicated
All inputs are finite; a program needn't handle non-finite values.
Results may differ from a plain program's by a relative error of at most 0.00002.
Values sent between devices are 32-bit elements; how exact they have to be, the bound alone decides.
No kernel may reach another device: no remote copies, remote signals or barrier semaphores. Data moves between devices by JAX's collectives and lax.ppermute only.
A program may use at most 64 MiB of HBM per device.

v0:
```python
import jax
import jax.numpy as jnp
from jax import lax
from jax.sharding import PartitionSpec as P

ITERS = 3


softness_factor = 0.1


def extended(block, sides, width):
    for axis, dim in sides:
        count = lax.axis_size(axis)
        forward = [(i, i + 1) for i in range(count - 1)]
        backward = [(target, source) for source, target in forward]
        low = lax.ppermute(
            lax.slice_in_dim(block, block.shape[dim] - width, None, axis=dim), axis, forward
        )
        high = lax.ppermute(lax.slice_in_dim(block, 0, width, axis=dim), axis, backward)
        block = jnp.concatenate([low, block, high], axis=dim)
    return block


def window_sum(padded):
    along = padded[:, :-2] + padded[:, 1:-1] + padded[:, 2:]
    across = along[:, :, :-2] + along[:, :, 1:-1] + along[:, :, 2:]
    blank = jnp.zeros_like(across[..., :1])
    return (
        across
        + jnp.concatenate([across[..., 1:], blank], -1)
        + jnp.concatenate([blank, across[..., :-1]], -1)
    )


def smooth_rect(value_entries):
    return softness_factor * jax.nn.softplus(value_entries / softness_factor)


def rect_slope(value_entries):
    return jax.nn.sigmoid(value_entries / softness_factor)


def local(prediction, vessel_mask):
    rows_here, cols_here, depth_here = prediction.shape
    levels = ITERS + 1
    mask_field = vessel_mask.astype(jnp.float32)
    field_stack = jnp.stack([prediction, mask_field])
    image_batch = [field_stack]
    opened = []
    erode_saved = []
    dilate_saved = []
    for level_index in range(levels):
        power_term = jnp.exp(-image_batch[-1] / softness_factor)
        padded = extended(power_term, (("gx", 1), ("gy", 2)), 1)
        running_totals = window_sum(padded)
        image_batch.append(-softness_factor * jnp.log(running_totals))
        erode_saved.append((power_term[0], running_totals[0]))
    increasing_part = jnp.exp(jnp.concatenate(image_batch[1:], 0) / softness_factor)
    padded = extended(increasing_part, (("gx", 1), ("gy", 2)), 1)
    dispersal = window_sum(padded)
    opening_stack = softness_factor * jnp.log(dispersal)
    for level_index in range(levels):
        opened.append(opening_stack[2 * level_index : 2 * level_index + 2])
        dilate_saved.append((increasing_part[2 * level_index], dispersal[2 * level_index]))
    skeleton = smooth_rect(image_batch[0] - opened[0])
    skeleton_list = [skeleton]
    delta_list = [skeleton]
    for level_index in range(1, ITERS + 1):
        delta = smooth_rect(image_batch[level_index] - opened[level_index])
        skeleton = skeleton + smooth_rect(delta - skeleton * delta)
        skeleton_list.append(skeleton)
        delta_list.append(delta)
    pred_skel = skeleton[0]
    mask_skel = skeleton[1]
    intersection_pred, mass_pred, intersection_mask, mass_mask = lax.psum(
        (
            jnp.sum(pred_skel * mask_field),
            jnp.sum(pred_skel),
            jnp.sum(mask_skel * prediction),
            jnp.sum(mask_skel),
        ),
        ("gx", "gy"),
    )
    precision = (intersection_pred + 1.0) / (mass_pred + 1.0)
    sensitivity = (intersection_mask + 1.0) / (mass_mask + 1.0)
    paired = precision + sensitivity
    loss_value = 1.0 - 2.0 * precision * sensitivity / paired
    slope_prec = -2.0 * sensitivity * sensitivity / (paired * paired)
    slope_sens = -2.0 * precision * precision / (paired * paired)
    coef_intersection = slope_prec / (mass_pred + 1.0)
    coef_mass = -slope_prec * (intersection_pred + 1.0) / ((mass_pred + 1.0) * (mass_pred + 1.0))
    coef_cross = slope_sens / (mass_mask + 1.0)
    seeds = (coef_intersection * mask_field + coef_mass)[None]
    field_count = seeds.shape[0]
    grad_skel = seeds
    grad_images = [None] * (levels + 1)
    grad_opened = [None] * levels
    for level_index in range(ITERS, 0, -1):
        previous = skeleton_list[level_index - 1][0]
        delta = delta_list[level_index][0]
        grad_inner = grad_skel * rect_slope(delta - previous * delta)
        grad_input = (
            grad_inner
            * (1.0 - previous)
            * rect_slope(image_batch[level_index][0] - opened[level_index][0])
        )
        grad_images[level_index] = grad_input
        grad_opened[level_index] = -grad_input
        grad_skel = grad_skel - grad_inner * delta
    grad_input = grad_skel * rect_slope(image_batch[0][0] - opened[0][0])
    grad_images[0] = grad_input
    grad_opened[0] = -grad_input
    grad_images[levels] = jnp.zeros_like(seeds)
    scaled = jnp.concatenate(
        [grad_opened[level_index] / dilate_saved[level_index][1] for level_index in range(levels)],
        0,
    )
    padded = extended(scaled, (("gx", 1), ("gy", 2)), 1)
    spread_back = window_sum(padded)
    for level_index in range(levels):
        grad_images[level_index + 1] = (
            grad_images[level_index + 1]
            + dilate_saved[level_index][0]
            * spread_back[level_index * field_count : (level_index + 1) * field_count]
        )
    for level_index in range(levels, 0, -1):
        power_term, running_totals = erode_saved[level_index - 1]
        padded = extended(grad_images[level_index] / running_totals, (("gx", 1), ("gy", 2)), 1)
        grad_images[level_index - 1] = grad_images[level_index - 1] + power_term * window_sum(
            padded
        )
    pulled = grad_images[0]
    gradient = pulled[0]
    gradient = gradient + coef_cross * mask_skel
    cell_count = float(
        rows_here * cols_here * depth_here * lax.axis_size("gx") * lax.axis_size("gy")
    )
    return (gradient * cell_count, loss_value)


def solution(mesh):
    placed = (P("gx", "gy", None), P("gx", "gy", None))
    return jax.shard_map(
        local, mesh=mesh, in_specs=placed, out_specs=(P("gx", "gy", None), P()), check_vma=False
    )
```

profile of v0, /device:TPU:0, one launch (start us, length us, event | category | flops | bytes accessed | tf_op | source)
XLA Modules:
  0.0 231.6 jit_solution(16532209787689238658)
XLA Ops:
  2.5 4.9 %collective-permute-start = (f32[2,1,16,256]{3,2,1,0:T(8,128)S(1)}, f32[2,1,16,256]{3,2,1,0:T(8,128)S(1)}, u32[]{:S(2)}, u32[]{:S(2)}) collective-permute-start(f32[2,1,16,256]{3,2,1,0:T(8,128)S(1)} %get-tuple-element.75), channel_id=1, source_target_pairs={{0,4},{4,8},{8,12},{12,16},{16,20},{20,24},{24,28},{1,5},{5,9},{9,... | collective-permute-start | bytes 98312 | tf_op jit(solution)/shard_map/ppermute | solution.py:17
  9.0 4.2 %collective-permute-done.1 = f32[2,1,16,256]{3,2,1,0:T(8,128)S(1)} collective-permute-done((f32[2,1,16,256]{3,2,1,0:T(8,128)S(1)}, f32[2,1,16,256]{3,2,1,0:T(8,128)S(1)}, u32[]{:S(2)}, u32[]{:S(2)}) %collective-permute-start.1) | collective-permute-done | bytes 32800 | tf_op jit(solution)/shard_map/ppermute | solution.py:20
  15.8 3.5 %collective-permute-done.3 = f32[2,10,1,256]{3,2,1,0:T(1,128)S(1)} collective-permute-done((f32[2,10,1,256]{3,2,1,0:T(1,128)S(1)}, f32[2,10,1,256]{3,2,1,0:T(1,128)S(1)}, u32[]{:S(2)}, u32[]{:S(2)}) %collective-permute-start.3) | collective-permute-done | bytes 20512 | tf_op jit(solution)/shard_map/ppermute | solution.py:20
  20.0 4.3 %collective-permute-start.4 = (f32[2,1,16,256]{3,2,1,0:T(8,128)S(1)}, f32[2,1,16,256]{3,2,1,0:T(8,128)S(1)}, u32[]{:S(2)}, u32[]{:S(2)}) collective-permute-start(f32[2,1,16,256]{3,2,1,0:T(8,128)S(1)} %get-tuple-element.71), channel_id=1, source_target_pairs={{0,4},{4,8},{8,12},{12,16},{16,20},{20,24},{24,28},{1,5},{5,9},{9,... | collective-permute-start | bytes 98312 | tf_op jit(solution)/shard_map/ppermute | solution.py:17
  25.9 4.2 %collective-permute-done.5 = f32[2,1,16,256]{3,2,1,0:T(8,128)S(1)} collective-permute-done((f32[2,1,16,256]{3,2,1,0:T(8,128)S(1)}, f32[2,1,16,256]{3,2,1,0:T(8,128)S(1)}, u32[]{:S(2)}, u32[]{:S(2)}) %collective-permute-start.5) | collective-permute-done | bytes 32800 | tf_op jit(solution)/shard_map/ppermute | solution.py:20
  30.1 3.0 %collective-permute-start.6 = (f32[2,10,1,256]{3,2,1,0:T(1,128)S(1)}, f32[2,10,1,256]{3,2,1,0:T(1,128)S(1)}, u32[]{:S(2)}, u32[]{:S(2)}) collective-permute-start(f32[2,10,1,256]{3,2,1,0:T(1,128)S(1)} %get-tuple-element.57), channel_id=1, source_target_pairs={{0,1},{1,2},{2,3},{4,5},{5,6},{6,7},{8,9},{9,10},{10,11},{12,13},{... | collective-permute-start | bytes 61448 | tf_op jit(solution)/shard_map/ppermute | solution.py:17
  37.8 3.4 %collective-permute-start.8 = (f32[2,1,16,256]{3,2,1,0:T(8,128)S(1)}, f32[2,1,16,256]{3,2,1,0:T(8,128)S(1)}, u32[]{:S(2)}, u32[]{:S(2)}) collective-permute-start(f32[2,1,16,256]{3,2,1,0:T(8,128)S(1)} %get-tuple-element.67), channel_id=1, source_target_pairs={{0,4},{4,8},{8,12},{12,16},{16,20},{20,24},{24,28},{1,5},{5,9},{9,... | collective-permute-start | bytes 98312 | tf_op jit(solution)/shard_map/ppermute | solution.py:17
  42.8 4.2 %collective-permute-done.9 = f32[2,1,16,256]{3,2,1,0:T(8,128)S(1)} collective-permute-done((f32[2,1,16,256]{3,2,1,0:T(8,128)S(1)}, f32[2,1,16,256]{3,2,1,0:T(8,128)S(1)}, u32[]{:S(2)}, u32[]{:S(2)}) %collective-permute-start.9) | collective-permute-done | bytes 32800 | tf_op jit(solution)/shard_map/ppermute | solution.py:20
  54.7 4.3 %collective-permute-start.12 = (f32[2,1,16,256]{3,2,1,0:T(8,128)S(1)}, f32[2,1,16,256]{3,2,1,0:T(8,128)S(1)}, u32[]{:S(2)}, u32[]{:S(2)}) collective-permute-start(f32[2,1,16,256]{3,2,1,0:T(8,128)S(1)} %get-tuple-element.63), channel_id=1, source_target_pairs={{0,4},{4,8},{8,12},{12,16},{16,20},{20,24},{24,28},{1,5},{5,9},{9,... | collective-permute-start | bytes 98312 | tf_op jit(solution)/shard_map/ppermute | solution.py:17
  60.6 4.2 %collective-permute-done.13 = f32[2,1,16,256]{3,2,1,0:T(8,128)S(1)} collective-permute-done((f32[2,1,16,256]{3,2,1,0:T(8,128)S(1)}, f32[2,1,16,256]{3,2,1,0:T(8,128)S(1)}, u32[]{:S(2)}, u32[]{:S(2)}) %collective-permute-start.13) | collective-permute-done | bytes 32800 | tf_op jit(solution)/shard_map/ppermute | solution.py:20
  73.3 3.4 %collective-permute-start.16 = (f32[8,1,16,256]{3,2,1,0:T(8,128)S(1)}, f32[8,1,16,256]{3,2,1,0:T(8,128)S(1)}, u32[]{:S(2)}, u32[]{:S(2)}) collective-permute-start(f32[8,1,16,256]{3,2,1,0:T(8,128)S(1)} %get-tuple-element.45), channel_id=1, source_target_pairs={{0,4},{4,8},{8,12},{12,16},{16,20},{20,24},{24,28},{1,5},{5,9},{9,... | collective-permute-start | bytes 393224 | tf_op jit(solution)/shard_map/ppermute | solution.py:17
  79.2 4.5 %collective-permute-done.17 = f32[8,1,16,256]{3,2,1,0:T(8,128)S(1)} collective-permute-done((f32[8,1,16,256]{3,2,1,0:T(8,128)S(1)}, f32[8,1,16,256]{3,2,1,0:T(8,128)S(1)}, u32[]{:S(2)}, u32[]{:S(2)}) %collective-permute-start.17) | collective-permute-done | bytes 131104 | tf_op jit(solution)/shard_map/ppermute | solution.py:20
  83.8 3.0 %collective-permute-start.18 = (f32[8,10,1,256]{3,2,1,0:T(1,128)S(1)}, f32[8,10,1,256]{3,2,1,0:T(1,128)S(1)}, u32[]{:S(2)}, u32[]{:S(2)}) collective-permute-start(f32[8,10,1,256]{3,2,1,0:T(1,128)S(1)} %get-tuple-element.41), channel_id=1, source_target_pairs={{0,1},{1,2},{2,3},{4,5},{5,6},{6,7},{8,9},{9,10},{10,11},{12,13},{... | collective-permute-start | bytes 245768 | tf_op jit(solution)/shard_map/ppermute | solution.py:17
  97.2 41.6 %all-reduce.20 = (f32[]{:T(128)}, f32[]{:T(128)}, f32[]{:T(128)}, f32[]{:T(128)}) all-reduce(f32[]{:T(128)} %get-tuple-element.5, f32[]{:T(128)} %get-tuple-element.3, f32[]{:T(128)} %get-tuple-element.4, f32[]{:T(128)} %get-tuple-element.2), channel_id=1, replica_groups=mesh['gx'=8,'gy'=4] {'gx','gy'}, use_global_device_ids=true, to_apply=%region_1.2 | all-reduce | flops 4 | bytes 32 | tf_op jit(solution)/shard_map/psum | solution.py:76
  145.2 4.4 %collective-permute-start.20 = (f32[4,1,16,256]{3,2,1,0:T(8,128)S(1)}, f32[4,1,16,256]{3,2,1,0:T(8,128)S(1)}, u32[]{:S(2)}, u32[]{:S(2)}) collective-permute-start(f32[4,1,16,256]{3,2,1,0:T(8,128)S(1)} %get-tuple-element.51), channel_id=1, source_target_pairs={{0,4},{4,8},{8,12},{12,16},{16,20},{20,24},{24,28},{1,5},{5,9},{9,... | collective-permute-start | bytes 196616 | tf_op jit(solution)/shard_map/ppermute | solution.py:17
  151.6 4.3 %collective-permute-done.21 = f32[4,1,16,256]{3,2,1,0:T(8,128)S(1)} collective-permute-done((f32[4,1,16,256]{3,2,1,0:T(8,128)S(1)}, f32[4,1,16,256]{3,2,1,0:T(8,128)S(1)}, u32[]{:S(2)}, u32[]{:S(2)}) %collective-permute-start.21) | collective-permute-done | bytes 65568 | tf_op jit(solution)/shard_map/ppermute | solution.py:20
  158.5 3.2 %collective-permute-done.23 = f32[4,10,1,256]{3,2,1,0:T(1,128)S(1)} collective-permute-done((f32[4,10,1,256]{3,2,1,0:T(1,128)S(1)}, f32[4,10,1,256]{3,2,1,0:T(1,128)S(1)}, u32[]{:S(2)}, u32[]{:S(2)}) %collective-permute-start.23) | collective-permute-done | bytes 40992 | tf_op jit(solution)/shard_map/ppermute | solution.py:20
  163.3 4.8 %collective-permute-start.24 = (f32[1,1,16,256]{3,2,1,0:T(8,128)S(1)}, f32[1,1,16,256]{3,2,1,0:T(8,128)S(1)}, u32[]{:S(2)}, u32[]{:S(2)}) collective-permute-start(f32[1,1,16,256]{3,2,1,0:T(8,128)S(1)} %get-tuple-element.99), channel_id=1, source_target_pairs={{0,4},{4,8},{8,12},{12,16},{16,20},{20,24},{24,28},{1,5},{5,9},{9,... | collective-permute-start | bytes 49160 | tf_op jit(solution)/shard_map/ppermute | solution.py:17
  169.6 4.2 %collective-permute-done.25 = f32[1,1,16,256]{3,2,1,0:T(8,128)S(1)} collective-permute-done((f32[1,1,16,256]{3,2,1,0:T(8,128)S(1)}, f32[1,1,16,256]{3,2,1,0:T(8,128)S(1)}, u32[]{:S(2)}, u32[]{:S(2)}) %collective-permute-start.25) | collective-permute-done | bytes 16416 | tf_op jit(solution)/shard_map/ppermute | solution.py:20
  173.8 3.2 %collective-permute-start.26 = (f32[1,10,1,256]{3,2,1,0:T(1,128)S(1)}, f32[1,10,1,256]{3,2,1,0:T(1,128)S(1)}, u32[]{:S(2)}, u32[]{:S(2)}) collective-permute-start(f32[1,10,1,256]{3,2,1,0:T(1,128)S(1)} %get-tuple-element.83), channel_id=1, source_target_pairs={{0,1},{1,2},{2,3},{4,5},{5,6},{6,7},{8,9},{9,10},{10,11},{12,13},{... | collective-permute-start | bytes 30728 | tf_op jit(solution)/shard_map/ppermute | solution.py:17
  185.6 4.2 %collective-permute-done.29 = f32[1,1,16,256]{3,2,1,0:T(8,128)S(1)} collective-permute-done((f32[1,1,16,256]{3,2,1,0:T(8,128)S(1)}, f32[1,1,16,256]{3,2,1,0:T(8,128)S(1)}, u32[]{:S(2)}, u32[]{:S(2)}) %collective-permute-start.29) | collective-permute-done | bytes 16416 | tf_op jit(solution)/shard_map/ppermute | solution.py:20
  197.1 4.0 %collective-permute-start.32 = (f32[1,1,16,256]{3,2,1,0:T(8,128)S(1)}, f32[1,1,16,256]{3,2,1,0:T(8,128)S(1)}, u32[]{:S(2)}, u32[]{:S(2)}) collective-permute-start(f32[1,1,16,256]{3,2,1,0:T(8,128)S(1)} %get-tuple-element.91), channel_id=1, source_target_pairs={{0,4},{4,8},{8,12},{12,16},{16,20},{20,24},{24,28},{1,5},{5,9},{9,... | collective-permute-start | bytes 49160 | tf_op jit(solution)/shard_map/ppermute | solution.py:17
  202.6 4.2 %collective-permute-done.33 = f32[1,1,16,256]{3,2,1,0:T(8,128)S(1)} collective-permute-done((f32[1,1,16,256]{3,2,1,0:T(8,128)S(1)}, f32[1,1,16,256]{3,2,1,0:T(8,128)S(1)}, u32[]{:S(2)}, u32[]{:S(2)}) %collective-permute-start.33) | collective-permute-done | bytes 16416 | tf_op jit(solution)/shard_map/ppermute | solution.py:20
  218.3 4.2 %collective-permute-done.37 = f32[1,1,16,256]{3,2,1,0:T(8,128)S(1)} collective-permute-done((f32[1,1,16,256]{3,2,1,0:T(8,128)S(1)}, f32[1,1,16,256]{3,2,1,0:T(8,128)S(1)}, u32[]{:S(2)}, u32[]{:S(2)}) %collective-permute-start.37) | collective-permute-done | bytes 16416 | tf_op jit(solution)/shard_map/ppermute | solution.py:20
  (177 shorter events, 92.2 us)
Async XLA Ops:
  2.5 6.5 %collective-permute-start = (f32[2,1,16,256]{3,2,1,0:T(8,128)S(1)}, f32[2,1,16,256]{3,2,1,0:T(8,128)S(1)}, u32[]{:S(2)}, u32[]{:S(2)}) collective-permute-start(f32[2,1,16,256]{3,2,1,0:T(8,128)S(1)} %get-tuple-element.75), channel_id=1, source_target_pairs={{0,4},{4,8},{8,12},{12,16},{16,20},{20,24},{24,28},{1,5},{5,9},{9,... | collective-permute-start | bytes 98312 | tf_op jit(solution)/shard_map/ppermute | solution.py:17
  7.4 5.8 %collective-permute-start.1 = (f32[2,1,16,256]{3,2,1,0:T(8,128)S(1)}, f32[2,1,16,256]{3,2,1,0:T(8,128)S(1)}, u32[]{:S(2)}, u32[]{:S(2)}) collective-permute-start(f32[2,1,16,256]{3,2,1,0:T(8,128)S(1)} %get-tuple-element.76), channel_id=1, source_target_pairs={{4,0},{8,4},{12,8},{16,12},{20,16},{24,20},{28,24},{5,1},{9,5},{13... | collective-permute-start | bytes 98312 | tf_op jit(solution)/shard_map/ppermute | solution.py:20
  14.5 4.8 %collective-permute-start.3 = (f32[2,10,1,256]{3,2,1,0:T(1,128)S(1)}, f32[2,10,1,256]{3,2,1,0:T(1,128)S(1)}, u32[]{:S(2)}, u32[]{:S(2)}) collective-permute-start(f32[2,10,1,256]{3,2,1,0:T(1,128)S(1)} %get-tuple-element.60), channel_id=1, source_target_pairs={{1,0},{2,1},{3,2},{5,4},{6,5},{7,6},{9,8},{10,9},{11,10},{13,12},{... | collective-permute-start | bytes 61448 | tf_op jit(solution)/shard_map/ppermute | solution.py:20
  20.0 5.9 %collective-permute-start.4 = (f32[2,1,16,256]{3,2,1,0:T(8,128)S(1)}, f32[2,1,16,256]{3,2,1,0:T(8,128)S(1)}, u32[]{:S(2)}, u32[]{:S(2)}) collective-permute-start(f32[2,1,16,256]{3,2,1,0:T(8,128)S(1)} %get-tuple-element.71), channel_id=1, source_target_pairs={{0,4},{4,8},{8,12},{12,16},{16,20},{20,24},{24,28},{1,5},{5,9},{9,... | collective-permute-start | bytes 98312 | tf_op jit(solution)/shard_map/ppermute | solution.py:17
  24.3 5.8 %collective-permute-start.5 = (f32[2,1,16,256]{3,2,1,0:T(8,128)S(1)}, f32[2,1,16,256]{3,2,1,0:T(8,128)S(1)}, u32[]{:S(2)}, u32[]{:S(2)}) collective-permute-start(f32[2,1,16,256]{3,2,1,0:T(8,128)S(1)} %get-tuple-element.72), channel_id=1, source_target_pairs={{4,0},{8,4},{12,8},{16,12},{20,16},{24,20},{28,24},{5,1},{9,5},{13... | collective-permute-start | bytes 98312 | tf_op jit(solution)/shard_map/ppermute | solution.py:20
  30.1 4.3 %collective-permute-start.6 = (f32[2,10,1,256]{3,2,1,0:T(1,128)S(1)}, f32[2,10,1,256]{3,2,1,0:T(1,128)S(1)}, u32[]{:S(2)}, u32[]{:S(2)}) collective-permute-start(f32[2,10,1,256]{3,2,1,0:T(1,128)S(1)} %get-tuple-element.57), channel_id=1, source_target_pairs={{0,1},{1,2},{2,3},{4,5},{5,6},{6,7},{8,9},{9,10},{10,11},{12,13},{... | collective-permute-start | bytes 61448 | tf_op jit(solution)/shard_map/ppermute | solution.py:17
  37.8 5.0 %collective-permute-start.8 = (f32[2,1,16,256]{3,2,1,0:T(8,128)S(1)}, f32[2,1,16,256]{3,2,1,0:T(8,128)S(1)}, u32[]{:S(2)}, u32[]{:S(2)}) collective-permute-start(f32[2,1,16,256]{3,2,1,0:T(8,128)S(1)} %get-tuple-element.67), channel_id=1, source_target_pairs={{0,4},{4,8},{8,12},{12,16},{16,20},{20,24},{24,28},{1,5},{5,9},{9,... | collective-permute-start | bytes 98312 | tf_op jit(solution)/shard_map/ppermute | solution.py:17
  41.2 5.8 %collective-permute-start.9 = (f32[2,1,16,256]{3,2,1,0:T(8,128)S(1)}, f32[2,1,16,256]{3,2,1,0:T(8,128)S(1)}, u32[]{:S(2)}, u32[]{:S(2)}) collective-permute-start(f32[2,1,16,256]{3,2,1,0:T(8,128)S(1)} %get-tuple-element.68), channel_id=1, source_target_pairs={{4,0},{8,4},{12,8},{16,12},{20,16},{24,20},{28,24},{5,1},{9,5},{13... | collective-permute-start | bytes 98312 | tf_op jit(solution)/shard_map/ppermute | solution.py:20
  54.7 5.9 %collective-permute-start.12 = (f32[2,1,16,256]{3,2,1,0:T(8,128)S(1)}, f32[2,1,16,256]{3,2,1,0:T(8,128)S(1)}, u32[]{:S(2)}, u32[]{:S(2)}) collective-permute-start(f32[2,1,16,256]{3,2,1,0:T(8,128)S(1)} %get-tuple-element.63), channel_id=1, source_target_pairs={{0,4},{4,8},{8,12},{12,16},{16,20},{20,24},{24,28},{1,5},{5,9},{9,... | collective-permute-start | bytes 98312 | tf_op jit(solution)/shard_map/ppermute | solution.py:17
  59.0 5.8 %collective-permute-start.13 = (f32[2,1,16,256]{3,2,1,0:T(8,128)S(1)}, f32[2,1,16,256]{3,2,1,0:T(8,128)S(1)}, u32[]{:S(2)}, u32[]{:S(2)}) collective-permute-start(f32[2,1,16,256]{3,2,1,0:T(8,128)S(1)} %get-tuple-element.64), channel_id=1, source_target_pairs={{4,0},{8,4},{12,8},{16,12},{20,16},{24,20},{28,24},{5,1},{9,5},{13... | collective-permute-start | bytes 98312 | tf_op jit(solution)/shard_map/ppermute | solution.py:20
  73.3 5.9 %collective-permute-start.16 = (f32[8,1,16,256]{3,2,1,0:T(8,128)S(1)}, f32[8,1,16,256]{3,2,1,0:T(8,128)S(1)}, u32[]{:S(2)}, u32[]{:S(2)}) collective-permute-start(f32[8,1,16,256]{3,2,1,0:T(8,128)S(1)} %get-tuple-element.45), channel_id=1, source_target_pairs={{0,4},{4,8},{8,12},{12,16},{16,20},{20,24},{24,28},{1,5},{5,9},{9,... | collective-permute-start | bytes 393224 | tf_op jit(solution)/shard_map/ppermute | solution.py:17
  76.7 7.0 %collective-permute-start.17 = (f32[8,1,16,256]{3,2,1,0:T(8,128)S(1)}, f32[8,1,16,256]{3,2,1,0:T(8,128)S(1)}, u32[]{:S(2)}, u32[]{:S(2)}) collective-permute-start(f32[8,1,16,256]{3,2,1,0:T(8,128)S(1)} %get-tuple-element.46), channel_id=1, source_target_pairs={{4,0},{8,4},{12,8},{16,12},{20,16},{24,20},{28,24},{5,1},{9,5},{13... | collective-permute-start | bytes 393224 | tf_op jit(solution)/shard_map/ppermute | solution.py:20
  83.8 4.3 %collective-permute-start.18 = (f32[8,10,1,256]{3,2,1,0:T(1,128)S(1)}, f32[8,10,1,256]{3,2,1,0:T(1,128)S(1)}, u32[]{:S(2)}, u32[]{:S(2)}) collective-permute-start(f32[8,10,1,256]{3,2,1,0:T(1,128)S(1)} %get-tuple-element.41), channel_id=1, source_target_pairs={{0,1},{1,2},{2,3},{4,5},{5,6},{6,7},{8,9},{9,10},{10,11},{12,13},{... | collective-permute-start | bytes 245768 | tf_op jit(solution)/shard_map/ppermute | solution.py:17
  145.2 6.3 %collective-permute-start.20 = (f32[4,1,16,256]{3,2,1,0:T(8,128)S(1)}, f32[4,1,16,256]{3,2,1,0:T(8,128)S(1)}, u32[]{:S(2)}, u32[]{:S(2)}) collective-permute-start(f32[4,1,16,256]{3,2,1,0:T(8,128)S(1)} %get-tuple-element.51), channel_id=1, source_target_pairs={{0,4},{4,8},{8,12},{12,16},{16,20},{20,24},{24,28},{1,5},{5,9},{9,... | collective-permute-start | bytes 196616 | tf_op jit(solution)/shard_map/ppermute | solution.py:17
  149.7 6.2 %collective-permute-start.21 = (f32[4,1,16,256]{3,2,1,0:T(8,128)S(1)}, f32[4,1,16,256]{3,2,1,0:T(8,128)S(1)}, u32[]{:S(2)}, u32[]{:S(2)}) collective-permute-start(f32[4,1,16,256]{3,2,1,0:T(8,128)S(1)} %get-tuple-element.52), channel_id=1, source_target_pairs={{4,0},{8,4},{12,8},{16,12},{20,16},{24,20},{28,24},{5,1},{9,5},{13... | collective-permute-start | bytes 196616 | tf_op jit(solution)/shard_map/ppermute | solution.py:20
  157.2 4.6 %collective-permute-start.23 = (f32[4,10,1,256]{3,2,1,0:T(1,128)S(1)}, f32[4,10,1,256]{3,2,1,0:T(1,128)S(1)}, u32[]{:S(2)}, u32[]{:S(2)}) collective-permute-start(f32[4,10,1,256]{3,2,1,0:T(1,128)S(1)} %get-tuple-element.48), channel_id=1, source_target_pairs={{1,0},{2,1},{3,2},{5,4},{6,5},{7,6},{9,8},{10,9},{11,10},{13,12},{... | collective-permute-start | bytes 122888 | tf_op jit(solution)/shard_map/ppermute | solution.py:20
  163.3 6.3 %collective-permute-start.24 = (f32[1,1,16,256]{3,2,1,0:T(8,128)S(1)}, f32[1,1,16,256]{3,2,1,0:T(8,128)S(1)}, u32[]{:S(2)}, u32[]{:S(2)}) collective-permute-start(f32[1,1,16,256]{3,2,1,0:T(8,128)S(1)} %get-tuple-element.99), channel_id=1, source_target_pairs={{0,4},{4,8},{8,12},{12,16},{16,20},{20,24},{24,28},{1,5},{5,9},{9,... | collective-permute-start | bytes 49160 | tf_op jit(solution)/shard_map/ppermute | solution.py:17
  168.1 5.6 %collective-permute-start.25 = (f32[1,1,16,256]{3,2,1,0:T(8,128)S(1)}, f32[1,1,16,256]{3,2,1,0:T(8,128)S(1)}, u32[]{:S(2)}, u32[]{:S(2)}) collective-permute-start(f32[1,1,16,256]{3,2,1,0:T(8,128)S(1)} %get-tuple-element.100), channel_id=1, source_target_pairs={{4,0},{8,4},{12,8},{16,12},{20,16},{24,20},{28,24},{5,1},{9,5},{13... | collective-permute-start | bytes 49160 | tf_op jit(solution)/shard_map/ppermute | solution.py:20
  173.8 4.5 %collective-permute-start.26 = (f32[1,10,1,256]{3,2,1,0:T(1,128)S(1)}, f32[1,10,1,256]{3,2,1,0:T(1,128)S(1)}, u32[]{:S(2)}, u32[]{:S(2)}) collective-permute-start(f32[1,10,1,256]{3,2,1,0:T(1,128)S(1)} %get-tuple-element.83), channel_id=1, source_target_pairs={{0,1},{1,2},{2,3},{4,5},{5,6},{6,7},{8,9},{9,10},{10,11},{12,13},{... | collective-permute-start | bytes 30728 | tf_op jit(solution)/shard_map/ppermute | solution.py:17
  184.2 5.6 %collective-permute-start.29 = (f32[1,1,16,256]{3,2,1,0:T(8,128)S(1)}, f32[1,1,16,256]{3,2,1,0:T(8,128)S(1)}, u32[]{:S(2)}, u32[]{:S(2)}) collective-permute-start(f32[1,1,16,256]{3,2,1,0:T(8,128)S(1)} %get-tuple-element.96), channel_id=1, source_target_pairs={{4,0},{8,4},{12,8},{16,12},{20,16},{24,20},{28,24},{5,1},{9,5},{13... | collective-permute-start | bytes 49160 | tf_op jit(solution)/shard_map/ppermute | solution.py:20
  197.1 5.4 %collective-permute-start.32 = (f32[1,1,16,256]{3,2,1,0:T(8,128)S(1)}, f32[1,1,16,256]{3,2,1,0:T(8,128)S(1)}, u32[]{:S(2)}, u32[]{:S(2)}) collective-permute-start(f32[1,1,16,256]{3,2,1,0:T(8,128)S(1)} %get-tuple-element.91), channel_id=1, source_target_pairs={{0,4},{4,8},{8,12},{12,16},{16,20},{20,24},{24,28},{1,5},{5,9},{9,... | collective-permute-start | bytes 49160 | tf_op jit(solution)/shard_map/ppermute | solution.py:17
  201.1 5.6 %collective-permute-start.33 = (f32[1,1,16,256]{3,2,1,0:T(8,128)S(1)}, f32[1,1,16,256]{3,2,1,0:T(8,128)S(1)}, u32[]{:S(2)}, u32[]{:S(2)}) collective-permute-start(f32[1,1,16,256]{3,2,1,0:T(8,128)S(1)} %get-tuple-element.92), channel_id=1, source_target_pairs={{4,0},{8,4},{12,8},{16,12},{20,16},{24,20},{28,24},{5,1},{9,5},{13... | collective-permute-start | bytes 49160 | tf_op jit(solution)/shard_map/ppermute | solution.py:20
  216.9 5.6 %collective-permute-start.37 = (f32[1,1,16,256]{3,2,1,0:T(8,128)S(1)}, f32[1,1,16,256]{3,2,1,0:T(8,128)S(1)}, u32[]{:S(2)}, u32[]{:S(2)}) collective-permute-start(f32[1,1,16,256]{3,2,1,0:T(8,128)S(1)} %get-tuple-element.88), channel_id=1, source_target_pairs={{4,0},{8,4},{12,8},{16,12},{20,16},{24,20},{28,24},{5,1},{9,5},{13... | collective-permute-start | bytes 49160 | tf_op jit(solution)/shard_map/ppermute | solution.py:20
  222.6 4.3 %collective-permute-start.38 = (f32[1,10,1,256]{3,2,1,0:T(1,128)S(1)}, f32[1,10,1,256]{3,2,1,0:T(1,128)S(1)}, u32[]{:S(2)}, u32[]{:S(2)}) collective-permute-start(f32[1,10,1,256]{3,2,1,0:T(1,128)S(1)} %get-tuple-element.77), channel_id=1, source_target_pairs={{0,1},{1,2},{2,3},{4,5},{5,6},{6,7},{8,9},{9,10},{10,11},{12,13},{... | collective-permute-start | bytes 30728 | tf_op jit(solution)/shard_map/ppermute | solution.py:17
  (35 other events, 425.6 us)
where the time goes:
time: 235 us; the launch traced here: 232 us
  starting transfers between devices  91.6 us (39%)
  waiting for transfers between devices  74.3 us (32%)
  blocking collectives  41.6 us (18%)
  other arithmetic  16.1 us (7%)
  between operations  5.72 us (2%)
    ppermute x20, waiting for transfers between devices, extended(): lax.ppermute(lax.slice_in_dim(block, 0, width, axis=dim), axis, backward)  70.9 us
    ppermute x20, starting transfers between devices, extended(): lax.ppermute(lax.slice_in_dim(block, block.shape[dim] - width, None, axis...  65.7 us
    psum x1, blocking collectives, local(): lax.psum((jnp.sum(pred_skel * mask_field), jnp.sum(pred_skel), jnp.sum(ma...  41.6 us
    ppermute x20, starting transfers between devices, extended(): lax.ppermute(lax.slice_in_dim(block, 0, width, axis=dim), axis, backward)  25.8 us
  transfers between devices with their start and end apart: 40, of which 30 were waited for; matrix products, arithmetic and copies ran while one was open for 0% of the time, Pallas kernels for 0%

commit v1 on v0

v1 whole, which is shorter than its diff:
```python
import jax
import jax.numpy as jnp
from jax import lax
from jax.sharding import PartitionSpec as P

ITERS = 3
LEVELS = ITERS + 1
REACH = LEVELS + 1
softness_factor = 0.1


def shifted(block, axis, step):
    count = lax.axis_size(axis)
    pairs = [(i, i + step) for i in range(count) if 0 <= i + step < count]
    return lax.ppermute(block, axis, pairs)


def swapped(block, axis):
    count = lax.axis_size(axis)
    return lax.ppermute(block, axis, [(i, i ^ 1) for i in range(count)])


def with_halo(prediction, mask_field):
    rows, cols, _ = prediction.shape
    wide, thin = 2 * REACH, REACH
    odd = lax.rem(lax.axis_index("gx"), 2) == 1
    other = swapped(jnp.concatenate([prediction, mask_field], 0), "gx")
    other_pred, other_mask = other[:rows], other[rows:]
    low_pred = jnp.where(odd, other_pred, prediction)
    high_pred = jnp.where(odd, prediction, other_pred)
    low_mask = jnp.where(odd, other_mask, mask_field)
    high_mask = jnp.where(odd, mask_field, other_mask)
    pair_pred = jnp.concatenate([low_pred, high_pred], 0)
    pair_mask = jnp.concatenate([low_mask, high_mask], 0)
    below = shifted(jnp.concatenate([pair_pred[-wide:], pair_mask[-thin:]], 0), "gx", 2)
    above = shifted(jnp.concatenate([pair_pred[:wide], pair_mask[:thin]], 0), "gx", -2)
    all_pred = jnp.concatenate([below[:wide], pair_pred, above[:wide]], 0)
    all_mask = jnp.concatenate([below[wide:], pair_mask, above[wide:]], 0)
    tall_pred = jnp.where(odd, all_pred[rows : 2 * rows + 2 * wide], all_pred[: rows + 2 * wide])
    tall_mask = jnp.where(odd, all_mask[rows : 2 * rows + 2 * thin], all_mask[: rows + 2 * thin])

    def edge(lo_pred, lo_mask):
        return jnp.concatenate([jnp.swapaxes(lo_pred, 0, 1), jnp.pad(jnp.swapaxes(lo_mask, 0, 1), ((0, 0), (0, 0), (0, 0)))], 0)

    tall = tall_pred.shape[0]
    short = tall_mask.shape[0]

    def packed(p, m):
        return jnp.concatenate([p.reshape(tall * wide, -1), m.reshape(short * thin, -1)], 0)

    left = shifted(packed(tall_pred[:, -wide:], tall_mask[:, -thin:]), "gy", 1)
    right = shifted(packed(tall_pred[:, :wide], tall_mask[:, :thin]), "gy", -1)

    def unpacked(b):
        return b[: tall * wide].reshape(tall, wide, -1), b[tall * wide :].reshape(short, thin, -1)

    left_pred, left_mask = unpacked(left)
    right_pred, right_mask = unpacked(right)
    return (
        jnp.concatenate([left_pred, tall_pred, right_pred], 1),
        jnp.concatenate([left_mask, tall_mask, right_mask], 1),
    )


def box(e):
    e = e[:-2] + e[1:-1] + e[2:]
    e = e[:, :-2] + e[:, 1:-1] + e[:, 2:]
    blank = jnp.zeros_like(e[..., :1])
    return e + jnp.concatenate([e[..., 1:], blank], -1) + jnp.concatenate([blank, e[..., :-1]], -1)


def crop(e, by):
    return e[by:-by, by:-by] if by else e


def levels_of(power_term, inside, keep):
    width = keep + REACH
    powers = [power_term * inside(width)]
    for _ in range(LEVELS):
        width -= 1
        powers.append(box(powers[-1]) * inside(width))
    return powers


def local(prediction, vessel_mask):
    rows, cols, depth = prediction.shape
    t = softness_factor
    mask_field = vessel_mask.astype(jnp.float32)
    row0 = lax.axis_index("gx") * rows
    col0 = lax.axis_index("gy") * cols
    row_count = rows * lax.axis_size("gx")
    col_count = cols * lax.axis_size("gy")

    def inside(width):
        r = lax.broadcasted_iota(jnp.int32, (rows + 2 * width, cols + 2 * width, 1), 0) + (row0 - width)
        c = lax.broadcasted_iota(jnp.int32, (rows + 2 * width, cols + 2 * width, 1), 1) + (col0 - width)
        return ((r >= 0) & (r < row_count) & (c >= 0) & (c < col_count)).astype(jnp.float32)

    pred_ext, mask_ext = with_halo(prediction, mask_field)

    def forward(field, keep):
        powers = levels_of(jnp.exp(-field / t), inside, keep)
        full = keep + REACH
        opened, inverse = [], []
        here = inside(keep)
        for k in range(1, LEVELS + 1):
            held = full - k
            inv = jnp.where(inside(held) > 0, 1.0 / powers[k], 0.0)
            inverse.append(inv)
            opened.append(box(crop(inv, held - keep - 1)))
        skel = None
        deltas, slopes, rects, skels = [], [], [], []
        for j in range(LEVELS):
            product = crop(powers[j], full - j - keep) * opened[j]
            product = jnp.where(here > 0, product, 1.0)
            slopes.append(1.0 / (1.0 + product))
            delta = jnp.log(1.0 + 1.0 / product)
            deltas.append(delta)
            if skel is None:
                skel = delta
            else:
                e = jnp.exp(delta * (1.0 - t * skel))
                rects.append(e / (1.0 + e))
                skel = skel + jnp.log(1.0 + e)
            skels.append(skel)
        return powers, inverse, opened, skels, deltas, slopes, rects

    _, _, _, mask_skels, _, _, _ = forward(mask_ext, 0)
    mask_skel = t * mask_skels[-1]
    powers, inverse, opened, skels, deltas, slopes, rects = forward(pred_ext, REACH)
    here = inside(REACH)
    pred_skel = t * crop(skels[-1], REACH)
    rest = here
    weights = [None] * LEVELS
    for j in range(ITERS, 0, -1):
        inner = rest * rects[j - 1]
        weights[j] = inner * (1.0 - t * skels[j - 1]) * slopes[j]
        rest = rest - inner * (t * deltas[j])
    weights[0] = rest * slopes[0]
    full = 2 * REACH

    def backward(seed):
        grown = None
        for k in range(LEVELS, 0, -1):
            spread = box(crop(seed * weights[k - 1] / jnp.where(here > 0, opened[k - 1], 1.0), REACH - k - 1))
            inv = crop(inverse[k - 1], full - k - k)
            part = -inv * inv * spread
            if k < LEVELS:
                part = part + crop(seed * weights[k], REACH - k) * inv + grown
            part = part * inside(k)
            grown = box(part)
        return crop(powers[0], full) * grown + crop(seed * weights[0], REACH)

    by_label = backward(mask_ext)
    by_one = backward(jnp.ones_like(mask_ext))
    sums = jnp.stack(
        [
            jnp.sum(pred_skel * mask_field),
            jnp.sum(pred_skel),
            jnp.sum(mask_skel * prediction),
            jnp.sum(mask_skel),
        ]
    )
    devices = lax.axis_size("gx") * lax.axis_size("gy")
    sent = jnp.broadcast_to(jnp.pad(sums, (0, 124))[None, None], (devices, 1, 128))
    got = lax.all_to_all(sent, ("gx", "gy"), 0, 0)
    totals = jnp.sum(got, (0, 1))
    intersection_pred, mass_pred, intersection_mask, mass_mask = (totals[i] for i in range(4))
    precision = (intersection_pred + 1.0) / (mass_pred + 1.0)
    sensitivity = (intersection_mask + 1.0) / (mass_mask + 1.0)
    paired = precision + sensitivity
    loss_value = 1.0 - 2.0 * precision * sensitivity / paired
    slope_prec = -2.0 * sensitivity * sensitivity / (paired * paired)
    slope_sens = -2.0 * precision * precision / (paired * paired)
    coef_intersection = slope_prec / (mass_pred + 1.0)
    coef_mass = -slope_prec * (intersection_pred + 1.0) / ((mass_pred + 1.0) * (mass_pred + 1.0))
    coef_cross = slope_sens / (mass_mask + 1.0)
    gradient = coef_intersection * by_label + coef_mass * by_one + coef_cross * mask_skel
    return (gradient * float(row_count * col_count * depth), loss_value)


def solution(mesh):
    placed = (P("gx", "gy", None), P("gx", "gy", None))
    return jax.shard_map(
        local, mesh=mesh, in_specs=placed, out_specs=(P("gx", "gy", None), P()), check_vma=False
    )
```

time: 235 us -> 109 us (0.46)
  starting transfers between devices: 91.6 us -> 22.8 us
  waiting for transfers between devices: 74.3 us -> 9.59 us
  blocking collectives: 41.6 us -> 0 us
  local copies, waits for them, and re-layouts: 2.29 us -> 30.4 us
  other arithmetic: 16.1 us -> 38.8 us
    ppermute x40 -> x5, starting transfers between devices: 91.6 us -> 11.5 us  [the longest x4 8.46 us: shifted(): return lax.ppermute(block, axis, pairs)]
    ppermute x40 -> x5, waiting for transfers between devices: 74.3 us -> 9.59 us  [the longest x4 7.19 us: shifted(): return lax.ppermute(block, axis, pairs)]
    psum x1 -> x0, blocking collectives: 41.6 us -> none  [local(): lax.psum((jnp.sum(pred_skel * mask_field), jnp.sum(pred_skel), jnp.sum(ma...]
    unnamed x38 -> x82, local copies, waits for them, and re-layouts: 0.75 us -> 13.9 us
    slice x19 -> x45, local copies, waits for them, and re-layouts: 1.53 us -> 13.3 us  [the longest x32 9.34 us: box(): e[..., 1:]]
    all_to_all x0 -> x1, starting transfers between devices: none -> 11.3 us  [local(): got = lax.all_to_all(sent, ('gx', 'gy'), 0, 0)]
    add x22 -> x65, other arithmetic: 3.7 us -> 10 us  [the longest x1 6.05 us: forward(): skel = skel + jnp.log(1.0 + e)]
    mul x6 -> x7, other arithmetic: 3.56 us -> 8.23 us  [the longest x4 5.88 us: backward(): part = part * inside(k)]
  transfers between devices with their start and end apart: 40 -> 6, of which waited for: 30 -> 4; matrix products, arithmetic and copies ran while one was open for 0% -> 12% of each run, Pallas kernels for 0% -> 0%
where the time goes in v1:
time: 109 us; the launch traced here: 108 us
  other arithmetic  38.8 us (36%)
  local copies, waits for them, and re-layouts  30.4 us (28%)
  starting transfers between devices  22.8 us (21%)
  waiting for transfers between devices  9.59 us (9%)
  between operations  5.93 us (5%)
    unnamed x82, local copies, waits for them, and re-layouts  13.9 us
    all_to_all x1, starting transfers between devices, local(): got = lax.all_to_all(sent, ('gx', 'gy'), 0, 0)  11.3 us
    slice x32, local copies, waits for them, and re-layouts, box(): e[..., 1:]  9.34 us
    ppermute x4, starting transfers between devices, shifted(): return lax.ppermute(block, axis, pairs)  8.46 us
    ppermute x4, waiting for transfers between devices, shifted(): return lax.ppermute(block, axis, pairs)  7.19 us
    div x3, other arithmetic, backward(): seed * weights[k - 1] / jnp.where(here > 0, opened[k - 1], 1.0)  7.06 us
    add x1, other arithmetic, forward(): skel = skel + jnp.log(1.0 + e)  6.05 us
    mul x4, other arithmetic, backward(): part = part * inside(k)  5.88 us
  transfers between devices with their start and end apart: 6, of which 4 were waited for; matrix products, arithmetic and copies ran while one was open for 12% of the time, Pallas kernels for 0%

profile of v1, /device:TPU:0, one launch (start us, length us, event | category | flops | bytes accessed | tf_op | source)
XLA Modules:
  0.0 107.6 jit_solution(4314633257721043235)
XLA Ops:
  2.6 3.0 %collective-permute-start = (f32[16,16,256]{2,1,0:T(8,128)S(1)}, f32[16,16,256]{2,1,0:T(8,128)S(1)}, u32[]{:S(2)}, u32[]{:S(2)}) collective-permute-start(f32[16,16,256]{2,1,0:T(8,128)S(1)} %pad_maximum_fusion.8), channel_id=1, source_target_pairs={{0,4},{4,0},{8,12},{12,8},{16,20},{20,16},{24,28},{28,24},{1,5},{5... | collective-permute-start | bytes 786440 | tf_op jit(solution)/shard_map/ppermute | solution.py:20
  9.5 2.4 %collective-permute-done = f32[16,16,256]{2,1,0:T(8,128)S(1)} collective-permute-done((f32[16,16,256]{2,1,0:T(8,128)S(1)}, f32[16,16,256]{2,1,0:T(8,128)S(1)}, u32[]{:S(2)}, u32[]{:S(2)}) %collective-permute-start) | collective-permute-done | bytes 262176 | tf_op jit(solution)/shard_map/ppermute | solution.py:20
  12.0 1.3 %collective-permute-start.2 = (f32[15,16,256]{2,1,0:T(8,128)S(1)}, f32[15,16,256]{2,1,0:T(8,128)S(1)}, u32[]{:S(2)}, u32[]{:S(2)}) collective-permute-start(f32[15,16,256]{2,1,0:T(8,128)S(1)} %fusion.31), channel_id=1, source_target_pairs={{8,0},{12,4},{16,8},{20,12},{24,16},{28,20},{9,1},{13,5},{17,9},{2... | collective-permute-start | bytes 737288 | tf_op jit(solution)/shard_map/ppermute | solution.py:15
  13.4 4.6 %collective-permute-start.1 = (f32[15,16,256]{2,1,0:T(8,128)S(1)}, f32[15,16,256]{2,1,0:T(8,128)S(1)}, u32[]{:S(2)}, u32[]{:S(2)}) collective-permute-start(f32[15,16,256]{2,1,0:T(8,128)S(1)} %pad_maximum_fusion.9), channel_id=1, source_target_pairs={{0,8},{4,12},{8,16},{12,20},{16,24},{20,28},{1,9},{5,13},{9,17},{1... | collective-permute-start | bytes 737288 | tf_op jit(solution)/shard_map/ppermute | solution.py:15
  18.0 3.0 %collective-permute-done.2 = f32[15,16,256]{2,1,0:T(8,128)S(1)} collective-permute-done((f32[15,16,256]{2,1,0:T(8,128)S(1)}, f32[15,16,256]{2,1,0:T(8,128)S(1)}, u32[]{:S(2)}, u32[]{:S(2)}) %collective-permute-start.2) | collective-permute-done | bytes 245792 | tf_op jit(solution)/shard_map/ppermute | solution.py:15
  22.7 1.3 %collective-permute-start.3 = (f32[370,256]{1,0:T(8,128)S(1)}, f32[370,256]{1,0:T(8,128)S(1)}, u32[]{:S(2)}, u32[]{:S(2)}) collective-permute-start(f32[370,256]{1,0:T(8,128)S(1)} %pad_maximum_fusion.2), channel_id=1, source_target_pairs={{0,1},{1,2},{2,3},{4,5},{5,6},{6,7},{8,9},{9,10},{10,11},{12,13},{... | collective-permute-start | bytes 1136648 | tf_op jit(solution)/shard_map/ppermute | solution.py:15
  24.1 1.3 %collective-permute-start.4 = (f32[370,256]{1,0:T(8,128)S(1)}, f32[370,256]{1,0:T(8,128)S(1)}, u32[]{:S(2)}, u32[]{:S(2)}) collective-permute-start(f32[370,256]{1,0:T(8,128)S(1)} %pad_maximum_fusion.3), channel_id=1, source_target_pairs={{1,0},{2,1},{3,2},{5,4},{6,5},{7,6},{9,8},{10,9},{11,10},{13,12},{... | collective-permute-start | bytes 1136648 | tf_op jit(solution)/shard_map/ppermute | solution.py:15
  26.4 2.9 %collective-permute-done.4 = f32[370,256]{1,0:T(8,128)S(1)} collective-permute-done((f32[370,256]{1,0:T(8,128)S(1)}, f32[370,256]{1,0:T(8,128)S(1)}, u32[]{:S(2)}, u32[]{:S(2)}) %collective-permute-start.4) | collective-permute-done | bytes 378912 | tf_op jit(solution)/shard_map/ppermute | solution.py:15
  37.6 1.3 %fusion.98 = (f32[18,26,255]{2,1,0:T(8,128)}, f32[18,26,255]{2,1,0:T(8,128)}) fusion(f32[18,26,256]{2,1,0:T(8,128)S(1)} %slice_add_fusion.16), kind=kLoop, calls=%fused_computation.363 | loop fusion | bytes 1909440 | tf_op jit(solution)/shard_map/slice | solution.py:69
  39.1 1.2 %fusion.100 = (f32[18,26,255]{2,1,0:T(8,128)}, f32[18,26,255]{2,1,0:T(8,128)}) fusion(f32[18,26,256]{2,1,0:T(8,128)S(1)} %slice_add_fusion.20), kind=kLoop, calls=%fused_computation.365 | loop fusion | bytes 1909440 | tf_op jit(solution)/shard_map/slice | solution.py:69
  41.2 1.3 %fusion.99 = (f32[18,26,255]{2,1,0:T(8,128)}, f32[18,26,255]{2,1,0:T(8,128)}) fusion(f32[18,26,256]{2,1,0:T(8,128)S(1)} %slice_add_fusion.24), kind=kLoop, calls=%fused_computation.364 | loop fusion | bytes 1909440 | tf_op jit(solution)/shard_map/slice | solution.py:69
  43.4 1.2 %fusion.97 = (f32[18,26,255]{2,1,0:T(8,128)}, f32[18,26,255]{2,1,0:T(8,128)}) fusion(f32[18,26,256]{2,1,0:T(8,128)S(1)} %slice_add_fusion.28), kind=kLoop, calls=%fused_computation.362 | loop fusion | bytes 1909440 | tf_op jit(solution)/shard_map/slice | solution.py:69
  44.7 1.5 %slice.1359 = f32[90,256]{1,0:T(8,128)} slice(f32[370,256]{1,0:T(8,128)} %copy-done.30), slice={[280:370], [0:256]} | slice | bytes 184320 | tf_op jit(solution)/shard_map/slice | solution.py:55
  47.1 1.5 %slice.1360 = f32[90,256]{1,0:T(8,128)} slice(f32[370,256]{1,0:T(8,128)} %copy-done.31), slice={[280:370], [0:256]} | slice | bytes 184320 | tf_op jit(solution)/shard_map/slice | solution.py:55
  48.6 1.6 %reshape.863 = f32[18,5,256]{2,1,0:T(8,128)} reshape(f32[90,256]{1,0:T(8,128)} %slice.1360) | data formatting | bytes 184320 | tf_op jit(solution)/shard_map/reshape | solution.py:55
  50.2 6.0 %fusion.24 = (f32[18,26,256]{2,1,0:T(8,128)S(1)}, f32[18,26,256]{2,1,0:T(8,128)S(1)}, f32[18,26,256]{2,1,0:T(8,128)S(1)}, f32[18,26,256]{2,1,0:T(8,128)S(1)}, f3...) fusion(f32[24,32,256]{2,1,0:T(8,128)} %copy-done.2, ...), kind=kLoop, calls=%fused_computation.179 | loop fusion | flops 5511168 | bytes 14841684 | tf_op jit(solution)/shard_map/add | solution.py:124
  57.4 2.8 %select_divide_fusion.3 = (f32[18,26,256]{2,1,0:T(8,128)S(1)}, f32[18,26,256]{2,1,0:T(8,128)}, f32[18,26,256]{2,1,0:T(8,128)S(1)}, f32[18,26,256]{2,1,0:T(8,128)...) fusion(f32[18,26,256]{2,1,0:T(8,128)S(1)} %get-tuple-element.8, pred[18,26]{1,0:T(8,128)(4,1)S(1)} %get-tuple-element.141, ...), kind=kLoop, calls=%fused_computation.87 | loop fusion | flops 6589440 | bytes 7190820 | tf_op jit(solution)/shard_map/div | solution.py:145
  60.2 3.0 %select_divide_fusion.1 = (f32[18,26,256]{2,1,0:T(8,128)S(1)}, f32[18,26,256]{2,1,0:T(8,128)}, f32[18,26,256]{2,1,0:T(8,128)S(1)}, f32[18,26,256]{2,1,0:T(8,128)...) fusion(f32[18,26,256]{2,1,0:T(8,128)S(1)} %get-tuple-element.11, ...), kind=kLoop, calls=%fused_computation.85 | loop fusion | flops 6829056 | bytes 9107748 | tf_op jit(solution)/shard_map/div | solution.py:145
  72.5 2.5 %select_maximum_fusion.1 = f32[128]{0:T(128)S(1)} fusion(f32[1]{0:T(128)} %bitcast.3, f32[1]{0:T(128)} %bitcast.2, f32[1]{0:T(128)} %bitcast.1, f32[1]{0:T(128)} %bitcast), kind=kLoop, calls=%fused_computation.317 | loop fusion | flops 1024 | bytes 528 | tf_op jit(solution)/shard_map/stack | solution.py:156
  75.5 11.3 %all-to-all-start = ((f32[32,1,128]{2,1,0:T(1,128)}), f32[32,1,128]{2,1,0:T(1,128)S(1)}, u32[]{:S(2)}, u32[]{:S(2)}) async-start(f32[32,1,128]{2,1,0:T(1,128)} %broadcast_in_dim.196), calls=%async_computation | async-start | bytes 32768 | tf_op jit(solution)/shard_map/all_to_all | solution.py:166
  89.1 1.8 %fusion.16 = (f32[14,22,256]{2,1,0:T(8,128)S(1)}, f32[14,22,256]{2,1,0:T(8,128)S(1)}) fusion(f32[18,26,256]{2,1,0:T(8,128)S(1)} %copy-done.24, f32[14,22,255]{2,1,0:T(8,128)S(1)} %get-tuple-element.84, f32[14,22,255]{2,1,0:T(8,128)S(1)} %get-tuple-element.83, f32[14,22,255]{2,1,0:T(8,128)S(1)} %get-tuple-element.82, ...), kind=kLoop, calls=%fused_computation.133 | loop fusion | flops 2207744 | bytes 7876176 | tf_op jit(solution)/shard_map/mul | solution.py:150
  94.7 1.6 %fusion.22 = (f32[12,20,256]{2,1,0:T(8,128)S(1)}, f32[12,20,256]{2,1,0:T(8,128)S(1)}) fusion(f32[18,26,256]{2,1,0:T(8,128)S(1)} %copy-done.25, f32[12,20,255]{2,1,0:T(8,128)S(1)} %get-tuple-element.94, f32[12,20,255]{2,1,0:T(8,128)S(1)} %get-tuple-element.93, f32[12,20,255]{2,1,0:T(8,128)S(1)} %get-tuple-element.92, ...), kind=kLoop, calls=%fused_computation.163 | loop fusion | flops 1720320 | bytes 6137280 | tf_op jit(solution)/shard_map/mul | solution.py:150
  99.0 1.8 %fusion.30 = (f32[10,18,256]{2,1,0:T(8,128)S(1)}, f32[10,18,256]{2,1,0:T(8,128)S(1)}) fusion(f32[18,26,256]{2,1,0:T(8,128)} %get-tuple-element.42, f32[10,18,255]{2,1,0:T(8,128)S(1)} %get-tuple-element.108, f32[10,18,255]{2,1,0:T(8,128)S(1)} %get-tuple-element.107, f32[10,18,255]{2,1,0:T(8,128)S(1)} %get-tuple-element.106, ...), kind=kLoop, calls=%fused_computation.202 | loop fusion | flops 1290240 | bytes 4602960 | tf_op jit(solution)/shard_map/mul | solution.py:150
  104.5 1.9 %fusion.36 = f32[8,16,256]{2,1,0:T(8,128)} fusion(f32[18,26,256]{2,1,0:T(8,128)} %copy-done.22, f32[18,26,256]{2,1,0:T(8,128)} %get-tuple-element.39, f32[8,16,256]{2,1,0:T(8,128)S(1)} %get-tuple-element.13, f32[8,16,255]{2,1,0:T(8,128)S(1)} %get-tuple-element.118, f32[8,16,255]{2,1,0:T(8,128)S(1)} %get-tuple-element.117, f32[28,36,256]{2,1,0:T(8,128)S(1)} %fusion.2, ...), kind=kLoop, calls=%fused_computation.233 | loop fusion | flops 589824 | bytes 1964044 | tf_op jit(solution)/shard_map/mul | solution.py:179
  (254 shorter events, 39.3 us)
Async XLA Ops:
  0.6 11.3 %copy-start.26 = (s32[8,16,256]{2,1,0:T(8,128)S(1)}, s32[8,16,256]{2,1,0:T(8,128)}, u32[]{:S(2)}) copy-start(s32[8,16,256]{2,1,0:T(8,128)} %param.3) | copy-start | bytes 393220
  0.6 11.3 %copy-start.28 = (f32[8,16,256]{2,1,0:T(8,128)S(1)}, f32[8,16,256]{2,1,0:T(8,128)}, u32[]{:S(2)}) copy-start(f32[8,16,256]{2,1,0:T(8,128)} %param.2) | copy-start | bytes 393220
  2.6 9.3 %collective-permute-start = (f32[16,16,256]{2,1,0:T(8,128)S(1)}, f32[16,16,256]{2,1,0:T(8,128)S(1)}, u32[]{:S(2)}, u32[]{:S(2)}) collective-permute-start(f32[16,16,256]{2,1,0:T(8,128)S(1)} %pad_maximum_fusion.8), channel_id=1, source_target_pairs={{0,4},{4,0},{8,12},{12,8},{16,20},{20,16},{24,28},{28,24},{1,5},{5... | collective-permute-start | bytes 786440 | tf_op jit(solution)/shard_map/ppermute | solution.py:20
  12.0 9.0 %collective-permute-start.2 = (f32[15,16,256]{2,1,0:T(8,128)S(1)}, f32[15,16,256]{2,1,0:T(8,128)S(1)}, u32[]{:S(2)}, u32[]{:S(2)}) collective-permute-start(f32[15,16,256]{2,1,0:T(8,128)S(1)} %fusion.31), channel_id=1, source_target_pairs={{8,0},{12,4},{16,8},{20,12},{24,16},{28,20},{9,1},{13,5},{17,9},{2... | collective-permute-start | bytes 737288 | tf_op jit(solution)/shard_map/ppermute | solution.py:15
  13.4 8.9 %collective-permute-start.1 = (f32[15,16,256]{2,1,0:T(8,128)S(1)}, f32[15,16,256]{2,1,0:T(8,128)S(1)}, u32[]{:S(2)}, u32[]{:S(2)}) collective-permute-start(f32[15,16,256]{2,1,0:T(8,128)S(1)} %pad_maximum_fusion.9), channel_id=1, source_target_pairs={{0,8},{4,12},{8,16},{12,20},{16,24},{20,28},{1,9},{5,13},{9,17},{1... | collective-permute-start | bytes 737288 | tf_op jit(solution)/shard_map/ppermute | solution.py:15
  22.6 1.5 %copy-start.11 = (f32[18,16,256]{2,1,0:T(8,128)}, f32[18,16,256]{2,1,0:T(8,128)S(1)}, u32[]{:S(2)}) copy-start(f32[18,16,256]{2,1,0:T(8,128)S(1)} %fusion.23) | copy-start | bytes 884740
  22.7 2.9 %collective-permute-start.3 = (f32[370,256]{1,0:T(8,128)S(1)}, f32[370,256]{1,0:T(8,128)S(1)}, u32[]{:S(2)}, u32[]{:S(2)}) collective-permute-start(f32[370,256]{1,0:T(8,128)S(1)} %pad_maximum_fusion.2), channel_id=1, source_target_pairs={{0,1},{1,2},{2,3},{4,5},{5,6},{6,7},{8,9},{9,10},{10,11},{12,13},{... | collective-permute-start | bytes 1136648 | tf_op jit(solution)/shard_map/ppermute | solution.py:15
  24.1 5.2 %collective-permute-start.4 = (f32[370,256]{1,0:T(8,128)S(1)}, f32[370,256]{1,0:T(8,128)S(1)}, u32[]{:S(2)}, u32[]{:S(2)}) collective-permute-start(f32[370,256]{1,0:T(8,128)S(1)} %pad_maximum_fusion.3), channel_id=1, source_target_pairs={{1,0},{2,1},{3,2},{5,4},{6,5},{7,6},{9,8},{10,9},{11,10},{13,12},{... | collective-permute-start | bytes 1136648 | tf_op jit(solution)/shard_map/ppermute | solution.py:15
  32.0 10.6 %copy-start.10 = (f32[26,34,256]{2,1,0:T(8,128)}, f32[26,34,256]{2,1,0:T(8,128)S(1)}, u32[]{:S(2)}) copy-start(f32[26,34,256]{2,1,0:T(8,128)S(1)} %get-tuple-element.36) | copy-start | bytes 2715652
  33.1 7.2 %copy-start.9 = (f32[24,32,256]{2,1,0:T(8,128)}, f32[24,32,256]{2,1,0:T(8,128)S(1)}, u32[]{:S(2)}) copy-start(f32[24,32,256]{2,1,0:T(8,128)S(1)} %get-tuple-element.34) | copy-start | bytes 2359300
  34.9 4.0 %copy-start.8 = (f32[22,30,256]{2,1,0:T(8,128)}, f32[22,30,256]{2,1,0:T(8,128)S(1)}, u32[]{:S(2)}) copy-start(f32[22,30,256]{2,1,0:T(8,128)S(1)} %get-tuple-element.32) | copy-start | bytes 2027524
  50.2 6.1 %copy-start.27 = (s32[8,16,256]{2,1,0:T(8,128)S(1)}, s32[8,16,256]{2,1,0:T(8,128)}, u32[]{:S(2)}) copy-start(s32[8,16,256]{2,1,0:T(8,128)} %param.3) | copy-start | bytes 393220
  50.2 6.8 %copy-start.12 = (f32[18,16,256]{2,1,0:T(8,128)S(1)}, f32[18,16,256]{2,1,0:T(8,128)}, u32[]{:S(2)}) copy-start(f32[18,16,256]{2,1,0:T(8,128)} %copy-done.11) | copy-start | bytes 884740
  50.2 6.8 %copy-start.23 = (f32[18,5,256]{2,1,0:T(8,128)S(1)}, f32[18,5,256]{2,1,0:T(8,128)}, u32[]{:S(2)}) copy-start(f32[18,5,256]{2,1,0:T(8,128)} %reshape.863) | copy-start | bytes 276484
  56.3 1.1 %copy-start.3 = (f32[24,32,256]{2,1,0:T(8,128)S(1)}, f32[24,32,256]{2,1,0:T(8,128)}, u32[]{:S(2)}) copy-start(f32[24,32,256]{2,1,0:T(8,128)} %copy-done.2) | copy-start | bytes 2359300
  57.4 2.8 %copy-start.5 = (f32[22,30,256]{2,1,0:T(8,128)S(1)}, f32[22,30,256]{2,1,0:T(8,128)}, u32[]{:S(2)}) copy-start(f32[22,30,256]{2,1,0:T(8,128)} %copy-done.4) | copy-start | bytes 2027524
  60.2 3.0 %copy-start.22 = (f32[18,26,256]{2,1,0:T(8,128)}, f32[18,26,256]{2,1,0:T(8,128)S(1)}, u32[]{:S(2)}) copy-start(f32[18,26,256]{2,1,0:T(8,128)S(1)} %get-tuple-element.40) | copy-start | bytes 1437700
  60.2 3.1 %copy-start.15 = (f32[18,26,256]{2,1,0:T(8,128)}, f32[18,26,256]{2,1,0:T(8,128)S(1)}, u32[]{:S(2)}) copy-start(f32[18,26,256]{2,1,0:T(8,128)S(1)} %get-tuple-element.22) | copy-start | bytes 1437700
  63.3 1.2 %copy-start.13 = (f32[18,26,256]{2,1,0:T(8,128)}, f32[18,26,256]{2,1,0:T(8,128)S(1)}, u32[]{:S(2)}) copy-start(f32[18,26,256]{2,1,0:T(8,128)S(1)} %get-tuple-element.25) | copy-start | bytes 1437700
  63.3 1.2 %copy-start.19 = (f32[18,26,256]{2,1,0:T(8,128)}, f32[18,26,256]{2,1,0:T(8,128)S(1)}, u32[]{:S(2)}) copy-start(f32[18,26,256]{2,1,0:T(8,128)S(1)} %get-tuple-element.43) | copy-start | bytes 1437700
  65.3 1.1 %copy-start.7 = (f32[20,28,256]{2,1,0:T(8,128)S(1)}, f32[20,28,256]{2,1,0:T(8,128)}, u32[]{:S(2)}) copy-start(f32[20,28,256]{2,1,0:T(8,128)} %copy-done.6) | copy-start | bytes 1720324
  75.5 25.5 %all-to-all-start = ((f32[32,1,128]{2,1,0:T(1,128)}), f32[32,1,128]{2,1,0:T(1,128)S(1)}, u32[]{:S(2)}, u32[]{:S(2)}) async-start(f32[32,1,128]{2,1,0:T(1,128)} %broadcast_in_dim.196), calls=%async_computation | async-start | bytes 32768 | tf_op jit(solution)/shard_map/all_to_all | solution.py:166
  87.8 1.2 %copy-start.24 = (f32[18,26,256]{2,1,0:T(8,128)S(1)}, f32[18,26,256]{2,1,0:T(8,128)}, u32[]{:S(2)}) copy-start(f32[18,26,256]{2,1,0:T(8,128)} %get-tuple-element.24) | copy-start | bytes 1437700
  93.4 1.2 %copy-start.25 = (f32[18,26,256]{2,1,0:T(8,128)S(1)}, f32[18,26,256]{2,1,0:T(8,128)}, u32[]{:S(2)}) copy-start(f32[18,26,256]{2,1,0:T(8,128)} %get-tuple-element.21) | copy-start | bytes 1437700
  (23 other events, 20.3 us)

commit v2 on v1

v2 whole, which is shorter than its diff:
```python
import jax
import jax.numpy as jnp
from jax import lax
from jax.experimental import pallas as pl
from jax.experimental.pallas import tpu as pltpu
from jax.sharding import PartitionSpec as P

ITERS = 3
LEVELS = ITERS + 1
REACH = LEVELS + 1
softness_factor = 0.1


def shifted(block, axis, step):
    count = lax.axis_size(axis)
    pairs = [(i, i + step) for i in range(count) if 0 <= i + step < count]
    return lax.ppermute(block, axis, pairs)


def swapped(block, axis):
    count = lax.axis_size(axis)
    return lax.ppermute(block, axis, [(i, i ^ 1) for i in range(count)])


def with_halo(prediction, mask_field):
    rows, cols, _ = prediction.shape
    wide, thin = 2 * REACH, REACH
    odd = lax.rem(lax.axis_index("gx"), 2) == 1
    other = swapped(jnp.concatenate([prediction, mask_field], 0), "gx")
    other_pred, other_mask = other[:rows], other[rows:]
    low_pred = jnp.where(odd, other_pred, prediction)
    high_pred = jnp.where(odd, prediction, other_pred)
    low_mask = jnp.where(odd, other_mask, mask_field)
    high_mask = jnp.where(odd, mask_field, other_mask)
    pair_pred = jnp.concatenate([low_pred, high_pred], 0)
    pair_mask = jnp.concatenate([low_mask, high_mask], 0)
    below = shifted(jnp.concatenate([pair_pred[-wide:], pair_mask[-thin:]], 0), "gx", 2)
    above = shifted(jnp.concatenate([pair_pred[:wide], pair_mask[:thin]], 0), "gx", -2)
    all_pred = jnp.concatenate([below[:wide], pair_pred, above[:wide]], 0)
    all_mask = jnp.concatenate([below[wide:], pair_mask, above[wide:]], 0)
    tall_pred = jnp.where(odd, all_pred[rows : 2 * rows + 2 * wide], all_pred[: rows + 2 * wide])
    tall_mask = jnp.where(odd, all_mask[rows : 2 * rows + 2 * thin], all_mask[: rows + 2 * thin])

    tall = tall_pred.shape[0]
    short = tall_mask.shape[0]

    def packed(p, m):
        return jnp.concatenate([p.reshape(tall * wide, -1), m.reshape(short * thin, -1)], 0)

    left = shifted(packed(tall_pred[:, -wide:], tall_mask[:, -thin:]), "gy", 1)
    right = shifted(packed(tall_pred[:, :wide], tall_mask[:, :thin]), "gy", -1)

    def unpacked(b):
        return b[: tall * wide].reshape(tall, wide, -1), b[tall * wide :].reshape(short, thin, -1)

    left_pred, left_mask = unpacked(left)
    right_pred, right_mask = unpacked(right)
    return (
        jnp.concatenate([left_pred, tall_pred, right_pred], 1),
        jnp.concatenate([left_mask, tall_mask, right_mask], 1),
    )


WIDE = 2 * REACH
LANES = 128
SUBLANES = 8
VMEM_BYTES = 40 * 1024 * 1024


def tiles_for(count):
    return -(-count // SUBLANES)


def depth_sum(low, high, first, last):
    low_up, high_up = pltpu.roll(low, 1, 1), pltpu.roll(high, 1, 1)
    low_down, high_down = pltpu.roll(low, LANES - 1, 1), pltpu.roll(high, LANES - 1, 1)
    return (
        low + jnp.where(first, 0.0, low_up) + jnp.where(last, high_down, low_down),
        high + jnp.where(first, low_up, high_up) + jnp.where(last, 0.0, high_down),
    )


def rows_box(ref, base, row_shift, col_shift, count, first, last):
    def across(x, h):
        parts = [ref[x + row_shift, h, pl.ds(base + (col_shift + d), SUBLANES), :] for d in range(3)]
        return parts[0] + parts[1] + parts[2]

    older = [across(0, h) for h in range(2)]
    newer = [across(1, h) for h in range(2)]
    for x in range(count):
        newest = [across(x + 2, h) for h in range(2)]
        low, high = (older[h] + newer[h] + newest[h] for h in range(2))
        older, newer = newer, newest
        yield depth_sum(low, high, first, last)


def over_tiles(count, step):
    def body(i, carry):
        step(pl.multiple_of(i * SUBLANES, SUBLANES))
        return carry

    lax.fori_loop(0, tiles_for(count), body, 0)


def skeleton_kernel(rows, cols, place, own_pred, pred, label, by_label, by_one, mask_skel, sums, *scratch):
    t = softness_factor
    scratch = list(scratch)
    powers = scratch[:5]
    inverses = scratch[5:9]
    opened = scratch[9:13]
    weights = scratch[13:17]
    spreads = scratch[17:25]
    parts = scratch[25:33]
    labels, skels = scratch[33:35]
    label_powers = scratch[35:40]
    label_inverses = scratch[40:44]
    label_opened = scratch[44:48]
    row0, col0, row_count, col_count = (place[i] for i in range(4))
    lane = lax.broadcasted_iota(jnp.int32, (SUBLANES, LANES), 1)
    sublane = lax.broadcasted_iota(jnp.int32, (SUBLANES, LANES), 0)
    first, last = lane == 0, lane == LANES - 1

    def column_index(base, width):
        index = sublane + (base + (col0 - width))
        return jnp.where(index < 0, 1 << 20, index)

    def column_limit(x, width):
        row = row0 + (x - width)
        return jnp.where((row >= 0) & (row < row_count), col_count, 0)

    def raise_field(field, powers, inverses, width):
        def start(base):
            index = column_index(base, width)
            for x in range(rows + 2 * width):
                ok = index < column_limit(x, width)
                for h in range(2):
                    value = field[x, pl.ds(base, SUBLANES), h * LANES : (h + 1) * LANES]
                    powers[0][x, h, pl.ds(base, SUBLANES), :] = jnp.where(ok, jnp.exp(value * (-1.0 / t)), 0.0)

        over_tiles(cols + 2 * width, start)
        for level in range(1, LEVELS + 1):
            here = width - level

            def erode(base, level=level, here=here):
                index = column_index(base, here)
                sums_of = rows_box(powers[level - 1], base, 0, 0, rows + 2 * here, first, last)
                for x, pair in enumerate(sums_of):
                    ok = index < column_limit(x, here)
                    for h in range(2):
                        powers[level][x, h, pl.ds(base, SUBLANES), :] = jnp.where(ok, pair[h], 0.0)
                        inverses[level - 1][x, h, pl.ds(base, SUBLANES), :] = jnp.where(ok, 1.0 / pair[h], 0.0)

            over_tiles(cols + 2 * here, erode)

    def open_field(inverses, opened, width, keep):
        for level in range(1, LEVELS + 1):
            shift = width - level - keep - 1

            def dilate(base, level=level, shift=shift):
                sums_of = rows_box(inverses[level - 1], base, shift, shift, rows + 2 * keep, first, last)
                for x, pair in enumerate(sums_of):
                    for h in range(2):
                        opened[level - 1][x, h, pl.ds(base, SUBLANES), :] = pair[h]

            over_tiles(cols + 2 * keep, dilate)

    def chain(power_of, opened_of):
        skel, saved = None, []
        for j in range(LEVELS):
            wide = opened_of(j)
            product = power_of(j) * wide
            over = 1.0 / (wide * (1.0 + product))
            slope = wide * over
            delta = -jnp.log(product * slope)
            if skel is None:
                skel = delta
                saved.append((slope, over, delta, None, None))
            else:
                left = 1.0 - t * skel
                e = jnp.exp(delta * left)
                grown = 1.0 + e
                saved.append((slope, over, delta, left, e / grown))
                skel = skel + jnp.log(grown)
        return skel, saved

    raise_field(label, label_powers, label_inverses, REACH)
    open_field(label_inverses, label_opened, REACH, 0)

    def label_chain(base):
        for x in range(rows):
            for h in range(2):
                skel, _ = chain(
                    lambda j: label_powers[j][x + REACH - j, h, pl.ds(base + (REACH - j), SUBLANES), :],
                    lambda j: label_opened[j][x, h, pl.ds(base, SUBLANES), :],
                )
                mask_skel[x, pl.ds(base, SUBLANES), h * LANES : (h + 1) * LANES] = t * skel

    over_tiles(cols, label_chain)

    def spread_label(base):
        for x in range(rows + 2 * REACH):
            for h in range(2):
                labels[x, h, pl.ds(base, SUBLANES), :] = label[x, pl.ds(base, SUBLANES), h * LANES : (h + 1) * LANES]

    over_tiles(cols + 2 * REACH, spread_label)

    raise_field(pred, powers, inverses, WIDE)
    open_field(inverses, opened, WIDE, REACH)

    chunk = 3

    def chain_chunk(base, x0):
        index = column_index(base, REACH)
        for dx in range(chunk):
            x = x0 + dx
            ok = index < column_limit(x, REACH)
            for h in range(2):
                skel, saved = chain(
                    lambda j: powers[j][x + REACH - j, h, pl.ds(base + (REACH - j), SUBLANES), :],
                    lambda j: opened[j][x, h, pl.ds(base, SUBLANES), :],
                )
                skels[x, h, pl.ds(base, SUBLANES), :] = t * skel
                seed = labels[x, h, pl.ds(base, SUBLANES), :]
                rest = jnp.where(ok, 1.0, 0.0)
                for j in range(ITERS, -1, -1):
                    slope, over, delta, left, rect = saved[j]
                    if j:
                        inner = rest * rect
                        scaled = inner * left
                        rest = rest - inner * (t * delta)
                    else:
                        scaled = rest
                    weights[j][x, h, pl.ds(base, SUBLANES), :] = jnp.where(ok, scaled * slope, 0.0)
                    spread = jnp.where(ok, scaled * over, 0.0)
                    spreads[j][x, h, pl.ds(base, SUBLANES), :] = spread
                    spreads[LEVELS + j][x, h, pl.ds(base, SUBLANES), :] = seed * spread

    def chain_tile(base):
        def body(i, carry):
            chain_chunk(base, i * chunk)
            return carry

        lax.fori_loop(0, (rows + 2 * REACH) // chunk, body, 0)

    over_tiles(cols + 2 * REACH, chain_tile)

    for level in range(LEVELS, 0, -1):
        for which in range(2):

            def pull(base, level=level, which=which):
                index = column_index(base, level)
                count = rows + 2 * level
                shift = REACH - level - 1
                spread_sums = rows_box(spreads[which * LEVELS + level - 1], base, shift, shift, count, first, last)
                if level < LEVELS:
                    grown_sums = rows_box(parts[which * LEVELS + level], base, 0, 0, count, first, last)
                for x in range(count):
                    ok = index < column_limit(x, level)
                    spread = next(spread_sums)
                    grown = next(grown_sums) if level < LEVELS else None
                    for h in range(2):
                        off = WIDE - 2 * level
                        inv = inverses[level - 1][x + off, h, pl.ds(base + off, SUBLANES), :]
                        part = -(inv * spread[h])
                        if level < LEVELS:
                            at = REACH - level
                            own = weights[level][x + at, h, pl.ds(base + at, SUBLANES), :]
                            if which:
                                own = own * labels[x + at, h, pl.ds(base + at, SUBLANES), :]
                            part = (part + own) * inv + grown[h]
                        else:
                            part = part * inv
                        parts[which * LEVELS + level - 1][x, h, pl.ds(base, SUBLANES), :] = jnp.where(ok, part, 0.0)

            over_tiles(cols + 2 * level, pull)

    def finish(base, totals):
        totals = list(totals)
        pairs = [rows_box(parts[which * LEVELS], base, 0, 0, rows, first, last) for which in range(2)]
        for x in range(rows):
            grown = [next(p) for p in pairs]
            for h in range(2):
                half = slice(h * LANES, (h + 1) * LANES)
                power = powers[0][x + WIDE, h, pl.ds(base + WIDE, SUBLANES), :]
                own = weights[0][x + REACH, h, pl.ds(base + REACH, SUBLANES), :]
                seed = labels[x + REACH, h, pl.ds(base + REACH, SUBLANES), :]
                by_one[x, pl.ds(base, SUBLANES), half] = power * grown[0][h] + own
                by_label[x, pl.ds(base, SUBLANES), half] = power * grown[1][h] + own * seed
                skel = skels[x + REACH, h, pl.ds(base + REACH, SUBLANES), :]
                other = mask_skel[x, pl.ds(base, SUBLANES), half]
                predicted = own_pred[x, pl.ds(base, SUBLANES), half]
                totals[0] += skel * seed
                totals[1] += skel
                totals[2] += other * predicted
                totals[3] += other
        return tuple(totals)

    nothing = jnp.zeros((SUBLANES, LANES), jnp.float32)
    totals = lax.fori_loop(
        0,
        tiles_for(cols),
        lambda i, c: finish(pl.multiple_of(i * SUBLANES, SUBLANES), c),
        (nothing,) * 4,
    )
    packed = jnp.concatenate([jnp.sum(v, 0, keepdims=True) for v in totals] * 2, 0)
    for i in range(sums.shape[0] // SUBLANES):
        sums[i * SUBLANES : (i + 1) * SUBLANES, :] = packed


def combine_kernel(cells, got, by_label, by_one, mask_skel, gradient, loss):
    total = jnp.zeros((SUBLANES, LANES), jnp.float32)
    for i in range(got.shape[0] // SUBLANES):
        total += got[i * SUBLANES : (i + 1) * SUBLANES, :]
    total = total + pltpu.roll(total, 4, 0)
    total = jnp.broadcast_to(jnp.sum(total, 1, keepdims=True), (SUBLANES, LANES))
    intersection_pred, mass_pred, intersection_mask, mass_mask = (total[i : i + 1] + 1.0 for i in range(4))
    precision = intersection_pred / mass_pred
    sensitivity = intersection_mask / mass_mask
    paired = precision + sensitivity
    loss[0] = jnp.max(1.0 - 2.0 * precision * sensitivity / paired)
    slope_prec = -2.0 * sensitivity * sensitivity / (paired * paired)
    slope_sens = -2.0 * precision * precision / (paired * paired)
    coef_intersection = cells * slope_prec / mass_pred
    coef_mass = -coef_intersection * precision
    coef_cross = cells * slope_sens / mass_mask
    a, b, c = (
        jnp.broadcast_to(jnp.concatenate([v, v], 1), (gradient.shape[1], 2 * LANES))
        for v in (coef_intersection, coef_mass, coef_cross)
    )
    for x in range(gradient.shape[0]):
        gradient[x] = a * by_label[x] + b * by_one[x] + c * mask_skel[x]


def local(prediction, vessel_mask):
    rows, cols, depth = prediction.shape
    mask_field = vessel_mask.astype(jnp.float32)
    gx, gy = lax.axis_size("gx"), lax.axis_size("gy")
    place = jnp.stack(
        [lax.axis_index("gx") * rows, lax.axis_index("gy") * cols, jnp.int32(gx * rows), jnp.int32(gy * cols)]
    ).astype(jnp.int32)
    pred_ext, mask_ext = with_halo(prediction, mask_field)

    def held(width, margin=2):
        return pltpu.VMEM((rows + 2 * width, 2, tiles_for(cols + 2 * width + margin + 6) * SUBLANES, LANES), jnp.float32)

    scratch = (
        [held(WIDE - k) for k in range(LEVELS + 1)]
        + [held(WIDE - k) for k in range(1, LEVELS + 1)]
        + [held(REACH)] * 4
        + [held(REACH)] * 4
        + [held(REACH)] * 8
        + [held(k) for k in range(1, LEVELS + 1)] * 2
        + [held(REACH)] * 2
        + [held(REACH - k) for k in range(LEVELS + 1)]
        + [held(REACH - k) for k in range(1, LEVELS + 1)]
        + [held(0)] * 4
    )
    block = jax.ShapeDtypeStruct((rows, cols, depth), jnp.float32)
    vmem = pl.BlockSpec(memory_space=pltpu.VMEM)
    smem = pl.BlockSpec(memory_space=pltpu.SMEM)
    pad = tiles_for(cols + 2 * WIDE) * SUBLANES - (cols + 2 * WIDE)
    pred_ext = jnp.pad(pred_ext, ((0, 0), (0, pad), (0, 0)))
    pad = tiles_for(cols + 2 * REACH) * SUBLANES - (cols + 2 * REACH)
    mask_ext = jnp.pad(mask_ext, ((0, 0), (0, pad), (0, 0)))
    by_label, by_one, mask_skel, sums = pl.pallas_call(
        lambda *refs: skeleton_kernel(rows, cols, *refs),
        out_shape=[block, block, block, jax.ShapeDtypeStruct((gx * gy * 4, LANES), jnp.float32)],
        in_specs=[smem, vmem, vmem, vmem],
        out_specs=[vmem] * 4,
        scratch_shapes=scratch,
        compiler_params=pltpu.CompilerParams(vmem_limit_bytes=VMEM_BYTES),
        name="skeleton",
    )(place, prediction, pred_ext, mask_ext)
    got = lax.all_to_all(sums, ("gx", "gy"), 0, 0, tiled=True)
    gradient, loss = pl.pallas_call(
        lambda *refs: combine_kernel(float(gx * rows * gy * cols * depth), *refs),
        out_shape=[block, jax.ShapeDtypeStruct((1,), jnp.float32)],
        in_specs=[vmem] * 4,
        out_specs=[vmem, smem],
        name="combine",
    )(got, by_label, by_one, mask_skel)
    return (gradient, loss[0])


def solution(mesh):
    placed = (P("gx", "gy", None), P("gx", "gy", None))
    return jax.shard_map(
        local, mesh=mesh, in_specs=placed, out_specs=(P("gx", "gy", None), P()), check_vma=False
    )
```

time: 109 us -> 70.9 us (0.65); the launches traced: 108 us -> 70.6 us
  other arithmetic: 38.8 us -> 3.4 us
  local copies, waits for them, and re-layouts: 30.4 us -> 3.13 us
  Pallas kernels: 0 us -> 18.8 us
  blocking collectives: 0 us -> 17.4 us
  starting transfers between devices: 22.8 us -> 12.4 us
  between operations: 5.93 us -> 0.93 us
  waiting for transfers between devices: 9.59 us -> 14.5 us
    pallas_call x0 -> x2, Pallas kernels: none -> 18.8 us  [the longest x1 17 us: local(): pl.pallas_call(lambda *refs: skeleton_kernel(rows, cols, *refs), out_shap...]
    all_to_all x0 -> x1, blocking collectives: none -> 17.4 us  [local(): got = lax.all_to_all(sums, ('gx', 'gy'), 0, 0, tiled=True)]
    all_to_all x1 -> x0, starting transfers between devices: 11.3 us -> none  [local(): got = lax.all_to_all(sent, ('gx', 'gy'), 0, 0)]
    unnamed x82 -> x8, local copies, waits for them, and re-layouts: 13.9 us -> 2.69 us
    add x65 -> x0, other arithmetic: 10 us -> none  [the longest x1 6.05 us: forward(): skel = skel + jnp.log(1.0 + e)]
    slice x33 -> x0, local copies, waits for them, and re-layouts: 9.99 us -> none  [the longest x32 9.34 us: box(): e[..., 1:]]
    mul x7 -> x0, other arithmetic: 8.23 us -> none  [the longest x4 5.88 us: backward(): part = part * inside(k)]
    div x3 -> x0, other arithmetic: 7.06 us -> none  [backward(): seed * weights[k - 1] / jnp.where(here > 0, opened[k - 1], 1.0)]
  transfers between devices with their start and end apart: 6 -> 5, of which waited for: 4 -> 4; matrix products, arithmetic and copies ran while one was open for 12% -> 0% of each run, Pallas kernels for 0% -> 0%
where the time goes in v2:
time: 70.9 us; the launch traced here: 70.6 us
  Pallas kernels  18.8 us (27%)
  blocking collectives  17.4 us (25%)
  waiting for transfers between devices  14.5 us (20%)
  starting transfers between devices  12.4 us (17%)
  other arithmetic  3.4 us (5%)
  local copies, waits for them, and re-layouts  3.13 us (4%)
  between operations  0.93 us (1%)
    all_to_all x1, blocking collectives, local(): got = lax.all_to_all(sums, ('gx', 'gy'), 0, 0, tiled=True)  17.4 us
    pallas_call x1, Pallas kernels, local(): pl.pallas_call(lambda *refs: skeleton_kernel(rows, cols, *refs), out_shap...  17 us
    ppermute x4, starting transfers between devices, shifted(): return lax.ppermute(block, axis, pairs)  9.35 us
    ppermute x4, waiting for transfers between devices, shifted(): return lax.ppermute(block, axis, pairs)  8.21 us
    ppermute x1, waiting for transfers between devices, swapped(): return lax.ppermute(block, axis, [(i, i ^ 1) for i in range(count)])  6.31 us
    ppermute x1, starting transfers between devices, swapped(): return lax.ppermute(block, axis, [(i, i ^ 1) for i in range(count)])  3.03 us
    unnamed x8, local copies, waits for them, and re-layouts  2.69 us
    pallas_call x1, Pallas kernels, local(): pl.pallas_call(lambda *refs: combine_kernel(float(gx * rows * gy * cols *...  1.87 us
  transfers between devices with their start and end apart: 5, of which 4 were waited for; matrix products, arithmetic and copies ran while one was open for 0% of the time, Pallas kernels for 0%

profile of v2, /device:TPU:0, one launch (start us, length us, event | category | flops | bytes accessed | tf_op | source)
XLA Modules:
  0.0 70.6 jit_solution(11713435490607217048)
XLA Ops:
  0.6 0.9 %convert_element_type.7 = f32[8,16,256]{2,1,0:T(8,128)S(1)} convert(s32[8,16,256]{2,1,0:T(8,128)} %param.3) | non-fusion elementwise | flops 32768 | bytes 262144 | tf_op jit(solution)/shard_map/convert_element_type | solution.py:336
  1.5 0.9 %pad_maximum_fusion.7 = f32[16,16,256]{2,1,0:T(8,128)S(1)} fusion(f32[8,16,256]{2,1,0:T(8,128)S(1)} %convert_element_type.7, f32[8,16,256]{2,1,0:T(8,128)} %refs_1_.1), kind=kLoop, calls=%fused_computation.15 | loop fusion | flops 65536 | bytes 524288 | tf_op jit(solution)/shard_map/concatenate | solution.py:29
  2.5 3.0 %collective-permute-start = (f32[16,16,256]{2,1,0:T(8,128)S(1)}, f32[16,16,256]{2,1,0:T(8,128)S(1)}, u32[]{:S(2)}, u32[]{:S(2)}) collective-permute-start(f32[16,16,256]{2,1,0:T(8,128)S(1)} %pad_maximum_fusion.7), channel_id=1, source_target_pairs={{0,4},{4,0},{8,12},{12,8},{16,20},{20,16},{24,28},{28,24},{1,5},{5... | collective-permute-start | bytes 786440 | tf_op jit(solution)/shard_map/ppermute | solution.py:22
  5.5 6.3 %collective-permute-done = f32[16,16,256]{2,1,0:T(8,128)S(1)} collective-permute-done((f32[16,16,256]{2,1,0:T(8,128)S(1)}, f32[16,16,256]{2,1,0:T(8,128)S(1)}, u32[]{:S(2)}, u32[]{:S(2)}) %collective-permute-start) | collective-permute-done | bytes 262176 | tf_op jit(solution)/shard_map/ppermute | solution.py:22
  11.8 1.0 %slice_select_fusion.3 = (f32[8,16,256]{2,1,0:T(8,128)S(1)}, f32[8,16,256]{2,1,0:T(8,128)S(1)}, f32[8,16,256]{2,1,0:T(8,128)S(1)}, f32[8,16,256]{2,1,0:T(8,128)S(1)}) fusion(f32[8,16,256]{2,1,0:T(8,128)} %refs_1_.1, f32[16,16,256]{2,1,0:T(8,128)S(1)} %collective-permute-done, pred[]{:T(512)S(6)} %eq.3, s32[8,16,256]{2,1,0:T(8,128)} %param.3), kind=kLoop, calls=%fused_computation.25 | loop fusion | flops 163840 | bytes 1048577 | tf_op jit(solution)/shard_map/jit(_where)/select_n | solution.py:32
  12.9 3.7 %collective-permute-start.1 = (f32[15,16,256]{2,1,0:T(8,128)S(1)}, f32[15,16,256]{2,1,0:T(8,128)S(1)}, u32[]{:S(2)}, u32[]{:S(2)}) collective-permute-start(f32[15,16,256]{2,1,0:T(8,128)S(1)} %pad_maximum_fusion.8), channel_id=1, source_target_pairs={{0,8},{4,12},{8,16},{12,20},{16,24},{20,28},{1,9},{5,13},{9,17},{1... | collective-permute-start | bytes 737288 | tf_op jit(solution)/shard_map/ppermute | solution.py:17
  16.7 1.3 %collective-permute-start.2 = (f32[15,16,256]{2,1,0:T(8,128)S(1)}, f32[15,16,256]{2,1,0:T(8,128)S(1)}, u32[]{:S(2)}, u32[]{:S(2)}) collective-permute-start(f32[15,16,256]{2,1,0:T(8,128)S(1)} %fusion.1), channel_id=1, source_target_pairs={{8,0},{12,4},{16,8},{20,12},{24,16},{28,20},{9,1},{13,5},{17,9},{2... | collective-permute-start | bytes 737288 | tf_op jit(solution)/shard_map/ppermute | solution.py:17
  18.0 3.0 %collective-permute-done.1 = f32[15,16,256]{2,1,0:T(8,128)S(1)} collective-permute-done((f32[15,16,256]{2,1,0:T(8,128)S(1)}, f32[15,16,256]{2,1,0:T(8,128)S(1)}, u32[]{:S(2)}, u32[]{:S(2)}) %collective-permute-start.1) | collective-permute-done | bytes 245792 | tf_op jit(solution)/shard_map/ppermute | solution.py:17
  21.0 4.1 %collective-permute-done.2 = f32[15,16,256]{2,1,0:T(8,128)S(1)} collective-permute-done((f32[15,16,256]{2,1,0:T(8,128)S(1)}, f32[15,16,256]{2,1,0:T(8,128)S(1)}, u32[]{:S(2)}, u32[]{:S(2)}) %collective-permute-start.2) | collective-permute-done | bytes 245792 | tf_op jit(solution)/shard_map/ppermute | solution.py:17
  25.4 0.1 fusion.3
  25.6 1.3 %collective-permute-start.4 = (f32[370,256]{1,0:T(8,128)S(1)}, f32[370,256]{1,0:T(8,128)S(1)}, u32[]{:S(2)}, u32[]{:S(2)}) collective-permute-start(f32[370,256]{1,0:T(8,128)S(1)} %pad_maximum_fusion.2), channel_id=1, source_target_pairs={{1,0},{2,1},{3,2},{5,4},{6,5},{7,6},{9,8},{10,9},{11,10},{13,12},{... | collective-permute-start | bytes 1136648 | tf_op jit(solution)/shard_map/ppermute | solution.py:17
  26.9 3.1 %collective-permute-start.3 = (f32[370,256]{1,0:T(8,128)S(1)}, f32[370,256]{1,0:T(8,128)S(1)}, u32[]{:S(2)}, u32[]{:S(2)}) collective-permute-start(f32[370,256]{1,0:T(8,128)S(1)} %pad_maximum_fusion.1), channel_id=1, source_target_pairs={{0,1},{1,2},{2,3},{4,5},{5,6},{6,7},{8,9},{9,10},{10,11},{12,13},{... | collective-permute-start | bytes 1136648 | tf_op jit(solution)/shard_map/ppermute | solution.py:17
  30.0 0.1 pad_add_fusion.refs_0_
  30.2 1.1 %collective-permute-done.3 = f32[370,256]{1,0:T(8,128)S(1)} collective-permute-done((f32[370,256]{1,0:T(8,128)S(1)}, f32[370,256]{1,0:T(8,128)S(1)}, u32[]{:S(2)}, u32[]{:S(2)}) %collective-permute-start.3) | collective-permute-done | bytes 378912 | tf_op jit(solution)/shard_map/ppermute | solution.py:17
  31.4 0.1 select_maximum_fusion.2.refs_3_
  31.5 0.0 copy-start
  31.5 0.1 select_maximum_fusion.refs_2_
  31.7 0.7 %copy-done = f32[8,16,256]{2,1,0:T(8,128)S(1)} copy-done((f32[8,16,256]{2,1,0:T(8,128)S(1)}, f32[8,16,256]{2,1,0:T(8,128)}, u32[]{:S(2)}) %copy-start) | copy-done | bytes 131096
  32.4 17.0 %skeleton.1 = (f32[8,16,256]{2,1,0:T(8,128)S(1)}, f32[8,16,256]{2,1,0:T(8,128)S(1)}, f32[8,16,256]{2,1,0:T(8,128)S(1)}, f32[128,128]{1,0:T(8,128)S(1)}) custom-call(s32[4]{0:T(128)S(1)} %pad_add_fusion.refs_0_, f32[8,16,256]{2,1,0:T(8,128)S(1)} %copy-done, f32[28,40,256]{2,1,0:T(8,128)S(1)} %select_maximum_fusion.refs_2_, ...), custom_call_target="tpu_custom_call" | custom-call | tf_op jit(solution)/shard_map/skeleton/pallas_call | solution.py:365
  49.4 0.6 copy-done.1
  50.0 0.6 copy-done.2
  50.7 0.6 copy-done.3
  51.3 17.4 %all_to_all.11 = f32[32,4,128]{2,1,0:T(4,128)} all-to-all(f32[32,4,128]{2,1,0:T(4,128)S(1)} %bitcast.5), channel_id=1, replica_groups=mesh['gx'=8,'gy'=4] {'gx','gy'}, dimensions={0} | all-to-all | bytes 131072 | tf_op jit(solution)/shard_map/all_to_all | solution.py:374
  68.7 1.9 %combine.1 = (f32[8,16,256]{2,1,0:T(8,128)}, f32[1]{0:T(128)}) custom-call(f32[128,128]{1,0:T(8,128)} %bitcast.6, f32[8,16,256]{2,1,0:T(8,128)} %copy-done.1, f32[8,16,256]{2,1,0:T(8,128)} %copy-done.2, f32[8,16,256]{2,1,0:T(8,128)} %copy-done.3), custom_call_target="tpu_custom_call" | custom-call | tf_op jit(solution)/shard_map/combine/pallas_call | solution.py:375
  (32 shorter events, 0.6 us)
Async XLA Ops:
  2.5 9.3 %collective-permute-start = (f32[16,16,256]{2,1,0:T(8,128)S(1)}, f32[16,16,256]{2,1,0:T(8,128)S(1)}, u32[]{:S(2)}, u32[]{:S(2)}) collective-permute-start(f32[16,16,256]{2,1,0:T(8,128)S(1)} %pad_maximum_fusion.7), channel_id=1, source_target_pairs={{0,4},{4,0},{8,12},{12,8},{16,20},{20,16},{24,28},{28,24},{1,5},{5... | collective-permute-start | bytes 786440 | tf_op jit(solution)/shard_map/ppermute | solution.py:22
  12.9 8.0 %collective-permute-start.1 = (f32[15,16,256]{2,1,0:T(8,128)S(1)}, f32[15,16,256]{2,1,0:T(8,128)S(1)}, u32[]{:S(2)}, u32[]{:S(2)}) collective-permute-start(f32[15,16,256]{2,1,0:T(8,128)S(1)} %pad_maximum_fusion.8), channel_id=1, source_target_pairs={{0,8},{4,12},{8,16},{12,20},{16,24},{20,28},{1,9},{5,13},{9,17},{1... | collective-permute-start | bytes 737288 | tf_op jit(solution)/shard_map/ppermute | solution.py:17
  16.7 8.4 %collective-permute-start.2 = (f32[15,16,256]{2,1,0:T(8,128)S(1)}, f32[15,16,256]{2,1,0:T(8,128)S(1)}, u32[]{:S(2)}, u32[]{:S(2)}) collective-permute-start(f32[15,16,256]{2,1,0:T(8,128)S(1)} %fusion.1), channel_id=1, source_target_pairs={{8,0},{12,4},{16,8},{20,12},{24,16},{28,20},{9,1},{13,5},{17,9},{2... | collective-permute-start | bytes 737288 | tf_op jit(solution)/shard_map/ppermute | solution.py:17
  25.6 4.5 %collective-permute-start.4 = (f32[370,256]{1,0:T(8,128)S(1)}, f32[370,256]{1,0:T(8,128)S(1)}, u32[]{:S(2)}, u32[]{:S(2)}) collective-permute-start(f32[370,256]{1,0:T(8,128)S(1)} %pad_maximum_fusion.2), channel_id=1, source_target_pairs={{1,0},{2,1},{3,2},{5,4},{6,5},{7,6},{9,8},{10,9},{11,10},{13,12},{... | collective-permute-start | bytes 1136648 | tf_op jit(solution)/shard_map/ppermute | solution.py:17
  26.9 4.4 %collective-permute-start.3 = (f32[370,256]{1,0:T(8,128)S(1)}, f32[370,256]{1,0:T(8,128)S(1)}, u32[]{:S(2)}, u32[]{:S(2)}) collective-permute-start(f32[370,256]{1,0:T(8,128)S(1)} %pad_maximum_fusion.1), channel_id=1, source_target_pairs={{0,1},{1,2},{2,3},{4,5},{5,6},{6,7},{8,9},{9,10},{10,11},{12,13},{... | collective-permute-start | bytes 1136648 | tf_op jit(solution)/shard_map/ppermute | solution.py:17
  31.5 0.9 %copy-start = (f32[8,16,256]{2,1,0:T(8,128)S(1)}, f32[8,16,256]{2,1,0:T(8,128)}, u32[]{:S(2)}) copy-start(f32[8,16,256]{2,1,0:T(8,128)} %refs_1_.1) | copy-start | bytes 393220
  49.4 0.7 copy-start.1
  50.0 0.6 copy-start.2
  50.7 0.6 copy-start.3

commit v3 on v2

--- a/solution.py
+++ b/solution.py
@@ -11,54 +11,54 @@
 softness_factor = 0.1
 
 
-def shifted(block, axis, step):
+def moved(block, axis, target):
     count = lax.axis_size(axis)
-    pairs = [(i, i + step) for i in range(count) if 0 <= i + step < count]
+    pairs = [(i, target(i)) for i in range(count) if 0 <= target(i) < count]
     return lax.ppermute(block, axis, pairs)
 
 
-def swapped(block, axis):
-    count = lax.axis_size(axis)
-    return lax.ppermute(block, axis, [(i, i ^ 1) for i in range(count)])
-
-
-def with_halo(prediction, mask_field):
-    rows, cols, _ = prediction.shape
+def with_halo(packed, rows):
     wide, thin = 2 * REACH, REACH
+    rest = wide - rows
+    cols = packed.shape[1]
     odd = lax.rem(lax.axis_index("gx"), 2) == 1
-    other = swapped(jnp.concatenate([prediction, mask_field], 0), "gx")
+    other = moved(packed, "gx", lambda i: i ^ 1)
+    own_pred, own_mask = packed[:rows], packed[rows:]
     other_pred, other_mask = other[:rows], other[rows:]
-    low_pred = jnp.where(odd, other_pred, prediction)
-    high_pred = jnp.where(odd, prediction, other_pred)
-    low_mask = jnp.where(odd, other_mask, mask_field)
-    high_mask = jnp.where(odd, mask_field, other_mask)
-    pair_pred = jnp.concatenate([low_pred, high_pred], 0)
-    pair_mask = jnp.concatenate([low_mask, high_mask], 0)
-    below = shifted(jnp.concatenate([pair_pred[-wide:], pair_mask[-thin:]], 0), "gx", 2)
-    above = shifted(jnp.concatenate([pair_pred[:wide], pair_mask[:thin]], 0), "gx", -2)
-    all_pred = jnp.concatenate([below[:wide], pair_pred, above[:wide]], 0)
-    all_mask = jnp.concatenate([below[wide:], pair_mask, above[wide:]], 0)
-    tall_pred = jnp.where(odd, all_pred[rows : 2 * rows + 2 * wide], all_pred[: rows + 2 * wide])
-    tall_mask = jnp.where(odd, all_mask[rows : 2 * rows + 2 * thin], all_mask[: rows + 2 * thin])
-
-    tall = tall_pred.shape[0]
-    short = tall_mask.shape[0]
-
-    def packed(p, m):
+    outer = jnp.where(
+        odd,
+        jnp.concatenate([other_pred, own_pred[:rest], other_mask[:thin]], 0),
+        jnp.concatenate([own_pred[rows - rest :], other_pred, other_mask[rows - thin :]], 0),
+    )
+    inner = jnp.where(odd, own_pred[rows - rest :], own_pred[:rest])
+    far = moved(outer, "gx", lambda i: i - 2 if i % 2 else i + 2)
+    near = moved(inner, "gx", lambda i: i + 2 if i % 2 else i - 2)
+    tall_pred = jnp.where(
+        odd,
+        jnp.concatenate([near, other_pred, own_pred, far[:wide]], 0),
+        jnp.concatenate([far[:wide], own_pred, other_pred, near], 0),
+    )
+    tall_mask = jnp.where(
+        odd,
+        jnp.concatenate([other_mask[rows - thin :], own_mask, far[wide:]], 0),
+        jnp.concatenate([far[wide:], own_mask, other_mask[:thin]], 0),
+    )
+    tall, short = tall_pred.shape[0], tall_mask.shape[0]
+
+    def side(p, m):
         return jnp.concatenate([p.reshape(tall * wide, -1), m.reshape(short * thin, -1)], 0)
 
-    left = shifted(packed(tall_pred[:, -wide:], tall_mask[:, -thin:]), "gy", 1)
-    right = shifted(packed(tall_pred[:, :wide], tall_mask[:, :thin]), "gy", -1)
-
-    def unpacked(b):
+    def unside(b):
         return b[: tall * wide].reshape(tall, wide, -1), b[tall * wide :].reshape(short, thin, -1)
 
-    left_pred, left_mask = unpacked(left)
-    right_pred, right_mask = unpacked(right)
-    return (
-        jnp.concatenate([left_pred, tall_pred, right_pred], 1),
-        jnp.concatenate([left_mask, tall_mask, right_mask], 1),
-    )
+    left_pred, left_mask = unside(moved(side(tall_pred[:, -wide:], tall_mask[:, -thin:]), "gy", lambda i: i + 1))
+    right_pred, right_mask = unside(moved(side(tall_pred[:, :wide], tall_mask[:, :thin]), "gy", lambda i: i - 1))
+
+    def framed(parts):
+        count = sum(p.shape[1] for p in parts)
+        return jnp.pad(jnp.concatenate(parts, 1), ((0, 0), (0, tiles_for(count) * SUBLANES - count), (0, 0)))
+
+    return framed([left_pred, tall_pred, right_pred]), framed([left_mask, tall_mask, right_mask])
 
 
 WIDE = 2 * REACH
@@ -95,16 +95,14 @@
 
 
 def over_tiles(count, step):
-    def body(i, carry):
-        step(pl.multiple_of(i * SUBLANES, SUBLANES))
-        return carry
-
-    lax.fori_loop(0, tiles_for(count), body, 0)
-
-
-def skeleton_kernel(rows, cols, place, own_pred, pred, label, by_label, by_one, mask_skel, sums, *scratch):
+    for i in range(tiles_for(count)):
+        step(i * SUBLANES)
+
+
+def skeleton_kernel(rows, cols, place, own_pred, pred, label, results, sums, *scratch):
     t = softness_factor
     scratch = list(scratch)
+    by_label, by_one, mask_skel = (results.at[i] for i in range(3))
     powers = scratch[:5]
     inverses = scratch[5:9]
     opened = scratch[9:13]
@@ -296,18 +294,15 @@
         return tuple(totals)
 
     nothing = jnp.zeros((SUBLANES, LANES), jnp.float32)
-    totals = lax.fori_loop(
-        0,
-        tiles_for(cols),
-        lambda i, c: finish(pl.multiple_of(i * SUBLANES, SUBLANES), c),
-        (nothing,) * 4,
-    )
+    totals = (nothing,) * 4
+    for i in range(tiles_for(cols)):
+        totals = finish(i * SUBLANES, totals)
     packed = jnp.concatenate([jnp.sum(v, 0, keepdims=True) for v in totals] * 2, 0)
     for i in range(sums.shape[0] // SUBLANES):
         sums[i * SUBLANES : (i + 1) * SUBLANES, :] = packed
 
 
-def combine_kernel(cells, got, by_label, by_one, mask_skel, gradient, loss):
+def combine_kernel(cells, got, results, gradient, loss):
     total = jnp.zeros((SUBLANES, LANES), jnp.float32)
     for i in range(got.shape[0] // SUBLANES):
         total += got[i * SUBLANES : (i + 1) * SUBLANES, :]
@@ -328,17 +323,17 @@
         for v in (coef_intersection, coef_mass, coef_cross)
     )
     for x in range(gradient.shape[0]):
-        gradient[x] = a * by_label[x] + b * by_one[x] + c * mask_skel[x]
+        gradient[x] = a * results[0, x] + b * results[1, x] + c * results[2, x]
 
 
 def local(prediction, vessel_mask):
     rows, cols, depth = prediction.shape
-    mask_field = vessel_mask.astype(jnp.float32)
+    packed = jnp.concatenate([prediction, vessel_mask.astype(jnp.float32)], 0)
     gx, gy = lax.axis_size("gx"), lax.axis_size("gy")
     place = jnp.stack(
         [lax.axis_index("gx") * rows, lax.axis_index("gy") * cols, jnp.int32(gx * rows), jnp.int32(gy * cols)]
     ).astype(jnp.int32)
-    pred_ext, mask_ext = with_halo(prediction, mask_field)
+    pred_ext, mask_ext = with_halo(packed, rows)
 
     def held(width, margin=2):
         return pltpu.VMEM((rows + 2 * width, 2, tiles_for(cols + 2 * width + margin + 6) * SUBLANES, LANES), jnp.float32)
@@ -358,27 +353,23 @@
     block = jax.ShapeDtypeStruct((rows, cols, depth), jnp.float32)
     vmem = pl.BlockSpec(memory_space=pltpu.VMEM)
     smem = pl.BlockSpec(memory_space=pltpu.SMEM)
-    pad = tiles_for(cols + 2 * WIDE) * SUBLANES - (cols + 2 * WIDE)
-    pred_ext = jnp.pad(pred_ext, ((0, 0), (0, pad), (0, 0)))
-    pad = tiles_for(cols + 2 * REACH) * SUBLANES - (cols + 2 * REACH)
-    mask_ext = jnp.pad(mask_ext, ((0, 0), (0, pad), (0, 0)))
-    by_label, by_one, mask_skel, sums = pl.pallas_call(
+    results, sums = pl.pallas_call(
         lambda *refs: skeleton_kernel(rows, cols, *refs),
-        out_shape=[block, block, block, jax.ShapeDtypeStruct((gx * gy * 4, LANES), jnp.float32)],
+        out_shape=[jax.ShapeDtypeStruct((3, rows, cols, depth), jnp.float32), jax.ShapeDtypeStruct((gx * gy * 4, LANES), jnp.float32)],
         in_specs=[smem, vmem, vmem, vmem],
-        out_specs=[vmem] * 4,
+        out_specs=[vmem] * 2,
         scratch_shapes=scratch,
         compiler_params=pltpu.CompilerParams(vmem_limit_bytes=VMEM_BYTES),
         name="skeleton",
-    )(place, prediction, pred_ext, mask_ext)
+    )(place, packed[:rows], pred_ext, mask_ext)
     got = lax.all_to_all(sums, ("gx", "gy"), 0, 0, tiled=True)
     gradient, loss = pl.pallas_call(
         lambda *refs: combine_kernel(float(gx * rows * gy * cols * depth), *refs),
         out_shape=[block, jax.ShapeDtypeStruct((1,), jnp.float32)],
-        in_specs=[vmem] * 4,
+        in_specs=[vmem] * 2,
         out_specs=[vmem, smem],
         name="combine",
-    )(got, by_label, by_one, mask_skel)
+    )(got, results)
     return (gradient, loss[0])
 
 

time: 70.9 us -> 58.4 us (0.82)
  Pallas kernels: 18.8 us -> 12.1 us
  waiting for transfers between devices: 14.5 us -> 11 us
  local copies, waits for them, and re-layouts: 3.13 us -> 1.18 us
    pallas_call x1, Pallas kernels: 17 us -> 10.3 us  [local(): pl.pallas_call(lambda *refs: skeleton_kernel(rows, cols, *refs), out_shap...]
    ppermute x5, waiting for transfers between devices: 14.5 us -> 11 us  [moved(): return lax.ppermute(block, axis, pairs)]
    unnamed x8 -> x4, local copies, waits for them, and re-layouts: 2.69 us -> 0.74 us
  transfers between devices with their start and end apart: 5 -> 5, of which waited for: 4 -> 4; matrix products, arithmetic and copies ran while one was open for 0% -> 2% of each run, Pallas kernels for 0% -> 0%
where the time goes in v3:
time: 58.4 us; the launch traced here: 58.1 us
  blocking collectives  17.3 us (30%)
  starting transfers between devices  12.5 us (21%)
  Pallas kernels  12.1 us (21%)
  waiting for transfers between devices  11 us (19%)
  other arithmetic  3.09 us (5%)
  local copies, waits for them, and re-layouts  1.18 us (2%)
  between operations  0.87 us (1%)
    all_to_all x1, blocking collectives, local(): got = lax.all_to_all(sums, ('gx', 'gy'), 0, 0, tiled=True)  17.3 us
    ppermute x5, starting transfers between devices, moved(): return lax.ppermute(block, axis, pairs)  12.5 us
    ppermute x5, waiting for transfers between devices, moved(): return lax.ppermute(block, axis, pairs)  11 us
    pallas_call x1, Pallas kernels, local(): pl.pallas_call(lambda *refs: skeleton_kernel(rows, cols, *refs), out_shap...  10.3 us
    pallas_call x1, Pallas kernels, local(): pl.pallas_call(lambda *refs: combine_kernel(float(gx * rows * gy * cols *...  1.84 us
  transfers between devices with their start and end apart: 5, of which 4 were waited for; matrix products, arithmetic and copies ran while one was open for 2% of the time, Pallas kernels for 0%

profile of v3, /device:TPU:0, one launch (start us, length us, event | category | flops | bytes accessed | tf_op | source)
XLA Modules:
  0.0 58.1 jit_solution(4771069899302727004)
XLA Ops:
  0.6 0.9 %convert_element_type.7 = f32[8,16,256]{2,1,0:T(8,128)S(1)} convert(s32[8,16,256]{2,1,0:T(8,128)} %param.3) | non-fusion elementwise | flops 32768 | bytes 262144 | tf_op jit(solution)/shard_map/convert_element_type | solution.py:331
  1.5 0.9 %pad_maximum_fusion.6 = f32[16,16,256]{2,1,0:T(8,128)S(1)} fusion(f32[8,16,256]{2,1,0:T(8,128)S(1)} %convert_element_type.7, f32[8,16,256]{2,1,0:T(8,128)} %refs_1_.1), kind=kLoop, calls=%fused_computation.19 | loop fusion | flops 65536 | bytes 524288 | tf_op jit(solution)/shard_map/concatenate | solution.py:331
  2.5 3.0 %collective-permute-start.1 = (f32[16,16,256]{2,1,0:T(8,128)S(1)}, f32[16,16,256]{2,1,0:T(8,128)S(1)}, u32[]{:S(2)}, u32[]{:S(2)}) collective-permute-start(f32[16,16,256]{2,1,0:T(8,128)S(1)} %pad_maximum_fusion.6), channel_id=1, source_target_pairs={{0,4},{4,0},{8,12},{12,8},{16,20},{20,16},{24,28},{28,24},{1,5},{5... | collective-permute-start | bytes 786440 | tf_op jit(solution)/shard_map/ppermute | solution.py:17
  5.5 0.8 %broadcast_select_fusion = (f32[2,16,256]{2,1,0:T(8,128)S(1)}, f32[2,16,256]{2,1,0:T(8,128)S(1)}, f32[2,16,256]{2,1,0:T(8,128)S(1)}) fusion(pred[]{:T(512)S(6)} %eq.3, f32[8,16,256]{2,1,0:T(8,128)} %refs_1_.1), kind=kLoop, calls=%fused_computation.21 | loop fusion | flops 8192 | bytes 163841 | tf_op jit(solution)/shard_map/jit(_where)/select_n | solution.py:33
  6.3 5.5 %collective-permute-done.1 = f32[16,16,256]{2,1,0:T(8,128)S(1)} collective-permute-done((f32[16,16,256]{2,1,0:T(8,128)S(1)}, f32[16,16,256]{2,1,0:T(8,128)S(1)}, u32[]{:S(2)}, u32[]{:S(2)}) %collective-permute-start.1) | collective-permute-done | bytes 262176 | tf_op jit(solution)/shard_map/ppermute | solution.py:17
  11.9 0.0 copy-start
  11.9 3.8 %collective-permute-start.2 = (f32[15,16,256]{2,1,0:T(8,128)S(1)}, f32[15,16,256]{2,1,0:T(8,128)S(1)}, u32[]{:S(2)}, u32[]{:S(2)}) collective-permute-start(f32[15,16,256]{2,1,0:T(8,128)S(1)} %maximum_select_fusion), channel_id=1, source_target_pairs={{0,8},{8,16},{12,4},{16,24},{20,12},{28,20},{1,9},{9,17},{13,5},{1... | collective-permute-start | bytes 737288 | tf_op jit(solution)/shard_map/ppermute | solution.py:17
  15.8 1.3 %collective-permute-start = (f32[2,16,256]{2,1,0:T(8,128)S(1)}, f32[2,16,256]{2,1,0:T(8,128)S(1)}, u32[]{:S(2)}, u32[]{:S(2)}) collective-permute-start(f32[2,16,256]{2,1,0:T(8,128)S(1)} %get-tuple-element.16), channel_id=1, source_target_pairs={{4,12},{8,0},{12,20},{16,8},{20,28},{24,16},{5,13},{9,1},{13,21},{... | collective-permute-start | bytes 98312 | tf_op jit(solution)/shard_map/ppermute | solution.py:17
  17.1 3.0 %collective-permute-done.2 = f32[15,16,256]{2,1,0:T(8,128)S(1)} collective-permute-done((f32[15,16,256]{2,1,0:T(8,128)S(1)}, f32[15,16,256]{2,1,0:T(8,128)S(1)}, u32[]{:S(2)}, u32[]{:S(2)}) %collective-permute-start.2) | collective-permute-done | bytes 245792 | tf_op jit(solution)/shard_map/ppermute | solution.py:17
  20.2 1.4 %collective-permute-done = f32[2,16,256]{2,1,0:T(8,128)S(1)} collective-permute-done((f32[2,16,256]{2,1,0:T(8,128)S(1)}, f32[2,16,256]{2,1,0:T(8,128)S(1)}, u32[]{:S(2)}, u32[]{:S(2)}) %collective-permute-start) | collective-permute-done | bytes 32800 | tf_op jit(solution)/shard_map/ppermute | solution.py:17
  21.6 0.0 copy-done
  21.6 0.1 fusion.7
  21.8 1.3 %collective-permute-start.4 = (f32[370,256]{1,0:T(8,128)S(1)}, f32[370,256]{1,0:T(8,128)S(1)}, u32[]{:S(2)}, u32[]{:S(2)}) collective-permute-start(f32[370,256]{1,0:T(8,128)S(1)} %pad_maximum_fusion.3), channel_id=1, source_target_pairs={{1,0},{2,1},{3,2},{5,4},{6,5},{7,6},{9,8},{10,9},{11,10},{13,12},{... | collective-permute-start | bytes 1136648 | tf_op jit(solution)/shard_map/ppermute | solution.py:17
  23.2 3.1 %collective-permute-start.3 = (f32[370,256]{1,0:T(8,128)S(1)}, f32[370,256]{1,0:T(8,128)S(1)}, u32[]{:S(2)}, u32[]{:S(2)}) collective-permute-start(f32[370,256]{1,0:T(8,128)S(1)} %pad_maximum_fusion.2), channel_id=1, source_target_pairs={{0,1},{1,2},{2,3},{4,5},{5,6},{6,7},{8,9},{9,10},{10,11},{12,13},{... | collective-permute-start | bytes 1136648 | tf_op jit(solution)/shard_map/ppermute | solution.py:17
  26.2 0.1 pad_add_fusion.refs_0_
  26.3 0.0 collective-permute-done.4
  26.4 1.1 %collective-permute-done.3 = f32[370,256]{1,0:T(8,128)S(1)} collective-permute-done((f32[370,256]{1,0:T(8,128)S(1)}, f32[370,256]{1,0:T(8,128)S(1)}, u32[]{:S(2)}, u32[]{:S(2)}) %collective-permute-start.3) | collective-permute-done | bytes 378912 | tf_op jit(solution)/shard_map/ppermute | solution.py:17
  27.6 0.1 select_maximum_fusion.2.refs_3_
  27.7 0.1 select_maximum_fusion.refs_2_
  27.9 10.3 %skeleton.1 = (f32[3,8,16,256]{3,2,1,0:T(8,128)S(1)}, f32[128,128]{1,0:T(8,128)S(1)}) custom-call(s32[4]{0:T(128)S(1)} %pad_add_fusion.refs_0_, f32[8,16,256]{2,1,0:T(8,128)S(1)} %copy-done, f32[28,40,256]{2,1,0:T(8,128)S(1)} %select_maximum_fusion.refs_2_, f32[18,32,256]{2,1,0:T(8,128)S(1)} %select_maximum_fusion.2.refs_3_), custom_call_target="tpu_custom_call" | custom-call | tf_op jit(solution)/shard_map/skeleton/pallas_call | solution.py:356
  38.2 0.0 copy-start.1
  38.2 0.7 %copy-done.1 = f32[3,8,16,256]{3,2,1,0:T(8,128)} copy-done((f32[3,8,16,256]{3,2,1,0:T(8,128)}, f32[3,8,16,256]{3,2,1,0:T(8,128)S(1)}, u32[]{:S(2)}) %copy-start.1) | copy-done | bytes 393240
  38.9 17.3 %all_to_all.11 = f32[32,4,128]{2,1,0:T(4,128)} all-to-all(f32[32,4,128]{2,1,0:T(4,128)S(1)} %bitcast.5), channel_id=1, replica_groups=mesh['gx'=8,'gy'=4] {'gx','gy'}, dimensions={0} | all-to-all | bytes 131072 | tf_op jit(solution)/shard_map/all_to_all | solution.py:365
  56.2 1.8 %combine.1 = (f32[8,16,256]{2,1,0:T(8,128)}, f32[1]{0:T(128)}) custom-call(f32[128,128]{1,0:T(8,128)} %bitcast.6, f32[3,8,16,256]{3,2,1,0:T(8,128)} %copy-done.1), custom_call_target="tpu_custom_call" | custom-call | tf_op jit(solution)/shard_map/combine/pallas_call | solution.py:366
  (23 shorter events, 0.5 us)
Async XLA Ops:
  2.5 9.3 %collective-permute-start.1 = (f32[16,16,256]{2,1,0:T(8,128)S(1)}, f32[16,16,256]{2,1,0:T(8,128)S(1)}, u32[]{:S(2)}, u32[]{:S(2)}) collective-permute-start(f32[16,16,256]{2,1,0:T(8,128)S(1)} %pad_maximum_fusion.6), channel_id=1, source_target_pairs={{0,4},{4,0},{8,12},{12,8},{16,20},{20,16},{24,28},{28,24},{1,5},{5... | collective-permute-start | bytes 786440 | tf_op jit(solution)/shard_map/ppermute | solution.py:17
  11.9 9.7 %copy-start = (f32[8,16,256]{2,1,0:T(8,128)S(1)}, f32[8,16,256]{2,1,0:T(8,128)}, u32[]{:S(2)}) copy-start(f32[8,16,256]{2,1,0:T(8,128)} %refs_1_.1) | copy-start | bytes 393220
  11.9 8.2 %collective-permute-start.2 = (f32[15,16,256]{2,1,0:T(8,128)S(1)}, f32[15,16,256]{2,1,0:T(8,128)S(1)}, u32[]{:S(2)}, u32[]{:S(2)}) collective-permute-start(f32[15,16,256]{2,1,0:T(8,128)S(1)} %maximum_select_fusion), channel_id=1, source_target_pairs={{0,8},{8,16},{12,4},{16,24},{20,12},{28,20},{1,9},{9,17},{13,5},{1... | collective-permute-start | bytes 737288 | tf_op jit(solution)/shard_map/ppermute | solution.py:17
  15.8 5.8 %collective-permute-start = (f32[2,16,256]{2,1,0:T(8,128)S(1)}, f32[2,16,256]{2,1,0:T(8,128)S(1)}, u32[]{:S(2)}, u32[]{:S(2)}) collective-permute-start(f32[2,16,256]{2,1,0:T(8,128)S(1)} %get-tuple-element.16), channel_id=1, source_target_pairs={{4,12},{8,0},{12,20},{16,8},{20,28},{24,16},{5,13},{9,1},{13,21},{... | collective-permute-start | bytes 98312 | tf_op jit(solution)/shard_map/ppermute | solution.py:17
  21.8 4.5 %collective-permute-start.4 = (f32[370,256]{1,0:T(8,128)S(1)}, f32[370,256]{1,0:T(8,128)S(1)}, u32[]{:S(2)}, u32[]{:S(2)}) collective-permute-start(f32[370,256]{1,0:T(8,128)S(1)} %pad_maximum_fusion.3), channel_id=1, source_target_pairs={{1,0},{2,1},{3,2},{5,4},{6,5},{7,6},{9,8},{10,9},{11,10},{13,12},{... | collective-permute-start | bytes 1136648 | tf_op jit(solution)/shard_map/ppermute | solution.py:17
  23.2 4.4 %collective-permute-start.3 = (f32[370,256]{1,0:T(8,128)S(1)}, f32[370,256]{1,0:T(8,128)S(1)}, u32[]{:S(2)}, u32[]{:S(2)}) collective-permute-start(f32[370,256]{1,0:T(8,128)S(1)} %pad_maximum_fusion.2), channel_id=1, source_target_pairs={{0,1},{1,2},{2,3},{4,5},{5,6},{6,7},{8,9},{9,10},{10,11},{12,13},{... | collective-permute-start | bytes 1136648 | tf_op jit(solution)/shard_map/ppermute | solution.py:17
  38.2 0.7 %copy-start.1 = (f32[3,8,16,256]{3,2,1,0:T(8,128)}, f32[3,8,16,256]{3,2,1,0:T(8,128)S(1)}, u32[]{:S(2)}) copy-start(f32[3,8,16,256]{3,2,1,0:T(8,128)S(1)} %get-tuple-element.7.refs_1_) | copy-start | bytes 1179652

commit v4 on v3

--- a/solution.py
+++ b/solution.py
@@ -20,29 +20,13 @@
 def with_halo(packed, rows):
     wide, thin = 2 * REACH, REACH
     rest = wide - rows
-    cols = packed.shape[1]
-    odd = lax.rem(lax.axis_index("gx"), 2) == 1
-    other = moved(packed, "gx", lambda i: i ^ 1)
     own_pred, own_mask = packed[:rows], packed[rows:]
-    other_pred, other_mask = other[:rows], other[rows:]
-    outer = jnp.where(
-        odd,
-        jnp.concatenate([other_pred, own_pred[:rest], other_mask[:thin]], 0),
-        jnp.concatenate([own_pred[rows - rest :], other_pred, other_mask[rows - thin :]], 0),
-    )
-    inner = jnp.where(odd, own_pred[rows - rest :], own_pred[:rest])
-    far = moved(outer, "gx", lambda i: i - 2 if i % 2 else i + 2)
-    near = moved(inner, "gx", lambda i: i + 2 if i % 2 else i - 2)
-    tall_pred = jnp.where(
-        odd,
-        jnp.concatenate([near, other_pred, own_pred, far[:wide]], 0),
-        jnp.concatenate([far[:wide], own_pred, other_pred, near], 0),
-    )
-    tall_mask = jnp.where(
-        odd,
-        jnp.concatenate([other_mask[rows - thin :], own_mask, far[wide:]], 0),
-        jnp.concatenate([far[wide:], own_mask, other_mask[:thin]], 0),
-    )
+    up = moved(jnp.concatenate([own_pred, own_mask[rows - thin :]], 0), "gx", lambda i: i + 1)
+    down = moved(jnp.concatenate([own_pred, own_mask[:thin]], 0), "gx", lambda i: i - 1)
+    far_up = moved(own_pred[rows - rest :], "gx", lambda i: i + 2)
+    far_down = moved(own_pred[:rest], "gx", lambda i: i - 2)
+    tall_pred = jnp.concatenate([far_up, up[:rows], own_pred, down[:rows], far_down], 0)
+    tall_mask = jnp.concatenate([up[rows:], own_mask, down[rows:]], 0)
     tall, short = tall_pred.shape[0], tall_mask.shape[0]
 
     def side(p, m):
@@ -102,7 +86,9 @@
 def skeleton_kernel(rows, cols, place, own_pred, pred, label, results, sums, *scratch):
     t = softness_factor
     scratch = list(scratch)
-    by_label, by_one, mask_skel = (results.at[i] for i in range(3))
+    stage, copied = scratch[48:]
+    by_label, by_one, mask_skel = (stage.at[i] for i in range(3))
+    copies = [pltpu.make_async_copy(stage.at[i], results.at[i], copied.at[i]) for i in range(3)]
     powers = scratch[:5]
     inverses = scratch[5:9]
     opened = scratch[9:13]
@@ -194,6 +180,7 @@
                 mask_skel[x, pl.ds(base, SUBLANES), h * LANES : (h + 1) * LANES] = t * skel
 
     over_tiles(cols, label_chain)
+    copies[2].start()
 
     def spread_label(base):
         for x in range(rows + 2 * REACH):
@@ -234,11 +221,8 @@
                     spreads[LEVELS + j][x, h, pl.ds(base, SUBLANES), :] = seed * spread
 
     def chain_tile(base):
-        def body(i, carry):
+        for i in range((rows + 2 * REACH) // chunk):
             chain_chunk(base, i * chunk)
-            return carry
-
-        lax.fori_loop(0, (rows + 2 * REACH) // chunk, body, 0)
 
     over_tiles(cols + 2 * REACH, chain_tile)
 
@@ -297,9 +281,13 @@
     totals = (nothing,) * 4
     for i in range(tiles_for(cols)):
         totals = finish(i * SUBLANES, totals)
+    copies[0].start()
+    copies[1].start()
     packed = jnp.concatenate([jnp.sum(v, 0, keepdims=True) for v in totals] * 2, 0)
     for i in range(sums.shape[0] // SUBLANES):
         sums[i * SUBLANES : (i + 1) * SUBLANES, :] = packed
+    for copy in copies:
+        copy.wait()
 
 
 def combine_kernel(cells, got, results, gradient, loss):
@@ -328,7 +316,10 @@
 
 def local(prediction, vessel_mask):
     rows, cols, depth = prediction.shape
-    packed = jnp.concatenate([prediction, vessel_mask.astype(jnp.float32)], 0)
+    none = (0, 0)
+    packed = lax.optimization_barrier(
+        jnp.pad(prediction, ((0, rows), none, none)) + jnp.pad(vessel_mask, ((rows, 0), none, none)).astype(jnp.float32)
+    )
     gx, gy = lax.axis_size("gx"), lax.axis_size("gy")
     place = jnp.stack(
         [lax.axis_index("gx") * rows, lax.axis_index("gy") * cols, jnp.int32(gx * rows), jnp.int32(gy * cols)]
@@ -349,6 +340,7 @@
         + [held(REACH - k) for k in range(LEVELS + 1)]
         + [held(REACH - k) for k in range(1, LEVELS + 1)]
         + [held(0)] * 4
+        + [pltpu.VMEM((3, rows, cols, depth), jnp.float32), pltpu.SemaphoreType.DMA((3,))]
     )
     block = jax.ShapeDtypeStruct((rows, cols, depth), jnp.float32)
     vmem = pl.BlockSpec(memory_space=pltpu.VMEM)
@@ -357,7 +349,7 @@
         lambda *refs: skeleton_kernel(rows, cols, *refs),
         out_shape=[jax.ShapeDtypeStruct((3, rows, cols, depth), jnp.float32), jax.ShapeDtypeStruct((gx * gy * 4, LANES), jnp.float32)],
         in_specs=[smem, vmem, vmem, vmem],
-        out_specs=[vmem] * 2,
+        out_specs=[pl.BlockSpec(memory_space=pltpu.HBM), vmem],
         scratch_shapes=scratch,
         compiler_params=pltpu.CompilerParams(vmem_limit_bytes=VMEM_BYTES),
         name="skeleton",

time: 58.4 us -> 54.9 us (0.940)
  blocking collectives: 17.3 us -> 15.4 us
  other arithmetic: 3.09 us -> 1.39 us
  Pallas kernels: 12.1 us -> 11 us
  starting transfers between devices: 12.5 us -> 13.5 us
    all_to_all x1, blocking collectives: 17.3 us -> 15.4 us  [local(): got = lax.all_to_all(sums, ('gx', 'gy'), 0, 0, tiled=True)]
    pallas_call x1, Pallas kernels: 10.3 us -> 9.13 us  [local(): pl.pallas_call(lambda *refs: skeleton_kernel(rows, cols, *refs), out_shap...]
    ppermute x5 -> x6, starting transfers between devices: 12.5 us -> 13.5 us  [moved(): return lax.ppermute(block, axis, pairs)]
    add x0 -> x1, other arithmetic: none -> 0.99 us  [local(): jnp.pad(prediction, ((0, rows), none, none))]
    convert_element_type x1 -> x0, other arithmetic: 0.92 us -> none  [local(): packed = jnp.concatenate([prediction, vessel_mask.astype(jnp.float32)], 0)]
    concatenate x1 -> x2, other arithmetic: 0.93 us -> 0.04 us  [the longest x1 0.02 us: with_halo(): tall_mask = jnp.concatenate([up[rows:], own_mask, down[rows:]], 0)]
    select_n x4 -> x0, other arithmetic: 0.87 us -> none  [the longest x1 0.78 us: with_halo(): inner = jnp.where(odd, own_pred[rows - rest:], own_pred[:rest])]
    ppermute x5 -> x6, waiting for transfers between devices: 11 us -> 11.1 us  [moved(): return lax.ppermute(block, axis, pairs)]
  transfers between devices with their start and end apart: 5 -> 6, of which waited for: 4 -> 3; matrix products, arithmetic and copies ran while one was open for 2% -> 1% of each run, Pallas kernels for 0% -> 0%
where the time goes in v4:
time: 54.9 us; the launch traced here: 54.6 us
  blocking collectives  15.4 us (28%)
  starting transfers between devices  13.5 us (25%)
  waiting for transfers between devices  11.1 us (20%)
  Pallas kernels  11 us (20%)
  other arithmetic  1.39 us (3%)
  local copies, waits for them, and re-layouts  1.23 us (2%)
  between operations  0.95 us (2%)
    all_to_all x1, blocking collectives, local(): got = lax.all_to_all(sums, ('gx', 'gy'), 0, 0, tiled=True)  15.4 us
    ppermute x6, starting transfers between devices, moved(): return lax.ppermute(block, axis, pairs)  13.5 us
    ppermute x6, waiting for transfers between devices, moved(): return lax.ppermute(block, axis, pairs)  11.1 us
    pallas_call x1, Pallas kernels, local(): pl.pallas_call(lambda *refs: skeleton_kernel(rows, cols, *refs), out_shap...  9.13 us
    pallas_call x1, Pallas kernels, local(): pl.pallas_call(lambda *refs: combine_kernel(float(gx * rows * gy * cols *...  1.84 us
  transfers between devices with their start and end apart: 6, of which 3 were waited for; matrix products, arithmetic and copies ran while one was open for 1% of the time, Pallas kernels for 0%

profile of v4, /device:TPU:0, one launch (start us, length us, event | category | flops | bytes accessed | tf_op | source)
XLA Modules:
  0.0 54.6 jit_solution(14756121872073006020)
XLA Ops:
  0.6 1.0 %convert_add_fusion = f32[16,16,256]{2,1,0:T(8,128)S(1)} fusion(s32[8,16,256]{2,1,0:T(8,128)} %param.3, f32[8,16,256]{2,1,0:T(8,128)} %param.2), kind=kLoop, calls=%fused_computation.14 | loop fusion | flops 131072 | bytes 524288 | tf_op jit(solution)/shard_map/add | solution.py:321
  1.7 4.9 %collective-permute-start.1 = (f32[13,16,256]{2,1,0:T(8,128)S(1)}, f32[13,16,256]{2,1,0:T(8,128)S(1)}, u32[]{:S(2)}, u32[]{:S(2)}) collective-permute-start(f32[13,16,256]{2,1,0:T(8,128)S(1)} %pad_maximum_fusion.3), channel_id=1, source_target_pairs={{0,4},{4,8},{8,12},{12,16},{16,20},{20,24},{24,28},{1,5},{5,9},{9,... | collective-permute-start | bytes 638984 | tf_op jit(solution)/shard_map/ppermute | solution.py:17
  6.6 3.5 %collective-permute-start = (f32[2,16,256]{2,1,0:T(8,128)S(1)}, f32[2,16,256]{2,1,0:T(8,128)S(1)}, u32[]{:S(2)}, u32[]{:S(2)}) collective-permute-start(f32[2,16,256]{2,1,0:T(8,128)S(1)} %get-tuple-element.15), channel_id=1, source_target_pairs={{0,8},{4,12},{8,16},{12,20},{16,24},{20,28},{1,9},{5,13},{9,17},{1... | collective-permute-start | bytes 98312 | tf_op jit(solution)/shard_map/ppermute | solution.py:17
  10.1 1.3 %collective-permute-start.2 = (f32[13,16,256]{2,1,0:T(8,128)S(1)}, f32[13,16,256]{2,1,0:T(8,128)S(1)}, u32[]{:S(2)}, u32[]{:S(2)}) collective-permute-start(f32[13,16,256]{2,1,0:T(8,128)S(1)} %concatenate.32), channel_id=1, source_target_pairs={{4,0},{8,4},{12,8},{16,12},{20,16},{24,20},{28,24},{5,1},{9,5},{13... | collective-permute-start | bytes 638984 | tf_op jit(solution)/shard_map/ppermute | solution.py:17
  11.4 1.3 %collective-permute-start.3 = (f32[2,16,256]{2,1,0:T(8,128)S(1)}, f32[2,16,256]{2,1,0:T(8,128)S(1)}, u32[]{:S(2)}, u32[]{:S(2)}) collective-permute-start(f32[2,16,256]{2,1,0:T(8,128)S(1)} %get-tuple-element.14), channel_id=1, source_target_pairs={{8,0},{12,4},{16,8},{20,12},{24,16},{28,20},{9,1},{13,5},{17,9},{2... | collective-permute-start | bytes 98312 | tf_op jit(solution)/shard_map/ppermute | solution.py:17
  12.7 0.0 collective-permute-done
  12.7 0.0 collective-permute-done.1
  12.8 5.6 %collective-permute-done.2 = f32[13,16,256]{2,1,0:T(8,128)S(1)} collective-permute-done((f32[13,16,256]{2,1,0:T(8,128)S(1)}, f32[13,16,256]{2,1,0:T(8,128)S(1)}, u32[]{:S(2)}, u32[]{:S(2)}) %collective-permute-start.2) | collective-permute-done | bytes 213024 | tf_op jit(solution)/shard_map/ppermute | solution.py:17
  18.5 1.6 %collective-permute-done.3 = f32[2,16,256]{2,1,0:T(8,128)S(1)} collective-permute-done((f32[2,16,256]{2,1,0:T(8,128)S(1)}, f32[2,16,256]{2,1,0:T(8,128)S(1)}, u32[]{:S(2)}, u32[]{:S(2)}) %collective-permute-start.3) | collective-permute-done | bytes 32800 | tf_op jit(solution)/shard_map/ppermute | solution.py:17
  20.1 0.1 fusion.5
  20.2 1.3 %collective-permute-start.4 = (f32[370,256]{1,0:T(8,128)S(1)}, f32[370,256]{1,0:T(8,128)S(1)}, u32[]{:S(2)}, u32[]{:S(2)}) collective-permute-start(f32[370,256]{1,0:T(8,128)S(1)} %pad_maximum_fusion), channel_id=1, source_target_pairs={{0,1},{1,2},{2,3},{4,5},{5,6},{6,7},{8,9},{9,10},{10,11},{12,13},{... | collective-permute-start | bytes 1136648 | tf_op jit(solution)/shard_map/ppermute | solution.py:17
  21.7 1.3 %collective-permute-start.5 = (f32[370,256]{1,0:T(8,128)S(1)}, f32[370,256]{1,0:T(8,128)S(1)}, u32[]{:S(2)}, u32[]{:S(2)}) collective-permute-start(f32[370,256]{1,0:T(8,128)S(1)} %pad_maximum_fusion.1), channel_id=1, source_target_pairs={{1,0},{2,1},{3,2},{5,4},{6,5},{7,6},{9,8},{10,9},{11,10},{13,12},{... | collective-permute-start | bytes 1136648 | tf_op jit(solution)/shard_map/ppermute | solution.py:17
  23.0 0.1 pad_add_fusion.refs_0_
  23.1 0.0 collective-permute-done.4
  23.1 3.9 %collective-permute-done.5 = f32[370,256]{1,0:T(8,128)S(1)} collective-permute-done((f32[370,256]{1,0:T(8,128)S(1)}, f32[370,256]{1,0:T(8,128)S(1)}, u32[]{:S(2)}, u32[]{:S(2)}) %collective-permute-start.5) | collective-permute-done | bytes 378912 | tf_op jit(solution)/shard_map/ppermute | solution.py:17
  27.2 0.1 select_maximum_fusion.2.refs_3_
  27.3 0.1 select_maximum_fusion.refs_2_
  27.4 9.1 %skeleton.1 = (f32[3,8,16,256]{3,2,1,0:T(8,128)S(1)}, f32[128,128]{1,0:T(8,128)S(1)}) custom-call(s32[4]{0:T(128)S(1)} %pad_add_fusion.refs_0_, f32[8,16,256]{2,1,0:T(8,128)S(1)} %slice.75.refs_1_, f32[28,40,256]{2,1,0:T(8,128)S(1)} %select_maximum_fusion.refs_2_, f32[18,32,256]{2,1,0:T(8,128)S(1)} %select_maximum_fusion.2.refs_3_), custom_call_target="tpu_custom_call" | custom-call | tf_op jit(solution)/shard_map/skeleton/pallas_call | solution.py:348
  36.6 0.0 copy-start
  36.6 0.7 %copy-done = f32[3,8,16,256]{3,2,1,0:T(8,128)} copy-done((f32[3,8,16,256]{3,2,1,0:T(8,128)}, f32[3,8,16,256]{3,2,1,0:T(8,128)S(1)}, u32[]{:S(2)}) %copy-start) | copy-done | bytes 393240
  37.3 15.4 %all_to_all.11 = f32[32,4,128]{2,1,0:T(4,128)} all-to-all(f32[32,4,128]{2,1,0:T(4,128)S(1)} %bitcast.5), channel_id=1, replica_groups=mesh['gx'=8,'gy'=4] {'gx','gy'}, dimensions={0} | all-to-all | bytes 131072 | tf_op jit(solution)/shard_map/all_to_all | solution.py:357
  52.7 1.8 %combine.1 = (f32[8,16,256]{2,1,0:T(8,128)}, f32[1]{0:T(128)}) custom-call(f32[128,128]{1,0:T(8,128)} %bitcast.6, f32[3,8,16,256]{3,2,1,0:T(8,128)} %copy-done), custom_call_target="tpu_custom_call" | custom-call | tf_op jit(solution)/shard_map/combine/pallas_call | solution.py:358
  (29 shorter events, 0.5 us)
Async XLA Ops:
  1.7 11.0 %collective-permute-start.1 = (f32[13,16,256]{2,1,0:T(8,128)S(1)}, f32[13,16,256]{2,1,0:T(8,128)S(1)}, u32[]{:S(2)}, u32[]{:S(2)}) collective-permute-start(f32[13,16,256]{2,1,0:T(8,128)S(1)} %pad_maximum_fusion.3), channel_id=1, source_target_pairs={{0,4},{4,8},{8,12},{12,16},{16,20},{20,24},{24,28},{1,5},{5,9},{9,... | collective-permute-start | bytes 638984 | tf_op jit(solution)/shard_map/ppermute | solution.py:17
  6.6 6.1 %collective-permute-start = (f32[2,16,256]{2,1,0:T(8,128)S(1)}, f32[2,16,256]{2,1,0:T(8,128)S(1)}, u32[]{:S(2)}, u32[]{:S(2)}) collective-permute-start(f32[2,16,256]{2,1,0:T(8,128)S(1)} %get-tuple-element.15), channel_id=1, source_target_pairs={{0,8},{4,12},{8,16},{12,20},{16,24},{20,28},{1,9},{5,13},{9,17},{1... | collective-permute-start | bytes 98312 | tf_op jit(solution)/shard_map/ppermute | solution.py:17
  10.1 8.3 %collective-permute-start.2 = (f32[13,16,256]{2,1,0:T(8,128)S(1)}, f32[13,16,256]{2,1,0:T(8,128)S(1)}, u32[]{:S(2)}, u32[]{:S(2)}) collective-permute-start(f32[13,16,256]{2,1,0:T(8,128)S(1)} %concatenate.32), channel_id=1, source_target_pairs={{4,0},{8,4},{12,8},{16,12},{20,16},{24,20},{28,24},{5,1},{9,5},{13... | collective-permute-start | bytes 638984 | tf_op jit(solution)/shard_map/ppermute | solution.py:17
  11.4 8.7 %collective-permute-start.3 = (f32[2,16,256]{2,1,0:T(8,128)S(1)}, f32[2,16,256]{2,1,0:T(8,128)S(1)}, u32[]{:S(2)}, u32[]{:S(2)}) collective-permute-start(f32[2,16,256]{2,1,0:T(8,128)S(1)} %get-tuple-element.14), channel_id=1, source_target_pairs={{8,0},{12,4},{16,8},{20,12},{24,16},{28,20},{9,1},{13,5},{17,9},{2... | collective-permute-start | bytes 98312 | tf_op jit(solution)/shard_map/ppermute | solution.py:17
  20.2 2.8 %collective-permute-start.4 = (f32[370,256]{1,0:T(8,128)S(1)}, f32[370,256]{1,0:T(8,128)S(1)}, u32[]{:S(2)}, u32[]{:S(2)}) collective-permute-start(f32[370,256]{1,0:T(8,128)S(1)} %pad_maximum_fusion), channel_id=1, source_target_pairs={{0,1},{1,2},{2,3},{4,5},{5,6},{6,7},{8,9},{9,10},{10,11},{12,13},{... | collective-permute-start | bytes 1136648 | tf_op jit(solution)/shard_map/ppermute | solution.py:17
  21.7 5.3 %collective-permute-start.5 = (f32[370,256]{1,0:T(8,128)S(1)}, f32[370,256]{1,0:T(8,128)S(1)}, u32[]{:S(2)}, u32[]{:S(2)}) collective-permute-start(f32[370,256]{1,0:T(8,128)S(1)} %pad_maximum_fusion.1), channel_id=1, source_target_pairs={{1,0},{2,1},{3,2},{5,4},{6,5},{7,6},{9,8},{10,9},{11,10},{13,12},{... | collective-permute-start | bytes 1136648 | tf_op jit(solution)/shard_map/ppermute | solution.py:17
  36.6 0.7 %copy-start = (f32[3,8,16,256]{3,2,1,0:T(8,128)}, f32[3,8,16,256]{3,2,1,0:T(8,128)S(1)}, u32[]{:S(2)}) copy-start(f32[3,8,16,256]{3,2,1,0:T(8,128)S(1)} %get-tuple-element.7.refs_1_) | copy-start | bytes 1179652

commit v5 on v4

--- a/solution.py
+++ b/solution.py
@@ -21,10 +21,26 @@
     wide, thin = 2 * REACH, REACH
     rest = wide - rows
     own_pred, own_mask = packed[:rows], packed[rows:]
-    up = moved(jnp.concatenate([own_pred, own_mask[rows - thin :]], 0), "gx", lambda i: i + 1)
-    down = moved(jnp.concatenate([own_pred, own_mask[:thin]], 0), "gx", lambda i: i - 1)
-    far_up = moved(own_pred[rows - rest :], "gx", lambda i: i + 2)
-    far_down = moved(own_pred[:rest], "gx", lambda i: i - 2)
+    spot = lax.axis_index("gx")
+    odd, upper = lax.rem(spot, 2) == 1, lax.rem(spot, 4) >= 2
+    to_up = jnp.concatenate([own_pred, own_mask[rows - thin :]], 0)
+    to_down = jnp.concatenate([own_pred, own_mask[:thin]], 0)
+    to_far_up, to_far_down = own_pred[rows - rest :], own_pred[:rest]
+    a, b, c, d = lax.optimization_barrier(
+        (
+            jnp.where(odd, to_down, to_up),
+            jnp.where(odd, to_up, to_down),
+            jnp.where(upper, to_far_down, to_far_up),
+            jnp.where(upper, to_far_up, to_far_down),
+        )
+    )
+    a = moved(a, "gx", lambda i: i ^ 1)
+    b = moved(b, "gx", lambda i: i + 1 if i % 2 else i - 1)
+    c = moved(c, "gx", lambda i: i ^ 2)
+    d = moved(d, "gx", lambda i: i + 2 if i % 4 >= 2 else i - 2)
+    a, b, c, d = lax.optimization_barrier((a, b, c, d))
+    up, down = jnp.where(odd, a, b), jnp.where(odd, b, a)
+    far_up, far_down = jnp.where(upper, c, d), jnp.where(upper, d, c)
     tall_pred = jnp.concatenate([far_up, up[:rows], own_pred, down[:rows], far_down], 0)
     tall_mask = jnp.concatenate([up[rows:], own_mask, down[rows:]], 0)
     tall, short = tall_pred.shape[0], tall_mask.shape[0]
@@ -35,8 +51,14 @@
     def unside(b):
         return b[: tall * wide].reshape(tall, wide, -1), b[tall * wide :].reshape(short, thin, -1)
 
-    left_pred, left_mask = unside(moved(side(tall_pred[:, -wide:], tall_mask[:, -thin:]), "gy", lambda i: i + 1))
-    right_pred, right_mask = unside(moved(side(tall_pred[:, :wide], tall_mask[:, :thin]), "gy", lambda i: i - 1))
+    col_odd = lax.rem(lax.axis_index("gy"), 2) == 1
+    high = side(tall_pred[:, -wide:], tall_mask[:, -thin:])
+    low = side(tall_pred[:, :wide], tall_mask[:, :thin])
+    first = moved(jnp.where(col_odd, low, high), "gy", lambda i: i ^ 1)
+    second = moved(jnp.where(col_odd, high, low), "gy", lambda i: i + 1 if i % 2 else i - 1)
+    first, second = lax.optimization_barrier((first, second))
+    left_pred, left_mask = unside(jnp.where(col_odd, first, second))
+    right_pred, right_mask = unside(jnp.where(col_odd, second, first))
 
     def framed(parts):
         count = sum(p.shape[1] for p in parts)
@@ -79,16 +101,20 @@
 
 
 def over_tiles(count, step):
-    for i in range(tiles_for(count)):
+    def body(i, carry):
         step(i * SUBLANES)
+        return carry
+
+    lax.fori_loop(0, tiles_for(count), body, 0, unroll=True)
 
 
 def skeleton_kernel(rows, cols, place, own_pred, pred, label, results, sums, *scratch):
     t = softness_factor
     scratch = list(scratch)
-    stage, copied = scratch[48:]
-    by_label, by_one, mask_skel = (stage.at[i] for i in range(3))
+    stage, sent, copied = scratch[48:]
+    mask_skel = stage.at[2]
     copies = [pltpu.make_async_copy(stage.at[i], results.at[i], copied.at[i]) for i in range(3)]
+    copies.append(pltpu.make_async_copy(sent, sums, copied.at[3]))
     powers = scratch[:5]
     inverses = scratch[5:9]
     opened = scratch[9:13]
@@ -221,13 +247,32 @@
                     spreads[LEVELS + j][x, h, pl.ds(base, SUBLANES), :] = seed * spread
 
     def chain_tile(base):
-        for i in range((rows + 2 * REACH) // chunk):
+        def body(i, carry):
             chain_chunk(base, i * chunk)
+            return carry
+
+        lax.fori_loop(0, (rows + 2 * REACH) // chunk, body, 0, unroll=True)
 
     over_tiles(cols + 2 * REACH, chain_tile)
 
-    for level in range(LEVELS, 0, -1):
-        for which in range(2):
+    totals = [jnp.zeros((SUBLANES, LANES), jnp.float32) for _ in range(4)]
+    for base in range(0, cols, SUBLANES):
+        for x in range(rows):
+            for h in range(2):
+                half = slice(h * LANES, (h + 1) * LANES)
+                skel = skels[x + REACH, h, pl.ds(base + REACH, SUBLANES), :]
+                other = mask_skel[x, pl.ds(base, SUBLANES), half]
+                totals[0] += skel * labels[x + REACH, h, pl.ds(base + REACH, SUBLANES), :]
+                totals[1] += skel
+                totals[2] += other * own_pred[x, pl.ds(base, SUBLANES), half]
+                totals[3] += other
+    packed = jnp.concatenate([jnp.sum(v, 0, keepdims=True) for v in totals] * 2, 0)
+    for i in range(sums.shape[0] // SUBLANES):
+        sent[i * SUBLANES : (i + 1) * SUBLANES, :] = packed
+    copies[3].start()
+
+    for which in range(2):
+        for level in range(LEVELS, 0, -1):
 
             def pull(base, level=level, which=which):
                 index = column_index(base, level)
@@ -256,36 +301,19 @@
 
             over_tiles(cols + 2 * level, pull)
 
-    def finish(base, totals):
-        totals = list(totals)
-        pairs = [rows_box(parts[which * LEVELS], base, 0, 0, rows, first, last) for which in range(2)]
-        for x in range(rows):
-            grown = [next(p) for p in pairs]
-            for h in range(2):
-                half = slice(h * LANES, (h + 1) * LANES)
-                power = powers[0][x + WIDE, h, pl.ds(base + WIDE, SUBLANES), :]
-                own = weights[0][x + REACH, h, pl.ds(base + REACH, SUBLANES), :]
-                seed = labels[x + REACH, h, pl.ds(base + REACH, SUBLANES), :]
-                by_one[x, pl.ds(base, SUBLANES), half] = power * grown[0][h] + own
-                by_label[x, pl.ds(base, SUBLANES), half] = power * grown[1][h] + own * seed
-                skel = skels[x + REACH, h, pl.ds(base + REACH, SUBLANES), :]
-                other = mask_skel[x, pl.ds(base, SUBLANES), half]
-                predicted = own_pred[x, pl.ds(base, SUBLANES), half]
-                totals[0] += skel * seed
-                totals[1] += skel
-                totals[2] += other * predicted
-                totals[3] += other
-        return tuple(totals)
-
-    nothing = jnp.zeros((SUBLANES, LANES), jnp.float32)
-    totals = (nothing,) * 4
-    for i in range(tiles_for(cols)):
-        totals = finish(i * SUBLANES, totals)
-    copies[0].start()
-    copies[1].start()
-    packed = jnp.concatenate([jnp.sum(v, 0, keepdims=True) for v in totals] * 2, 0)
-    for i in range(sums.shape[0] // SUBLANES):
-        sums[i * SUBLANES : (i + 1) * SUBLANES, :] = packed
+        def finish(base, which=which):
+            grown_sums = rows_box(parts[which * LEVELS], base, 0, 0, rows, first, last)
+            for x, grown in enumerate(grown_sums):
+                for h in range(2):
+                    power = powers[0][x + WIDE, h, pl.ds(base + WIDE, SUBLANES), :]
+                    own = weights[0][x + REACH, h, pl.ds(base + REACH, SUBLANES), :]
+                    if which:
+                        own = own * labels[x + REACH, h, pl.ds(base + REACH, SUBLANES), :]
+                    stage[1 - which, x, pl.ds(base, SUBLANES), h * LANES : (h + 1) * LANES] = power * grown[h] + own
+
+        over_tiles(cols, finish)
+        copies[1 - which].start()
+
     for copy in copies:
         copy.wait()
 
@@ -340,7 +368,7 @@
         + [held(REACH - k) for k in range(LEVELS + 1)]
         + [held(REACH - k) for k in range(1, LEVELS + 1)]
         + [held(0)] * 4
-        + [pltpu.VMEM((3, rows, cols, depth), jnp.float32), pltpu.SemaphoreType.DMA((3,))]
+        + [pltpu.VMEM((3, rows, cols, depth), jnp.float32), pltpu.VMEM((gx * gy * 4, LANES), jnp.float32), pltpu.SemaphoreType.DMA((4,))]
     )
     block = jax.ShapeDtypeStruct((rows, cols, depth), jnp.float32)
     vmem = pl.BlockSpec(memory_space=pltpu.VMEM)
@@ -349,7 +377,7 @@
         lambda *refs: skeleton_kernel(rows, cols, *refs),
         out_shape=[jax.ShapeDtypeStruct((3, rows, cols, depth), jnp.float32), jax.ShapeDtypeStruct((gx * gy * 4, LANES), jnp.float32)],
         in_specs=[smem, vmem, vmem, vmem],
-        out_specs=[pl.BlockSpec(memory_space=pltpu.HBM), vmem],
+        out_specs=[pl.BlockSpec(memory_space=pltpu.HBM)] * 2,
         scratch_shapes=scratch,
         compiler_params=pltpu.CompilerParams(vmem_limit_bytes=VMEM_BYTES),
         name="skeleton",

time: 54.9 us -> 49.6 us (0.903)
  waiting for transfers between devices: 11.1 us -> 6.22 us
  starting transfers between devices: 13.5 us -> 10.9 us
  blocking collectives: 15.4 us -> 17.2 us
    ppermute x6, waiting for transfers between devices: 11.1 us -> 6.22 us  [moved(): return lax.ppermute(block, axis, pairs)]
    ppermute x6, starting transfers between devices: 13.5 us -> 10.9 us  [moved(): return lax.ppermute(block, axis, pairs)]
    all_to_all x1, blocking collectives: 15.4 us -> 17.2 us  [local(): got = lax.all_to_all(sums, ('gx', 'gy'), 0, 0, tiled=True)]
  transfers between devices with their start and end apart: 6 -> 6, of which waited for: 3 -> 2; matrix products, arithmetic and copies ran while one was open for 1% -> 0% of each run, Pallas kernels for 0% -> 0%
where the time goes in v5:
time: 49.6 us; the launch traced here: 49.4 us
  blocking collectives  17.2 us (35%)
  Pallas kernels  11.2 us (23%)
  starting transfers between devices  10.9 us (22%)
  waiting for transfers between devices  6.22 us (13%)
  other arithmetic  1.53 us (3%)
  local copies, waits for them, and re-layouts  1.27 us (3%)
  between operations  0.96 us (2%)
    all_to_all x1, blocking collectives, local(): got = lax.all_to_all(sums, ('gx', 'gy'), 0, 0, tiled=True)  17.2 us
    ppermute x6, starting transfers between devices, moved(): return lax.ppermute(block, axis, pairs)  10.9 us
    pallas_call x1, Pallas kernels, local(): pl.pallas_call(lambda *refs: skeleton_kernel(rows, cols, *refs), out_shap...  9.4 us
    ppermute x6, waiting for transfers between devices, moved(): return lax.ppermute(block, axis, pairs)  6.22 us
    pallas_call x1, Pallas kernels, local(): pl.pallas_call(lambda *refs: combine_kernel(float(gx * rows * gy * cols *...  1.84 us
  transfers between devices with their start and end apart: 6, of which 2 were waited for; matrix products, arithmetic and copies ran while one was open for 0% of the time, Pallas kernels for 0%

profile of v5, /device:TPU:0, one launch (start us, length us, event | category | flops | bytes accessed | tf_op | source)
XLA Modules:
  0.0 49.4 jit_solution(18319334585976511008)
XLA Ops:
  0.6 1.0 %convert_add_fusion = f32[16,16,256]{2,1,0:T(8,128)S(1)} fusion(s32[8,16,256]{2,1,0:T(8,128)} %param.3, f32[8,16,256]{2,1,0:T(8,128)} %param.2), kind=kLoop, calls=%fused_computation.12 | loop fusion | flops 131072 | bytes 524288 | tf_op jit(solution)/shard_map/add | solution.py:349
  1.7 3.0 %collective-permute-start = (f32[13,16,256]{2,1,0:T(8,128)S(1)}, f32[13,16,256]{2,1,0:T(8,128)S(1)}, u32[]{:S(2)}, u32[]{:S(2)}) collective-permute-start(f32[13,16,256]{2,1,0:T(8,128)S(1)} %get-tuple-element.16), channel_id=1, source_target_pairs={{0,4},{4,0},{8,12},{12,8},{16,20},{20,16},{24,28},{28,24},{1,5},{5... | collective-permute-start | bytes 638984 | tf_op jit(solution)/shard_map/ppermute | solution.py:17
  4.8 0.7 %collective-permute-start.1 = (f32[13,16,256]{2,1,0:T(8,128)S(1)}, f32[13,16,256]{2,1,0:T(8,128)S(1)}, u32[]{:S(2)}, u32[]{:S(2)}) collective-permute-start(f32[13,16,256]{2,1,0:T(8,128)S(1)} %get-tuple-element.17), channel_id=1, source_target_pairs={{4,8},{8,4},{12,16},{16,12},{20,24},{24,20},{5,9},{9,5},{13,17},{1... | collective-permute-start | bytes 638984 | tf_op jit(solution)/shard_map/ppermute | solution.py:17
  5.4 2.9 %collective-permute-start.2 = (f32[2,16,256]{2,1,0:T(8,128)S(1)}, f32[2,16,256]{2,1,0:T(8,128)S(1)}, u32[]{:S(2)}, u32[]{:S(2)}) collective-permute-start(f32[2,16,256]{2,1,0:T(8,128)S(1)} %get-tuple-element.18), channel_id=1, source_target_pairs={{0,8},{4,12},{8,0},{12,4},{16,24},{20,28},{24,16},{28,20},{1,9},{5... | collective-permute-start | bytes 98312 | tf_op jit(solution)/shard_map/ppermute | solution.py:17
  8.3 0.7 %collective-permute-start.3 = (f32[2,16,256]{2,1,0:T(8,128)S(1)}, f32[2,16,256]{2,1,0:T(8,128)S(1)}, u32[]{:S(2)}, u32[]{:S(2)}) collective-permute-start(f32[2,16,256]{2,1,0:T(8,128)S(1)} %get-tuple-element.19), channel_id=1, source_target_pairs={{8,16},{12,20},{16,8},{20,12},{9,17},{13,21},{17,9},{21,13},{10,18... | collective-permute-start | bytes 98312 | tf_op jit(solution)/shard_map/ppermute | solution.py:17
  9.0 5.0 %collective-permute-done.2 = f32[2,16,256]{2,1,0:T(8,128)S(1)} collective-permute-done((f32[2,16,256]{2,1,0:T(8,128)S(1)}, f32[2,16,256]{2,1,0:T(8,128)S(1)}, u32[]{:S(2)}, u32[]{:S(2)}) %collective-permute-start.2) | collective-permute-done | bytes 32800 | tf_op jit(solution)/shard_map/ppermute | solution.py:17
  13.9 0.0 collective-permute-done.3
  13.9 0.0 collective-permute-done
  13.9 0.0 collective-permute-done.1
  14.2 0.1 fusion.5
  14.5 0.1 broadcast_select_fusion.2
  14.6 0.7 %collective-permute-start.5 = (f32[370,256]{1,0:T(8,128)S(1)}, f32[370,256]{1,0:T(8,128)S(1)}, u32[]{:S(2)}, u32[]{:S(2)}) collective-permute-start(f32[370,256]{1,0:T(8,128)S(1)} %get-tuple-element.32), channel_id=1, source_target_pairs={{1,2},{2,1},{5,6},{6,5},{9,10},{10,9},{13,14},{14,13},{17,18},{18,... | collective-permute-start | bytes 1136648 | tf_op jit(solution)/shard_map/ppermute | solution.py:17
  15.3 3.0 %collective-permute-start.4 = (f32[370,256]{1,0:T(8,128)S(1)}, f32[370,256]{1,0:T(8,128)S(1)}, u32[]{:S(2)}, u32[]{:S(2)}) collective-permute-start(f32[370,256]{1,0:T(8,128)S(1)} %get-tuple-element.33), channel_id=1, source_target_pairs={{0,1},{1,0},{2,3},{3,2},{4,5},{5,4},{6,7},{7,6},{8,9},{9,8},{10,11... | collective-permute-start | bytes 1136648 | tf_op jit(solution)/shard_map/ppermute | solution.py:17
  18.3 0.1 pad_add_fusion.refs_0_
  18.3 0.0 collective-permute-done.5
  18.3 1.3 %collective-permute-done.4 = f32[370,256]{1,0:T(8,128)S(1)} collective-permute-done((f32[370,256]{1,0:T(8,128)S(1)}, f32[370,256]{1,0:T(8,128)S(1)}, u32[]{:S(2)}, u32[]{:S(2)}) %collective-permute-start.4) | collective-permute-done | bytes 378912 | tf_op jit(solution)/shard_map/ppermute | solution.py:17
  19.6 0.1 broadcast_select_fusion.1
  19.9 0.1 select_maximum_fusion.2.refs_3_
  20.0 0.1 select_maximum_fusion.refs_2_
  20.1 9.4 %skeleton.1 = (f32[3,8,16,256]{3,2,1,0:T(8,128)S(1)}, f32[128,128]{1,0:T(8,128)S(1)}) custom-call(s32[4]{0:T(128)S(1)} %pad_add_fusion.refs_0_, f32[8,16,256]{2,1,0:T(8,128)S(1)} %slice.75.refs_1_, f32[28,40,256]{2,1,0:T(8,128)S(1)} %select_maximum_fusion.refs_2_, f32[18,32,256]{2,1,0:T(8,128)S(1)} %select_maximum_fusion.2.refs_3_), custom_call_target="tpu_custom_call" | custom-call | tf_op jit(solution)/shard_map/skeleton/pallas_call | solution.py:376
  29.5 0.0 copy-start
  29.6 0.7 %copy-done = f32[3,8,16,256]{3,2,1,0:T(8,128)} copy-done((f32[3,8,16,256]{3,2,1,0:T(8,128)}, f32[3,8,16,256]{3,2,1,0:T(8,128)S(1)}, u32[]{:S(2)}) %copy-start) | copy-done | bytes 393240
  30.3 17.2 %all_to_all.11 = f32[32,4,128]{2,1,0:T(4,128)} all-to-all(f32[32,4,128]{2,1,0:T(4,128)S(1)} %bitcast.5), channel_id=1, replica_groups=mesh['gx'=8,'gy'=4] {'gx','gy'}, dimensions={0} | all-to-all | bytes 131072 | tf_op jit(solution)/shard_map/all_to_all | solution.py:385
  47.5 1.8 %combine.1 = (f32[8,16,256]{2,1,0:T(8,128)}, f32[1]{0:T(128)}) custom-call(f32[128,128]{1,0:T(8,128)} %bitcast.6, f32[3,8,16,256]{3,2,1,0:T(8,128)} %copy-done), custom_call_target="tpu_custom_call" | custom-call | tf_op jit(solution)/shard_map/combine/pallas_call | solution.py:386
  (30 shorter events, 0.6 us)
Async XLA Ops:
  1.7 12.2 %collective-permute-start = (f32[13,16,256]{2,1,0:T(8,128)S(1)}, f32[13,16,256]{2,1,0:T(8,128)S(1)}, u32[]{:S(2)}, u32[]{:S(2)}) collective-permute-start(f32[13,16,256]{2,1,0:T(8,128)S(1)} %get-tuple-element.16), channel_id=1, source_target_pairs={{0,4},{4,0},{8,12},{12,8},{16,20},{20,16},{24,28},{28,24},{1,5},{5... | collective-permute-start | bytes 638984 | tf_op jit(solution)/shard_map/ppermute | solution.py:17
  4.8 9.2 %collective-permute-start.1 = (f32[13,16,256]{2,1,0:T(8,128)S(1)}, f32[13,16,256]{2,1,0:T(8,128)S(1)}, u32[]{:S(2)}, u32[]{:S(2)}) collective-permute-start(f32[13,16,256]{2,1,0:T(8,128)S(1)} %get-tuple-element.17), channel_id=1, source_target_pairs={{4,8},{8,4},{12,16},{16,12},{20,24},{24,20},{5,9},{9,5},{13,17},{1... | collective-permute-start | bytes 638984 | tf_op jit(solution)/shard_map/ppermute | solution.py:17
  5.4 8.5 %collective-permute-start.2 = (f32[2,16,256]{2,1,0:T(8,128)S(1)}, f32[2,16,256]{2,1,0:T(8,128)S(1)}, u32[]{:S(2)}, u32[]{:S(2)}) collective-permute-start(f32[2,16,256]{2,1,0:T(8,128)S(1)} %get-tuple-element.18), channel_id=1, source_target_pairs={{0,8},{4,12},{8,0},{12,4},{16,24},{20,28},{24,16},{28,20},{1,9},{5... | collective-permute-start | bytes 98312 | tf_op jit(solution)/shard_map/ppermute | solution.py:17
  8.3 5.6 %collective-permute-start.3 = (f32[2,16,256]{2,1,0:T(8,128)S(1)}, f32[2,16,256]{2,1,0:T(8,128)S(1)}, u32[]{:S(2)}, u32[]{:S(2)}) collective-permute-start(f32[2,16,256]{2,1,0:T(8,128)S(1)} %get-tuple-element.19), channel_id=1, source_target_pairs={{8,16},{12,20},{16,8},{20,12},{9,17},{13,21},{17,9},{21,13},{10,18... | collective-permute-start | bytes 98312 | tf_op jit(solution)/shard_map/ppermute | solution.py:17
  14.6 3.8 %collective-permute-start.5 = (f32[370,256]{1,0:T(8,128)S(1)}, f32[370,256]{1,0:T(8,128)S(1)}, u32[]{:S(2)}, u32[]{:S(2)}) collective-permute-start(f32[370,256]{1,0:T(8,128)S(1)} %get-tuple-element.32), channel_id=1, source_target_pairs={{1,2},{2,1},{5,6},{6,5},{9,10},{10,9},{13,14},{14,13},{17,18},{18,... | collective-permute-start | bytes 1136648 | tf_op jit(solution)/shard_map/ppermute | solution.py:17
  15.3 4.3 %collective-permute-start.4 = (f32[370,256]{1,0:T(8,128)S(1)}, f32[370,256]{1,0:T(8,128)S(1)}, u32[]{:S(2)}, u32[]{:S(2)}) collective-permute-start(f32[370,256]{1,0:T(8,128)S(1)} %get-tuple-element.33), channel_id=1, source_target_pairs={{0,1},{1,0},{2,3},{3,2},{4,5},{5,4},{6,7},{7,6},{8,9},{9,8},{10,11... | collective-permute-start | bytes 1136648 | tf_op jit(solution)/shard_map/ppermute | solution.py:17
  29.5 0.8 %copy-start = (f32[3,8,16,256]{3,2,1,0:T(8,128)}, f32[3,8,16,256]{3,2,1,0:T(8,128)S(1)}, u32[]{:S(2)}) copy-start(f32[3,8,16,256]{3,2,1,0:T(8,128)S(1)} %get-tuple-element.27.refs_1_) | copy-start | bytes 1179652

commit v6 on v5

--- a/solution.py
+++ b/solution.py
@@ -71,6 +71,7 @@
 LANES = 128
 SUBLANES = 8
 VMEM_BYTES = 40 * 1024 * 1024
+KEPT = 210
 
 
 def tiles_for(count):
@@ -113,8 +114,12 @@
     scratch = list(scratch)
     stage, sent, copied = scratch[48:]
     mask_skel = stage.at[2]
-    copies = [pltpu.make_async_copy(stage.at[i], results.at[i], copied.at[i]) for i in range(3)]
-    copies.append(pltpu.make_async_copy(sent, sums, copied.at[3]))
+    tiles = [pl.ds(base, SUBLANES) for base in range(0, cols, SUBLANES)]
+    copies = [
+        [pltpu.make_async_copy(stage.at[i, :, t], results.at[i, :, t], copied.at[i, n]) for n, t in enumerate(tiles)]
+        for i in range(3)
+    ]
+    copies.append([pltpu.make_async_copy(sent, sums, copied.at[3, 0])])
     powers = scratch[:5]
     inverses = scratch[5:9]
     opened = scratch[9:13]
@@ -206,7 +211,8 @@
                 mask_skel[x, pl.ds(base, SUBLANES), h * LANES : (h + 1) * LANES] = t * skel
 
     over_tiles(cols, label_chain)
-    copies[2].start()
+    for copy in copies[2]:
+        copy.start()
 
     def spread_label(base):
         for x in range(rows + 2 * REACH):
@@ -266,10 +272,11 @@
                 totals[1] += skel
                 totals[2] += other * own_pred[x, pl.ds(base, SUBLANES), half]
                 totals[3] += other
-    packed = jnp.concatenate([jnp.sum(v, 0, keepdims=True) for v in totals] * 2, 0)
+    totals = [jnp.sum(jnp.sum(v, 0, keepdims=True), 1, keepdims=True) for v in totals]
+    packed = jnp.broadcast_to(jnp.concatenate(totals * 2, 0), (SUBLANES, LANES))
     for i in range(sums.shape[0] // SUBLANES):
         sent[i * SUBLANES : (i + 1) * SUBLANES, :] = packed
-    copies[3].start()
+    copies[3][0].start()
 
     for which in range(2):
         for level in range(LEVELS, 0, -1):
@@ -311,10 +318,11 @@
                         own = own * labels[x + REACH, h, pl.ds(base + REACH, SUBLANES), :]
                     stage[1 - which, x, pl.ds(base, SUBLANES), h * LANES : (h + 1) * LANES] = power * grown[h] + own
 
-        over_tiles(cols, finish)
-        copies[1 - which].start()
-
-    for copy in copies:
+        for tile in range(tiles_for(cols)):
+            finish(tile * SUBLANES)
+            copies[1 - which][tile].start()
+
+    for copy in sum(copies, []):
         copy.wait()
 
 
@@ -323,12 +331,11 @@
     for i in range(got.shape[0] // SUBLANES):
         total += got[i * SUBLANES : (i + 1) * SUBLANES, :]
     total = total + pltpu.roll(total, 4, 0)
-    total = jnp.broadcast_to(jnp.sum(total, 1, keepdims=True), (SUBLANES, LANES))
     intersection_pred, mass_pred, intersection_mask, mass_mask = (total[i : i + 1] + 1.0 for i in range(4))
     precision = intersection_pred / mass_pred
     sensitivity = intersection_mask / mass_mask
     paired = precision + sensitivity
-    loss[0] = jnp.max(1.0 - 2.0 * precision * sensitivity / paired)
+    loss[0] = (1.0 - 2.0 * precision * sensitivity / paired)[0, 0]
     slope_prec = -2.0 * sensitivity * sensitivity / (paired * paired)
     slope_sens = -2.0 * precision * precision / (paired * paired)
     coef_intersection = cells * slope_prec / mass_pred
@@ -368,14 +375,14 @@
         + [held(REACH - k) for k in range(LEVELS + 1)]
         + [held(REACH - k) for k in range(1, LEVELS + 1)]
         + [held(0)] * 4
-        + [pltpu.VMEM((3, rows, cols, depth), jnp.float32), pltpu.VMEM((gx * gy * 4, LANES), jnp.float32), pltpu.SemaphoreType.DMA((4,))]
+        + [pltpu.VMEM((3, rows, cols, depth), jnp.float32), pltpu.VMEM((gx * gy * 4, LANES), jnp.float32), pltpu.SemaphoreType.DMA((4, tiles_for(cols)))]
     )
     block = jax.ShapeDtypeStruct((rows, cols, depth), jnp.float32)
     vmem = pl.BlockSpec(memory_space=pltpu.VMEM)
     smem = pl.BlockSpec(memory_space=pltpu.SMEM)
     results, sums = pl.pallas_call(
         lambda *refs: skeleton_kernel(rows, cols, *refs),
-        out_shape=[jax.ShapeDtypeStruct((3, rows, cols, depth), jnp.float32), jax.ShapeDtypeStruct((gx * gy * 4, LANES), jnp.float32)],
+        out_shape=[jax.ShapeDtypeStruct((KEPT, rows, cols, depth), jnp.float32), jax.ShapeDtypeStruct((gx * gy * 4, LANES), jnp.float32)],
         in_specs=[smem, vmem, vmem, vmem],
         out_specs=[pl.BlockSpec(memory_space=pltpu.HBM)] * 2,
         scratch_shapes=scratch,
@@ -386,8 +393,12 @@
     gradient, loss = pl.pallas_call(
         lambda *refs: combine_kernel(float(gx * rows * gy * cols * depth), *refs),
         out_shape=[block, jax.ShapeDtypeStruct((1,), jnp.float32)],
-        in_specs=[vmem] * 2,
-        out_specs=[vmem, smem],
+        grid=(1,),
+        in_specs=[
+            pl.BlockSpec(got.shape, lambda i: (0, 0)),
+            pl.BlockSpec((3, rows, cols, depth), lambda i: (0, 0, 0, 0)),
+        ],
+        out_specs=[pl.BlockSpec(block.shape, lambda i: (0, 0, 0)), smem],
         name="combine",
     )(got, results)
     return (gradient, loss[0])

time: 49.6 us -> 48.8 us (0.984)
  local copies, waits for them, and re-layouts: 1.27 us -> 0.53 us
    unnamed x6 -> x4, local copies, waits for them, and re-layouts: 0.81 us -> 0.06 us
where the time goes in v6:
time: 48.8 us; the launch traced here: 48.6 us
  blocking collectives  17.3 us (35%)
  Pallas kernels  11.2 us (23%)
  starting transfers between devices  10.9 us (22%)
  waiting for transfers between devices  6.22 us (13%)
  other arithmetic  1.53 us (3%)
  between operations  0.95 us (2%)
  local copies, waits for them, and re-layouts  0.53 us (1%)
    all_to_all x1, blocking collectives, local(): got = lax.all_to_all(sums, ('gx', 'gy'), 0, 0, tiled=True)  17.3 us
    ppermute x6, starting transfers between devices, moved(): return lax.ppermute(block, axis, pairs)  10.9 us
    pallas_call x1, Pallas kernels, local(): pl.pallas_call(lambda *refs: skeleton_kernel(rows, cols, *refs), out_shap...  9.42 us
    ppermute x6, waiting for transfers between devices, moved(): return lax.ppermute(block, axis, pairs)  6.22 us
    pallas_call x1, Pallas kernels, local(): pl.pallas_call(lambda *refs: combine_kernel(float(gx * rows * gy * cols *...  1.77 us
    add x1, other arithmetic, local(): jnp.pad(prediction, ((0, rows), none, none))  0.99 us
  transfers between devices with their start and end apart: 6, of which 2 were waited for; matrix products, arithmetic and copies ran while one was open for 0% of the time, Pallas kernels for 0%

profile of v6, /device:TPU:0, one launch (start us, length us, event | category | flops | bytes accessed | tf_op | source)
XLA Modules:
  0.0 48.6 jit_solution(5912272917291617002)
XLA Ops:
  0.6 1.0 %convert_add_fusion = f32[16,16,256]{2,1,0:T(8,128)S(1)} fusion(s32[8,16,256]{2,1,0:T(8,128)} %param.3, f32[8,16,256]{2,1,0:T(8,128)} %param.2), kind=kLoop, calls=%fused_computation.12 | loop fusion | flops 131072 | bytes 524288 | tf_op jit(solution)/shard_map/add | solution.py:356
  1.7 3.0 %collective-permute-start = (f32[13,16,256]{2,1,0:T(8,128)S(1)}, f32[13,16,256]{2,1,0:T(8,128)S(1)}, u32[]{:S(2)}, u32[]{:S(2)}) collective-permute-start(f32[13,16,256]{2,1,0:T(8,128)S(1)} %get-tuple-element.16), channel_id=1, source_target_pairs={{0,4},{4,0},{8,12},{12,8},{16,20},{20,16},{24,28},{28,24},{1,5},{5... | collective-permute-start | bytes 638984 | tf_op jit(solution)/shard_map/ppermute | solution.py:17
  4.8 0.7 %collective-permute-start.1 = (f32[13,16,256]{2,1,0:T(8,128)S(1)}, f32[13,16,256]{2,1,0:T(8,128)S(1)}, u32[]{:S(2)}, u32[]{:S(2)}) collective-permute-start(f32[13,16,256]{2,1,0:T(8,128)S(1)} %get-tuple-element.17), channel_id=1, source_target_pairs={{4,8},{8,4},{12,16},{16,12},{20,24},{24,20},{5,9},{9,5},{13,17},{1... | collective-permute-start | bytes 638984 | tf_op jit(solution)/shard_map/ppermute | solution.py:17
  5.4 2.9 %collective-permute-start.2 = (f32[2,16,256]{2,1,0:T(8,128)S(1)}, f32[2,16,256]{2,1,0:T(8,128)S(1)}, u32[]{:S(2)}, u32[]{:S(2)}) collective-permute-start(f32[2,16,256]{2,1,0:T(8,128)S(1)} %get-tuple-element.18), channel_id=1, source_target_pairs={{0,8},{4,12},{8,0},{12,4},{16,24},{20,28},{24,16},{28,20},{1,9},{5... | collective-permute-start | bytes 98312 | tf_op jit(solution)/shard_map/ppermute | solution.py:17
  8.3 0.7 %collective-permute-start.3 = (f32[2,16,256]{2,1,0:T(8,128)S(1)}, f32[2,16,256]{2,1,0:T(8,128)S(1)}, u32[]{:S(2)}, u32[]{:S(2)}) collective-permute-start(f32[2,16,256]{2,1,0:T(8,128)S(1)} %get-tuple-element.19), channel_id=1, source_target_pairs={{8,16},{12,20},{16,8},{20,12},{9,17},{13,21},{17,9},{21,13},{10,18... | collective-permute-start | bytes 98312 | tf_op jit(solution)/shard_map/ppermute | solution.py:17
  9.0 5.0 %collective-permute-done.2 = f32[2,16,256]{2,1,0:T(8,128)S(1)} collective-permute-done((f32[2,16,256]{2,1,0:T(8,128)S(1)}, f32[2,16,256]{2,1,0:T(8,128)S(1)}, u32[]{:S(2)}, u32[]{:S(2)}) %collective-permute-start.2) | collective-permute-done | bytes 32800 | tf_op jit(solution)/shard_map/ppermute | solution.py:17
  13.9 0.0 collective-permute-done.3
  13.9 0.0 collective-permute-done
  13.9 0.0 collective-permute-done.1
  14.2 0.1 fusion.5
  14.5 0.1 broadcast_select_fusion.2
  14.6 0.7 %collective-permute-start.5 = (f32[370,256]{1,0:T(8,128)S(1)}, f32[370,256]{1,0:T(8,128)S(1)}, u32[]{:S(2)}, u32[]{:S(2)}) collective-permute-start(f32[370,256]{1,0:T(8,128)S(1)} %get-tuple-element.32), channel_id=1, source_target_pairs={{1,2},{2,1},{5,6},{6,5},{9,10},{10,9},{13,14},{14,13},{17,18},{18,... | collective-permute-start | bytes 1136648 | tf_op jit(solution)/shard_map/ppermute | solution.py:17
  15.3 3.0 %collective-permute-start.4 = (f32[370,256]{1,0:T(8,128)S(1)}, f32[370,256]{1,0:T(8,128)S(1)}, u32[]{:S(2)}, u32[]{:S(2)}) collective-permute-start(f32[370,256]{1,0:T(8,128)S(1)} %get-tuple-element.33), channel_id=1, source_target_pairs={{0,1},{1,0},{2,3},{3,2},{4,5},{5,4},{6,7},{7,6},{8,9},{9,8},{10,11... | collective-permute-start | bytes 1136648 | tf_op jit(solution)/shard_map/ppermute | solution.py:17
  18.3 0.1 pad_add_fusion.refs_0_
  18.3 0.0 collective-permute-done.5
  18.3 1.3 %collective-permute-done.4 = f32[370,256]{1,0:T(8,128)S(1)} collective-permute-done((f32[370,256]{1,0:T(8,128)S(1)}, f32[370,256]{1,0:T(8,128)S(1)}, u32[]{:S(2)}, u32[]{:S(2)}) %collective-permute-start.4) | collective-permute-done | bytes 378912 | tf_op jit(solution)/shard_map/ppermute | solution.py:17
  19.6 0.1 broadcast_select_fusion.1
  19.9 0.1 select_maximum_fusion.2.refs_3_
  20.0 0.1 select_maximum_fusion.refs_2_
  20.1 9.4 %skeleton.1 = (f32[210,8,16,256]{3,2,1,0:T(8,128)}, f32[128,128]{1,0:T(8,128)S(1)}) custom-call(s32[4]{0:T(128)S(1)} %pad_add_fusion.refs_0_, f32[8,16,256]{2,1,0:T(8,128)S(1)} %slice.75.refs_1_, f32[28,40,256]{2,1,0:T(8,128)S(1)} %select_maximum_fusion.refs_2_, f32[18,32,256]{2,1,0:T(8,128)S(1)} %select_maximum_fusion.2.refs_3_), custom_call_target="tpu_custom_call" | custom-call | tf_op jit(solution)/shard_map/skeleton/pallas_call | solution.py:383
  29.6 17.3 %all_to_all.11 = f32[32,4,128]{2,1,0:T(4,128)} all-to-all(f32[32,4,128]{2,1,0:T(4,128)S(1)} %bitcast.5), channel_id=1, replica_groups=mesh['gx'=8,'gy'=4] {'gx','gy'}, dimensions={0} | all-to-all | bytes 131072 | tf_op jit(solution)/shard_map/all_to_all | solution.py:392
  46.8 1.8 %combine.1 = (f32[8,16,256]{2,1,0:T(8,128)}, f32[1]{0:T(128)}) custom-call(f32[128,128]{1,0:T(8,128)} %bitcast.6, f32[210,8,16,256]{3,2,1,0:T(8,128)} %get-tuple-element.27.refs_1_), custom_call_target="tpu_custom_call" | custom-call | tf_op jit(solution)/shard_map/combine/pallas_call | solution.py:393
  (30 shorter events, 0.6 us)
Async XLA Ops:
  1.7 12.2 %collective-permute-start = (f32[13,16,256]{2,1,0:T(8,128)S(1)}, f32[13,16,256]{2,1,0:T(8,128)S(1)}, u32[]{:S(2)}, u32[]{:S(2)}) collective-permute-start(f32[13,16,256]{2,1,0:T(8,128)S(1)} %get-tuple-element.16), channel_id=1, source_target_pairs={{0,4},{4,0},{8,12},{12,8},{16,20},{20,16},{24,28},{28,24},{1,5},{5... | collective-permute-start | bytes 638984 | tf_op jit(solution)/shard_map/ppermute | solution.py:17
  4.8 9.2 %collective-permute-start.1 = (f32[13,16,256]{2,1,0:T(8,128)S(1)}, f32[13,16,256]{2,1,0:T(8,128)S(1)}, u32[]{:S(2)}, u32[]{:S(2)}) collective-permute-start(f32[13,16,256]{2,1,0:T(8,128)S(1)} %get-tuple-element.17), channel_id=1, source_target_pairs={{4,8},{8,4},{12,16},{16,12},{20,24},{24,20},{5,9},{9,5},{13,17},{1... | collective-permute-start | bytes 638984 | tf_op jit(solution)/shard_map/ppermute | solution.py:17
  5.4 8.5 %collective-permute-start.2 = (f32[2,16,256]{2,1,0:T(8,128)S(1)}, f32[2,16,256]{2,1,0:T(8,128)S(1)}, u32[]{:S(2)}, u32[]{:S(2)}) collective-permute-start(f32[2,16,256]{2,1,0:T(8,128)S(1)} %get-tuple-element.18), channel_id=1, source_target_pairs={{0,8},{4,12},{8,0},{12,4},{16,24},{20,28},{24,16},{28,20},{1,9},{5... | collective-permute-start | bytes 98312 | tf_op jit(solution)/shard_map/ppermute | solution.py:17
  8.3 5.6 %collective-permute-start.3 = (f32[2,16,256]{2,1,0:T(8,128)S(1)}, f32[2,16,256]{2,1,0:T(8,128)S(1)}, u32[]{:S(2)}, u32[]{:S(2)}) collective-permute-start(f32[2,16,256]{2,1,0:T(8,128)S(1)} %get-tuple-element.19), channel_id=1, source_target_pairs={{8,16},{12,20},{16,8},{20,12},{9,17},{13,21},{17,9},{21,13},{10,18... | collective-permute-start | bytes 98312 | tf_op jit(solution)/shard_map/ppermute | solution.py:17
  14.6 3.8 %collective-permute-start.5 = (f32[370,256]{1,0:T(8,128)S(1)}, f32[370,256]{1,0:T(8,128)S(1)}, u32[]{:S(2)}, u32[]{:S(2)}) collective-permute-start(f32[370,256]{1,0:T(8,128)S(1)} %get-tuple-element.32), channel_id=1, source_target_pairs={{1,2},{2,1},{5,6},{6,5},{9,10},{10,9},{13,14},{14,13},{17,18},{18,... | collective-permute-start | bytes 1136648 | tf_op jit(solution)/shard_map/ppermute | solution.py:17
  15.3 4.3 %collective-permute-start.4 = (f32[370,256]{1,0:T(8,128)S(1)}, f32[370,256]{1,0:T(8,128)S(1)}, u32[]{:S(2)}, u32[]{:S(2)}) collective-permute-start(f32[370,256]{1,0:T(8,128)S(1)} %get-tuple-element.33), channel_id=1, source_target_pairs={{0,1},{1,0},{2,3},{3,2},{4,5},{5,4},{6,7},{7,6},{8,9},{9,8},{10,11... | collective-permute-start | bytes 1136648 | tf_op jit(solution)/shard_map/ppermute | solution.py:17

commit v7 on v6

--- a/solution.py
+++ b/solution.py
@@ -92,13 +92,13 @@
         parts = [ref[x + row_shift, h, pl.ds(base + (col_shift + d), SUBLANES), :] for d in range(3)]
         return parts[0] + parts[1] + parts[2]
 
-    older = [across(0, h) for h in range(2)]
-    newer = [across(1, h) for h in range(2)]
-    for x in range(count):
-        newest = [across(x + 2, h) for h in range(2)]
-        low, high = (older[h] + newer[h] + newest[h] for h in range(2))
-        older, newer = newer, newest
-        yield depth_sum(low, high, first, last)
+    rows = [[across(x, h) for h in range(2)] for x in range(2)]
+    for x in range(0, count, 2):
+        rows += [[across(x + d, h) for h in range(2)] for d in (2, 3)]
+        shared = [rows[1][h] + rows[2][h] for h in range(2)]
+        yield depth_sum(*(rows[0][h] + shared[h] for h in range(2)), first, last)
+        yield depth_sum(*(shared[h] + rows[3][h] for h in range(2)), first, last)
+        rows = rows[2:]
 
 
 def over_tiles(count, step):
@@ -109,17 +109,16 @@
     lax.fori_loop(0, tiles_for(count), body, 0, unroll=True)
 
 
-def skeleton_kernel(rows, cols, place, own_pred, pred, label, results, sums, *scratch):
+def skeleton_kernel(rows, cols, own_pred, pred, label, results, sums, *scratch):
     t = softness_factor
     scratch = list(scratch)
-    stage, sent, copied = scratch[48:]
+    stage, copied = scratch[48:]
     mask_skel = stage.at[2]
     tiles = [pl.ds(base, SUBLANES) for base in range(0, cols, SUBLANES)]
     copies = [
         [pltpu.make_async_copy(stage.at[i, :, t], results.at[i, :, t], copied.at[i, n]) for n, t in enumerate(tiles)]
         for i in range(3)
     ]
-    copies.append([pltpu.make_async_copy(sent, sums, copied.at[3, 0])])
     powers = scratch[:5]
     inverses = scratch[5:9]
     opened = scratch[9:13]
@@ -130,7 +129,8 @@
     label_powers = scratch[35:40]
     label_inverses = scratch[40:44]
     label_opened = scratch[44:48]
-    row0, col0, row_count, col_count = (place[i] for i in range(4))
+    row0, row_count = lax.axis_index("gx") * rows, lax.axis_size("gx") * rows
+    col0, col_count = lax.axis_index("gy") * cols, lax.axis_size("gy") * cols
     lane = lax.broadcasted_iota(jnp.int32, (SUBLANES, LANES), 1)
     sublane = lax.broadcasted_iota(jnp.int32, (SUBLANES, LANES), 0)
     first, last = lane == 0, lane == LANES - 1
@@ -143,13 +143,15 @@
         row = row0 + (x - width)
         return jnp.where((row >= 0) & (row < row_count), col_count, 0)
 
-    def raise_field(field, powers, inverses, width):
+    def raise_field(field, powers, inverses, width, kept=None):
         def start(base):
             index = column_index(base, width)
             for x in range(rows + 2 * width):
                 ok = index < column_limit(x, width)
                 for h in range(2):
                     value = field[x, pl.ds(base, SUBLANES), h * LANES : (h + 1) * LANES]
+                    if kept is not None:
+                        kept[x, h, pl.ds(base, SUBLANES), :] = value
                     powers[0][x, h, pl.ds(base, SUBLANES), :] = jnp.where(ok, jnp.exp(value * (-1.0 / t)), 0.0)
 
         over_tiles(cols + 2 * width, start)
@@ -162,7 +164,8 @@
                 for x, pair in enumerate(sums_of):
                     ok = index < column_limit(x, here)
                     for h in range(2):
-                        powers[level][x, h, pl.ds(base, SUBLANES), :] = jnp.where(ok, pair[h], 0.0)
+                        if level < LEVELS:
+                            powers[level][x, h, pl.ds(base, SUBLANES), :] = jnp.where(ok, pair[h], 0.0)
                         inverses[level - 1][x, h, pl.ds(base, SUBLANES), :] = jnp.where(ok, 1.0 / pair[h], 0.0)
 
             over_tiles(cols + 2 * here, erode)
@@ -198,7 +201,7 @@
                 skel = skel + jnp.log(grown)
         return skel, saved
 
-    raise_field(label, label_powers, label_inverses, REACH)
+    raise_field(label, label_powers, label_inverses, REACH, labels)
     open_field(label_inverses, label_opened, REACH, 0)
 
     def label_chain(base):
@@ -214,32 +217,24 @@
     for copy in copies[2]:
         copy.start()
 
-    def spread_label(base):
-        for x in range(rows + 2 * REACH):
-            for h in range(2):
-                labels[x, h, pl.ds(base, SUBLANES), :] = label[x, pl.ds(base, SUBLANES), h * LANES : (h + 1) * LANES]
-
-    over_tiles(cols + 2 * REACH, spread_label)
-
     raise_field(pred, powers, inverses, WIDE)
     open_field(inverses, opened, WIDE, REACH)
 
-    chunk = 3
-
-    def chain_chunk(base, x0):
+    def chain_tile(base):
         index = column_index(base, REACH)
-        for dx in range(chunk):
-            x = x0 + dx
+        for x in range(rows + 2 * REACH):
+            away = max(REACH - x, x - REACH - rows + 1)
             ok = index < column_limit(x, REACH)
             for h in range(2):
                 skel, saved = chain(
                     lambda j: powers[j][x + REACH - j, h, pl.ds(base + (REACH - j), SUBLANES), :],
                     lambda j: opened[j][x, h, pl.ds(base, SUBLANES), :],
                 )
-                skels[x, h, pl.ds(base, SUBLANES), :] = t * skel
+                if away <= 0:
+                    skels[x, h, pl.ds(base, SUBLANES), :] = t * skel
                 seed = labels[x, h, pl.ds(base, SUBLANES), :]
                 rest = jnp.where(ok, 1.0, 0.0)
-                for j in range(ITERS, -1, -1):
+                for j in range(ITERS, max(0, away - 2) - 1, -1):
                     slope, over, delta, left, rect = saved[j]
                     if j:
                         inner = rest * rect
@@ -247,19 +242,56 @@
                         rest = rest - inner * (t * delta)
                     else:
                         scaled = rest
-                    weights[j][x, h, pl.ds(base, SUBLANES), :] = jnp.where(ok, scaled * slope, 0.0)
+                    if away <= j:
+                        weights[j][x, h, pl.ds(base, SUBLANES), :] = jnp.where(ok, scaled * slope, 0.0)
                     spread = jnp.where(ok, scaled * over, 0.0)
                     spreads[j][x, h, pl.ds(base, SUBLANES), :] = spread
                     spreads[LEVELS + j][x, h, pl.ds(base, SUBLANES), :] = seed * spread
 
-    def chain_tile(base):
-        def body(i, carry):
-            chain_chunk(base, i * chunk)
-            return carry
-
-        lax.fori_loop(0, (rows + 2 * REACH) // chunk, body, 0, unroll=True)
-
     over_tiles(cols + 2 * REACH, chain_tile)
+
+    for which in range(2):
+        for level in range(LEVELS, 0, -1):
+
+            def pull(base, level=level, which=which):
+                index = column_index(base, level)
+                count = rows + 2 * level
+                shift = REACH - level - 1
+                spread_sums = rows_box(spreads[which * LEVELS + level - 1], base, shift, shift, count, first, last)
+                if level < LEVELS:
+                    grown_sums = rows_box(parts[which * LEVELS + level], base, 0, 0, count, first, last)
+                for x in range(count):
+                    ok = index < column_limit(x, level)
+                    spread = next(spread_sums)
+                    grown = next(grown_sums) if level < LEVELS else None
+                    for h in range(2):
+                        off = WIDE - 2 * level
+                        inv = inverses[level - 1][x + off, h, pl.ds(base + off, SUBLANES), :]
+                        if level < LEVELS:
+                            at = REACH - level
+                            own = weights[level][x + at, h, pl.ds(base + at, SUBLANES), :]
+                            if which:
+                                own = own * labels[x + at, h, pl.ds(base + at, SUBLANES), :]
+                            part = (own - inv * spread[h]) * inv + grown[h]
+                        else:
+                            part = inv * inv * -spread[h]
+                        parts[which * LEVELS + level - 1][x, h, pl.ds(base, SUBLANES), :] = jnp.where(ok, part, 0.0)
+
+            over_tiles(cols + 2 * level, pull)
+
+        def finish(base, which=which):
+            grown_sums = rows_box(parts[which * LEVELS], base, 0, 0, rows, first, last)
+            for x, grown in enumerate(grown_sums):
+                for h in range(2):
+                    power = powers[0][x + WIDE, h, pl.ds(base + WIDE, SUBLANES), :]
+                    own = weights[0][x + REACH, h, pl.ds(base + REACH, SUBLANES), :]
+                    if which:
+                        own = own * labels[x + REACH, h, pl.ds(base + REACH, SUBLANES), :]
+                    stage[1 - which, x, pl.ds(base, SUBLANES), h * LANES : (h + 1) * LANES] = power * grown[h] + own
+
+        for tile in range(tiles_for(cols)):
+            finish(tile * SUBLANES)
+            copies[1 - which][tile].start()
 
     totals = [jnp.zeros((SUBLANES, LANES), jnp.float32) for _ in range(4)]
     for base in range(0, cols, SUBLANES):
@@ -275,53 +307,7 @@
     totals = [jnp.sum(jnp.sum(v, 0, keepdims=True), 1, keepdims=True) for v in totals]
     packed = jnp.broadcast_to(jnp.concatenate(totals * 2, 0), (SUBLANES, LANES))
     for i in range(sums.shape[0] // SUBLANES):
-        sent[i * SUBLANES : (i + 1) * SUBLANES, :] = packed
-    copies[3][0].start()
-
-    for which in range(2):
-        for level in range(LEVELS, 0, -1):
-
-            def pull(base, level=level, which=which):
-                index = column_index(base, level)
-                count = rows + 2 * level
-                shift = REACH - level - 1
-                spread_sums = rows_box(spreads[which * LEVELS + level - 1], base, shift, shift, count, first, last)
-                if level < LEVELS:
-                    grown_sums = rows_box(parts[which * LEVELS + level], base, 0, 0, count, first, last)
-                for x in range(count):
-                    ok = index < column_limit(x, level)
-                    spread = next(spread_sums)
-                    grown = next(grown_sums) if level < LEVELS else None
-                    for h in range(2):
-                        off = WIDE - 2 * level
-                        inv = inverses[level - 1][x + off, h, pl.ds(base + off, SUBLANES), :]
-                        part = -(inv * spread[h])
-                        if level < LEVELS:
-                            at = REACH - level
-                            own = weights[level][x + at, h, pl.ds(base + at, SUBLANES), :]
-                            if which:
-                                own = own * labels[x + at, h, pl.ds(base + at, SUBLANES), :]
-                            part = (part + own) * inv + grown[h]
-                        else:
-                            part = part * inv
-                        parts[which * LEVELS + level - 1][x, h, pl.ds(base, SUBLANES), :] = jnp.where(ok, part, 0.0)
-
-            over_tiles(cols + 2 * level, pull)
-
-        def finish(base, which=which):
-            grown_sums = rows_box(parts[which * LEVELS], base, 0, 0, rows, first, last)
-            for x, grown in enumerate(grown_sums):
-                for h in range(2):
-                    power = powers[0][x + WIDE, h, pl.ds(base + WIDE, SUBLANES), :]
-                    own = weights[0][x + REACH, h, pl.ds(base + REACH, SUBLANES), :]
-                    if which:
-                        own = own * labels[x + REACH, h, pl.ds(base + REACH, SUBLANES), :]
-                    stage[1 - which, x, pl.ds(base, SUBLANES), h * LANES : (h + 1) * LANES] = power * grown[h] + own
-
-        for tile in range(tiles_for(cols)):
-            finish(tile * SUBLANES)
-            copies[1 - which][tile].start()
-
+        sums[i * SUBLANES : (i + 1) * SUBLANES, :] = packed
     for copy in sum(copies, []):
         copy.wait()
 
@@ -356,9 +342,6 @@
         jnp.pad(prediction, ((0, rows), none, none)) + jnp.pad(vessel_mask, ((rows, 0), none, none)).astype(jnp.float32)
     )
     gx, gy = lax.axis_size("gx"), lax.axis_size("gy")
-    place = jnp.stack(
-        [lax.axis_index("gx") * rows, lax.axis_index("gy") * cols, jnp.int32(gx * rows), jnp.int32(gy * cols)]
-    ).astype(jnp.int32)
     pred_ext, mask_ext = with_halo(packed, rows)
 
     def held(width, margin=2):
@@ -375,7 +358,7 @@
         + [held(REACH - k) for k in range(LEVELS + 1)]
         + [held(REACH - k) for k in range(1, LEVELS + 1)]
         + [held(0)] * 4
-        + [pltpu.VMEM((3, rows, cols, depth), jnp.float32), pltpu.VMEM((gx * gy * 4, LANES), jnp.float32), pltpu.SemaphoreType.DMA((4, tiles_for(cols)))]
+        + [pltpu.VMEM((3, rows, cols, depth), jnp.float32), pltpu.SemaphoreType.DMA((3, tiles_for(cols)))]
     )
     block = jax.ShapeDtypeStruct((rows, cols, depth), jnp.float32)
     vmem = pl.BlockSpec(memory_space=pltpu.VMEM)
@@ -383,12 +366,12 @@
     results, sums = pl.pallas_call(
         lambda *refs: skeleton_kernel(rows, cols, *refs),
         out_shape=[jax.ShapeDtypeStruct((KEPT, rows, cols, depth), jnp.float32), jax.ShapeDtypeStruct((gx * gy * 4, LANES), jnp.float32)],
-        in_specs=[smem, vmem, vmem, vmem],
-        out_specs=[pl.BlockSpec(memory_space=pltpu.HBM)] * 2,
+        in_specs=[vmem, vmem, vmem],
+        out_specs=[pl.BlockSpec(memory_space=pltpu.HBM), vmem],
         scratch_shapes=scratch,
         compiler_params=pltpu.CompilerParams(vmem_limit_bytes=VMEM_BYTES),
         name="skeleton",
-    )(place, packed[:rows], pred_ext, mask_ext)
+    )(packed[:rows], pred_ext, mask_ext)
     got = lax.all_to_all(sums, ("gx", "gy"), 0, 0, tiled=True)
     gradient, loss = pl.pallas_call(
         lambda *refs: combine_kernel(float(gx * rows * gy * cols * depth), *refs),

time: 48.8 us -> 48 us (0.984)
  Pallas kernels: 11.2 us -> 10.3 us
    pallas_call x1, Pallas kernels: 9.42 us -> 8.57 us  [local(): pl.pallas_call(lambda *refs: skeleton_kernel(rows, cols, *refs), out_shap...]
where the time goes in v7:
time: 48 us; the launch traced here: 47.7 us
  blocking collectives  17.3 us (36%)
  starting transfers between devices  10.9 us (23%)
  Pallas kernels  10.3 us (21%)
  waiting for transfers between devices  6.31 us (13%)
  other arithmetic  1.45 us (3%)
  between operations  0.95 us (2%)
  local copies, waits for them, and re-layouts  0.53 us (1%)
    all_to_all x1, blocking collectives, local(): got = lax.all_to_all(sums, ('gx', 'gy'), 0, 0, tiled=True)  17.3 us
    ppermute x6, starting transfers between devices, moved(): return lax.ppermute(block, axis, pairs)  10.9 us
    pallas_call x1, Pallas kernels, local(): pl.pallas_call(lambda *refs: skeleton_kernel(rows, cols, *refs), out_shap...  8.57 us
    ppermute x6, waiting for transfers between devices, moved(): return lax.ppermute(block, axis, pairs)  6.31 us
    pallas_call x1, Pallas kernels, local(): pl.pallas_call(lambda *refs: combine_kernel(float(gx * rows * gy * cols *...  1.77 us
    add x1, other arithmetic, local(): jnp.pad(prediction, ((0, rows), none, none))  0.99 us
  transfers between devices with their start and end apart: 6, of which 2 were waited for; matrix products, arithmetic and copies ran while one was open for 0% of the time, Pallas kernels for 0%

profile of v7, /device:TPU:0, one launch (start us, length us, event | category | flops | bytes accessed | tf_op | source)
XLA Modules:
  0.0 47.7 jit_solution(2624728173880227094)
XLA Ops:
  0.6 1.0 %convert_add_fusion = f32[16,16,256]{2,1,0:T(8,128)S(1)} fusion(s32[8,16,256]{2,1,0:T(8,128)} %param.3, f32[8,16,256]{2,1,0:T(8,128)} %param.2), kind=kLoop, calls=%fused_computation.12 | loop fusion | flops 131072 | bytes 524288 | tf_op jit(solution)/shard_map/add | solution.py:342
  1.7 3.0 %collective-permute-start = (f32[13,16,256]{2,1,0:T(8,128)S(1)}, f32[13,16,256]{2,1,0:T(8,128)S(1)}, u32[]{:S(2)}, u32[]{:S(2)}) collective-permute-start(f32[13,16,256]{2,1,0:T(8,128)S(1)} %get-tuple-element.16), channel_id=1, source_target_pairs={{0,4},{4,0},{8,12},{12,8},{16,20},{20,16},{24,28},{28,24},{1,5},{5... | collective-permute-start | bytes 638984 | tf_op jit(solution)/shard_map/ppermute | solution.py:17
  4.8 0.7 %collective-permute-start.1 = (f32[13,16,256]{2,1,0:T(8,128)S(1)}, f32[13,16,256]{2,1,0:T(8,128)S(1)}, u32[]{:S(2)}, u32[]{:S(2)}) collective-permute-start(f32[13,16,256]{2,1,0:T(8,128)S(1)} %get-tuple-element.17), channel_id=1, source_target_pairs={{4,8},{8,4},{12,16},{16,12},{20,24},{24,20},{5,9},{9,5},{13,17},{1... | collective-permute-start | bytes 638984 | tf_op jit(solution)/shard_map/ppermute | solution.py:17
  5.4 2.9 %collective-permute-start.2 = (f32[2,16,256]{2,1,0:T(8,128)S(1)}, f32[2,16,256]{2,1,0:T(8,128)S(1)}, u32[]{:S(2)}, u32[]{:S(2)}) collective-permute-start(f32[2,16,256]{2,1,0:T(8,128)S(1)} %get-tuple-element.18), channel_id=1, source_target_pairs={{0,8},{4,12},{8,0},{12,4},{16,24},{20,28},{24,16},{28,20},{1,9},{5... | collective-permute-start | bytes 98312 | tf_op jit(solution)/shard_map/ppermute | solution.py:17
  8.3 0.7 %collective-permute-start.3 = (f32[2,16,256]{2,1,0:T(8,128)S(1)}, f32[2,16,256]{2,1,0:T(8,128)S(1)}, u32[]{:S(2)}, u32[]{:S(2)}) collective-permute-start(f32[2,16,256]{2,1,0:T(8,128)S(1)} %get-tuple-element.19), channel_id=1, source_target_pairs={{8,16},{12,20},{16,8},{20,12},{9,17},{13,21},{17,9},{21,13},{10,18... | collective-permute-start | bytes 98312 | tf_op jit(solution)/shard_map/ppermute | solution.py:17
  9.0 5.0 %collective-permute-done.2 = f32[2,16,256]{2,1,0:T(8,128)S(1)} collective-permute-done((f32[2,16,256]{2,1,0:T(8,128)S(1)}, f32[2,16,256]{2,1,0:T(8,128)S(1)}, u32[]{:S(2)}, u32[]{:S(2)}) %collective-permute-start.2) | collective-permute-done | bytes 32800 | tf_op jit(solution)/shard_map/ppermute | solution.py:17
  13.9 0.0 collective-permute-done.3
  13.9 0.0 collective-permute-done
  13.9 0.0 collective-permute-done.1
  14.2 0.1 fusion.5
  14.5 0.1 broadcast_select_fusion.2
  14.6 0.7 %collective-permute-start.5 = (f32[370,256]{1,0:T(8,128)S(1)}, f32[370,256]{1,0:T(8,128)S(1)}, u32[]{:S(2)}, u32[]{:S(2)}) collective-permute-start(f32[370,256]{1,0:T(8,128)S(1)} %get-tuple-element.32), channel_id=1, source_target_pairs={{1,2},{2,1},{5,6},{6,5},{9,10},{10,9},{13,14},{14,13},{17,18},{18,... | collective-permute-start | bytes 1136648 | tf_op jit(solution)/shard_map/ppermute | solution.py:17
  15.3 3.0 %collective-permute-start.4 = (f32[370,256]{1,0:T(8,128)S(1)}, f32[370,256]{1,0:T(8,128)S(1)}, u32[]{:S(2)}, u32[]{:S(2)}) collective-permute-start(f32[370,256]{1,0:T(8,128)S(1)} %get-tuple-element.33), channel_id=1, source_target_pairs={{0,1},{1,0},{2,3},{3,2},{4,5},{5,4},{6,7},{7,6},{8,9},{9,8},{10,11... | collective-permute-start | bytes 1136648 | tf_op jit(solution)/shard_map/ppermute | solution.py:17
  18.3 0.0 collective-permute-done.5
  18.3 1.3 %collective-permute-done.4 = f32[370,256]{1,0:T(8,128)S(1)} collective-permute-done((f32[370,256]{1,0:T(8,128)S(1)}, f32[370,256]{1,0:T(8,128)S(1)}, u32[]{:S(2)}, u32[]{:S(2)}) %collective-permute-start.4) | collective-permute-done | bytes 378912 | tf_op jit(solution)/shard_map/ppermute | solution.py:17
  19.6 0.1 broadcast_select_fusion.1
  19.9 0.1 select_maximum_fusion.2.refs_2_
  20.0 0.1 select_maximum_fusion.refs_1_
  20.1 8.6 %skeleton.1 = (f32[210,8,16,256]{3,2,1,0:T(8,128)}, f32[128,128]{1,0:T(8,128)S(1)}) custom-call(f32[8,16,256]{2,1,0:T(8,128)S(1)} %slice.75.refs_0_, f32[28,40,256]{2,1,0:T(8,128)S(1)} %select_maximum_fusion.refs_1_, f32[18,32,256]{2,1,0:T(8,128)S(1)} %select_maximum_fusion.2.refs_2_), custom_call_target="tpu_custom_call" | custom-call | tf_op jit(solution)/shard_map/skeleton/pallas_call | solution.py:366
  28.7 17.3 %all_to_all.11 = f32[32,4,128]{2,1,0:T(4,128)} all-to-all(f32[32,4,128]{2,1,0:T(4,128)S(1)} %bitcast.3), channel_id=1, replica_groups=mesh['gx'=8,'gy'=4] {'gx','gy'}, dimensions={0} | all-to-all | bytes 131072 | tf_op jit(solution)/shard_map/all_to_all | solution.py:375
  46.0 1.8 %combine.1 = (f32[8,16,256]{2,1,0:T(8,128)}, f32[1]{0:T(128)}) custom-call(f32[128,128]{1,0:T(8,128)} %bitcast.4, f32[210,8,16,256]{3,2,1,0:T(8,128)} %get-tuple-element.27.refs_1_), custom_call_target="tpu_custom_call" | custom-call | tf_op jit(solution)/shard_map/combine/pallas_call | solution.py:376
  (29 shorter events, 0.6 us)
Async XLA Ops:
  1.7 12.2 %collective-permute-start = (f32[13,16,256]{2,1,0:T(8,128)S(1)}, f32[13,16,256]{2,1,0:T(8,128)S(1)}, u32[]{:S(2)}, u32[]{:S(2)}) collective-permute-start(f32[13,16,256]{2,1,0:T(8,128)S(1)} %get-tuple-element.16), channel_id=1, source_target_pairs={{0,4},{4,0},{8,12},{12,8},{16,20},{20,16},{24,28},{28,24},{1,5},{5... | collective-permute-start | bytes 638984 | tf_op jit(solution)/shard_map/ppermute | solution.py:17
  4.8 9.2 %collective-permute-start.1 = (f32[13,16,256]{2,1,0:T(8,128)S(1)}, f32[13,16,256]{2,1,0:T(8,128)S(1)}, u32[]{:S(2)}, u32[]{:S(2)}) collective-permute-start(f32[13,16,256]{2,1,0:T(8,128)S(1)} %get-tuple-element.17), channel_id=1, source_target_pairs={{4,8},{8,4},{12,16},{16,12},{20,24},{24,20},{5,9},{9,5},{13,17},{1... | collective-permute-start | bytes 638984 | tf_op jit(solution)/shard_map/ppermute | solution.py:17
  5.4 8.5 %collective-permute-start.2 = (f32[2,16,256]{2,1,0:T(8,128)S(1)}, f32[2,16,256]{2,1,0:T(8,128)S(1)}, u32[]{:S(2)}, u32[]{:S(2)}) collective-permute-start(f32[2,16,256]{2,1,0:T(8,128)S(1)} %get-tuple-element.18), channel_id=1, source_target_pairs={{0,8},{4,12},{8,0},{12,4},{16,24},{20,28},{24,16},{28,20},{1,9},{5... | collective-permute-start | bytes 98312 | tf_op jit(solution)/shard_map/ppermute | solution.py:17
  8.3 5.6 %collective-permute-start.3 = (f32[2,16,256]{2,1,0:T(8,128)S(1)}, f32[2,16,256]{2,1,0:T(8,128)S(1)}, u32[]{:S(2)}, u32[]{:S(2)}) collective-permute-start(f32[2,16,256]{2,1,0:T(8,128)S(1)} %get-tuple-element.19), channel_id=1, source_target_pairs={{8,16},{12,20},{16,8},{20,12},{9,17},{13,21},{17,9},{21,13},{10,18... | collective-permute-start | bytes 98312 | tf_op jit(solution)/shard_map/ppermute | solution.py:17
  14.6 3.7 %collective-permute-start.5 = (f32[370,256]{1,0:T(8,128)S(1)}, f32[370,256]{1,0:T(8,128)S(1)}, u32[]{:S(2)}, u32[]{:S(2)}) collective-permute-start(f32[370,256]{1,0:T(8,128)S(1)} %get-tuple-element.32), channel_id=1, source_target_pairs={{1,2},{2,1},{5,6},{6,5},{9,10},{10,9},{13,14},{14,13},{17,18},{18,... | collective-permute-start | bytes 1136648 | tf_op jit(solution)/shard_map/ppermute | solution.py:17
  15.3 4.3 %collective-permute-start.4 = (f32[370,256]{1,0:T(8,128)S(1)}, f32[370,256]{1,0:T(8,128)S(1)}, u32[]{:S(2)}, u32[]{:S(2)}) collective-permute-start(f32[370,256]{1,0:T(8,128)S(1)} %get-tuple-element.33), channel_id=1, source_target_pairs={{0,1},{1,0},{2,3},{3,2},{4,5},{5,4},{6,7},{7,6},{8,9},{9,8},{10,11... | collective-permute-start | bytes 1136648 | tf_op jit(solution)/shard_map/ppermute | solution.py:17

commit v8 on v7

--- a/solution.py
+++ b/solution.py
@@ -46,10 +46,8 @@
     tall, short = tall_pred.shape[0], tall_mask.shape[0]
 
     def side(p, m):
-        return jnp.concatenate([p.reshape(tall * wide, -1), m.reshape(short * thin, -1)], 0)
-
-    def unside(b):
-        return b[: tall * wide].reshape(tall, wide, -1), b[tall * wide :].reshape(short, thin, -1)
+        flat = jnp.concatenate([p.reshape(tall * wide, -1), m.reshape(short * thin, -1)], 0)
+        return jnp.pad(flat, ((0, -flat.shape[0] % SUBLANES), (0, 0)))
 
     col_odd = lax.rem(lax.axis_index("gy"), 2) == 1
     high = side(tall_pred[:, -wide:], tall_mask[:, -thin:])
@@ -57,14 +55,7 @@
     first = moved(jnp.where(col_odd, low, high), "gy", lambda i: i ^ 1)
     second = moved(jnp.where(col_odd, high, low), "gy", lambda i: i + 1 if i % 2 else i - 1)
     first, second = lax.optimization_barrier((first, second))
-    left_pred, left_mask = unside(jnp.where(col_odd, first, second))
-    right_pred, right_mask = unside(jnp.where(col_odd, second, first))
-
-    def framed(parts):
-        count = sum(p.shape[1] for p in parts)
-        return jnp.pad(jnp.concatenate(parts, 1), ((0, 0), (0, tiles_for(count) * SUBLANES - count), (0, 0)))
-
-    return framed([left_pred, tall_pred, right_pred]), framed([left_mask, tall_mask, right_mask])
+    return tall_pred, tall_mask, jnp.where(col_odd, first, second), jnp.where(col_odd, second, first)
 
 
 WIDE = 2 * REACH
@@ -109,7 +100,7 @@
     lax.fori_loop(0, tiles_for(count), body, 0, unroll=True)
 
 
-def skeleton_kernel(rows, cols, own_pred, pred, label, results, sums, *scratch):
+def skeleton_kernel(rows, cols, own_pred, pred, label, left, right, results, sums, *scratch):
     t = softness_factor
     scratch = list(scratch)
     stage, copied = scratch[48:]
@@ -143,18 +134,28 @@
         row = row0 + (x - width)
         return jnp.where((row >= 0) & (row < row_count), col_count, 0)
 
-    def raise_field(field, powers, inverses, width, kept=None):
-        def start(base):
-            index = column_index(base, width)
-            for x in range(rows + 2 * width):
-                ok = index < column_limit(x, width)
+    def raise_field(middle, offset, powers, inverses, width, kept=None):
+        last_tile = max(width - SUBLANES, 0)
+        sides = (0, last_tile) if last_tile else (0,)
+        tiles = [(at, left, at) for at in sides]
+        tiles += [(width + at, None, at) for at in range(0, cols, SUBLANES)]
+        tiles += [(width + cols + at, right, at) for at in sides]
+        indices = [column_index(base, width) for base, _, _ in tiles]
+        for x in range(rows + 2 * width):
+            limit = column_limit(x, width)
+            for (base, source, at), index in zip(tiles, indices):
+                ok = index < limit
                 for h in range(2):
-                    value = field[x, pl.ds(base, SUBLANES), h * LANES : (h + 1) * LANES]
+                    half = slice(h * LANES, (h + 1) * LANES)
+                    if source is None:
+                        value = middle[x, at : at + SUBLANES, half]
+                    else:
+                        row = offset + x * width + at
+                        value = source[row : row + SUBLANES, half]
                     if kept is not None:
                         kept[x, h, pl.ds(base, SUBLANES), :] = value
                     powers[0][x, h, pl.ds(base, SUBLANES), :] = jnp.where(ok, jnp.exp(value * (-1.0 / t)), 0.0)
 
-        over_tiles(cols + 2 * width, start)
         for level in range(1, LEVELS + 1):
             here = width - level
 
@@ -201,7 +202,7 @@
                 skel = skel + jnp.log(grown)
         return skel, saved
 
-    raise_field(label, label_powers, label_inverses, REACH, labels)
+    raise_field(label, (rows + 2 * WIDE) * WIDE, label_powers, label_inverses, REACH, labels)
     open_field(label_inverses, label_opened, REACH, 0)
 
     def label_chain(base):
@@ -217,7 +218,7 @@
     for copy in copies[2]:
         copy.start()
 
-    raise_field(pred, powers, inverses, WIDE)
+    raise_field(pred, 0, powers, inverses, WIDE)
     open_field(inverses, opened, WIDE, REACH)
 
     def chain_tile(base):
@@ -342,7 +343,7 @@
         jnp.pad(prediction, ((0, rows), none, none)) + jnp.pad(vessel_mask, ((rows, 0), none, none)).astype(jnp.float32)
     )
     gx, gy = lax.axis_size("gx"), lax.axis_size("gy")
-    pred_ext, mask_ext = with_halo(packed, rows)
+    halo = with_halo(packed, rows)
 
     def held(width, margin=2):
         return pltpu.VMEM((rows + 2 * width, 2, tiles_for(cols + 2 * width + margin + 6) * SUBLANES, LANES), jnp.float32)
@@ -366,12 +367,12 @@
     results, sums = pl.pallas_call(
         lambda *refs: skeleton_kernel(rows, cols, *refs),
         out_shape=[jax.ShapeDtypeStruct((KEPT, rows, cols, depth), jnp.float32), jax.ShapeDtypeStruct((gx * gy * 4, LANES), jnp.float32)],
-        in_specs=[vmem, vmem, vmem],
+        in_specs=[vmem] * 5,
         out_specs=[pl.BlockSpec(memory_space=pltpu.HBM), vmem],
         scratch_shapes=scratch,
         compiler_params=pltpu.CompilerParams(vmem_limit_bytes=VMEM_BYTES),
         name="skeleton",
-    )(packed[:rows], pred_ext, mask_ext)
+    )(packed[:rows], *halo)
     got = lax.all_to_all(sums, ("gx", "gy"), 0, 0, tiled=True)
     gradient, loss = pl.pallas_call(
         lambda *refs: combine_kernel(float(gx * rows * gy * cols * depth), *refs),

time: 48 us -> 47.8 us (level)
  Pallas kernels: 10.3 us -> 10.8 us
where the time goes in v8:
time: 47.8 us; the launch traced here: 47.6 us
  blocking collectives  17.3 us (36%)
  starting transfers between devices  10.9 us (23%)
  Pallas kernels  10.8 us (23%)
  waiting for transfers between devices  6.31 us (13%)
  other arithmetic  1.22 us (3%)
  between operations  0.85 us (2%)
    all_to_all x1, blocking collectives, local(): got = lax.all_to_all(sums, ('gx', 'gy'), 0, 0, tiled=True)  17.3 us
    ppermute x6, starting transfers between devices, moved(): return lax.ppermute(block, axis, pairs)  10.9 us
    pallas_call x1, Pallas kernels, local(): pl.pallas_call(lambda *refs: skeleton_kernel(rows, cols, *refs), out_shap...  9 us
    ppermute x6, waiting for transfers between devices, moved(): return lax.ppermute(block, axis, pairs)  6.31 us
    pallas_call x1, Pallas kernels, local(): pl.pallas_call(lambda *refs: combine_kernel(float(gx * rows * gy * cols *...  1.77 us
    add x1, other arithmetic, local(): jnp.pad(prediction, ((0, rows), none, none))  0.99 us
  transfers between devices with their start and end apart: 6, of which 2 were waited for; matrix products, arithmetic and copies ran while one was open for 0% of the time, Pallas kernels for 0%

profile of v8, /device:TPU:0, one launch (start us, length us, event | category | flops | bytes accessed | tf_op | source)
XLA Modules:
  0.0 47.6 jit_solution(12467699007304659095)
XLA Ops:
  0.6 1.0 %convert_add_fusion = f32[16,16,256]{2,1,0:T(8,128)S(1)} fusion(s32[8,16,256]{2,1,0:T(8,128)} %param.3, f32[8,16,256]{2,1,0:T(8,128)} %param.2), kind=kLoop, calls=%fused_computation.4 | loop fusion | flops 131072 | bytes 524288 | tf_op jit(solution)/shard_map/add | solution.py:343
  1.7 3.0 %collective-permute-start = (f32[13,16,256]{2,1,0:T(8,128)S(1)}, f32[13,16,256]{2,1,0:T(8,128)S(1)}, u32[]{:S(2)}, u32[]{:S(2)}) collective-permute-start(f32[13,16,256]{2,1,0:T(8,128)S(1)} %get-tuple-element.16), channel_id=1, source_target_pairs={{0,4},{4,0},{8,12},{12,8},{16,20},{20,16},{24,28},{28,24},{1,5},{5... | collective-permute-start | bytes 638984 | tf_op jit(solution)/shard_map/ppermute | solution.py:17
  4.8 0.7 %collective-permute-start.1 = (f32[13,16,256]{2,1,0:T(8,128)S(1)}, f32[13,16,256]{2,1,0:T(8,128)S(1)}, u32[]{:S(2)}, u32[]{:S(2)}) collective-permute-start(f32[13,16,256]{2,1,0:T(8,128)S(1)} %get-tuple-element.17), channel_id=1, source_target_pairs={{4,8},{8,4},{12,16},{16,12},{20,24},{24,20},{5,9},{9,5},{13,17},{1... | collective-permute-start | bytes 638984 | tf_op jit(solution)/shard_map/ppermute | solution.py:17
  5.4 2.9 %collective-permute-start.2 = (f32[2,16,256]{2,1,0:T(8,128)S(1)}, f32[2,16,256]{2,1,0:T(8,128)S(1)}, u32[]{:S(2)}, u32[]{:S(2)}) collective-permute-start(f32[2,16,256]{2,1,0:T(8,128)S(1)} %get-tuple-element.18), channel_id=1, source_target_pairs={{0,8},{4,12},{8,0},{12,4},{16,24},{20,28},{24,16},{28,20},{1,9},{5... | collective-permute-start | bytes 98312 | tf_op jit(solution)/shard_map/ppermute | solution.py:17
  8.3 0.7 %collective-permute-start.3 = (f32[2,16,256]{2,1,0:T(8,128)S(1)}, f32[2,16,256]{2,1,0:T(8,128)S(1)}, u32[]{:S(2)}, u32[]{:S(2)}) collective-permute-start(f32[2,16,256]{2,1,0:T(8,128)S(1)} %get-tuple-element.19), channel_id=1, source_target_pairs={{8,16},{12,20},{16,8},{20,12},{9,17},{13,21},{17,9},{21,13},{10,18... | collective-permute-start | bytes 98312 | tf_op jit(solution)/shard_map/ppermute | solution.py:17
  9.0 5.0 %collective-permute-done.2 = f32[2,16,256]{2,1,0:T(8,128)S(1)} collective-permute-done((f32[2,16,256]{2,1,0:T(8,128)S(1)}, f32[2,16,256]{2,1,0:T(8,128)S(1)}, u32[]{:S(2)}, u32[]{:S(2)}) %collective-permute-start.2) | collective-permute-done | bytes 32800 | tf_op jit(solution)/shard_map/ppermute | solution.py:17
  13.9 0.0 collective-permute-done.3
  13.9 0.0 collective-permute-done
  13.9 0.0 collective-permute-done.1
  14.2 0.1 fusion.2
  14.4 0.1 fusion.1
  14.5 0.7 %collective-permute-start.5 = (f32[376,256]{1,0:T(8,128)S(1)}, f32[376,256]{1,0:T(8,128)S(1)}, u32[]{:S(2)}, u32[]{:S(2)}) collective-permute-start(f32[376,256]{1,0:T(8,128)S(1)} %get-tuple-element.32), channel_id=1, source_target_pairs={{1,2},{2,1},{5,6},{6,5},{9,10},{10,9},{13,14},{14,13},{17,18},{18,... | collective-permute-start | bytes 1155080 | tf_op jit(solution)/shard_map/ppermute | solution.py:17
  15.2 3.0 %collective-permute-start.4 = (f32[376,256]{1,0:T(8,128)S(1)}, f32[376,256]{1,0:T(8,128)S(1)}, u32[]{:S(2)}, u32[]{:S(2)}) collective-permute-start(f32[376,256]{1,0:T(8,128)S(1)} %get-tuple-element.33), channel_id=1, source_target_pairs={{0,1},{1,0},{2,3},{3,2},{4,5},{5,4},{6,7},{7,6},{8,9},{9,8},{10,11... | collective-permute-start | bytes 1155080 | tf_op jit(solution)/shard_map/ppermute | solution.py:17
  18.2 0.0 collective-permute-done.5
  18.2 1.3 %collective-permute-done.4 = f32[376,256]{1,0:T(8,128)S(1)} collective-permute-done((f32[376,256]{1,0:T(8,128)S(1)}, f32[376,256]{1,0:T(8,128)S(1)}, u32[]{:S(2)}, u32[]{:S(2)}) %collective-permute-start.4) | collective-permute-done | bytes 385056 | tf_op jit(solution)/shard_map/ppermute | solution.py:17
  19.5 0.1 broadcast_select_fusion
  19.6 9.0 %skeleton.1 = (f32[210,8,16,256]{3,2,1,0:T(8,128)}, f32[128,128]{1,0:T(8,128)S(1)}) custom-call(f32[8,16,256]{2,1,0:T(8,128)S(1)} %slice.59.refs_0_, f32[28,16,256]{2,1,0:T(8,128)S(1)} %select_dynamic-update-slice_fusion.refs_1_, f32[18,16,256]{2,1,0:T(8,128)S(1)} %pad_maximum_fusion.refs_2_, f32[376,256]{1,0:T(8,128)S(1)} %get-tuple-element.31.refs_3_, ...), custom_call_target="tpu_custom_call" | custom-call | tf_op jit(solution)/shard_map/skeleton/pallas_call | solution.py:367
  28.6 17.3 %all_to_all.11 = f32[32,4,128]{2,1,0:T(4,128)} all-to-all(f32[32,4,128]{2,1,0:T(4,128)S(1)} %bitcast.3), channel_id=1, replica_groups=mesh['gx'=8,'gy'=4] {'gx','gy'}, dimensions={0} | all-to-all | bytes 131072 | tf_op jit(solution)/shard_map/all_to_all | solution.py:376
  45.8 1.8 %combine.1 = (f32[8,16,256]{2,1,0:T(8,128)}, f32[1]{0:T(128)}) custom-call(f32[128,128]{1,0:T(8,128)} %bitcast.4, f32[210,8,16,256]{3,2,1,0:T(8,128)} %get-tuple-element.27.refs_1_), custom_call_target="tpu_custom_call" | custom-call | tf_op jit(solution)/shard_map/combine/pallas_call | solution.py:377
  (18 shorter events, 0.3 us)
Async XLA Ops:
  1.7 12.2 %collective-permute-start = (f32[13,16,256]{2,1,0:T(8,128)S(1)}, f32[13,16,256]{2,1,0:T(8,128)S(1)}, u32[]{:S(2)}, u32[]{:S(2)}) collective-permute-start(f32[13,16,256]{2,1,0:T(8,128)S(1)} %get-tuple-element.16), channel_id=1, source_target_pairs={{0,4},{4,0},{8,12},{12,8},{16,20},{20,16},{24,28},{28,24},{1,5},{5... | collective-permute-start | bytes 638984 | tf_op jit(solution)/shard_map/ppermute | solution.py:17
  4.8 9.2 %collective-permute-start.1 = (f32[13,16,256]{2,1,0:T(8,128)S(1)}, f32[13,16,256]{2,1,0:T(8,128)S(1)}, u32[]{:S(2)}, u32[]{:S(2)}) collective-permute-start(f32[13,16,256]{2,1,0:T(8,128)S(1)} %get-tuple-element.17), channel_id=1, source_target_pairs={{4,8},{8,4},{12,16},{16,12},{20,24},{24,20},{5,9},{9,5},{13,17},{1... | collective-permute-start | bytes 638984 | tf_op jit(solution)/shard_map/ppermute | solution.py:17
  5.4 8.5 %collective-permute-start.2 = (f32[2,16,256]{2,1,0:T(8,128)S(1)}, f32[2,16,256]{2,1,0:T(8,128)S(1)}, u32[]{:S(2)}, u32[]{:S(2)}) collective-permute-start(f32[2,16,256]{2,1,0:T(8,128)S(1)} %get-tuple-element.18), channel_id=1, source_target_pairs={{0,8},{4,12},{8,0},{12,4},{16,24},{20,28},{24,16},{28,20},{1,9},{5... | collective-permute-start | bytes 98312 | tf_op jit(solution)/shard_map/ppermute | solution.py:17
  8.3 5.6 %collective-permute-start.3 = (f32[2,16,256]{2,1,0:T(8,128)S(1)}, f32[2,16,256]{2,1,0:T(8,128)S(1)}, u32[]{:S(2)}, u32[]{:S(2)}) collective-permute-start(f32[2,16,256]{2,1,0:T(8,128)S(1)} %get-tuple-element.19), channel_id=1, source_target_pairs={{8,16},{12,20},{16,8},{20,12},{9,17},{13,21},{17,9},{21,13},{10,18... | collective-permute-start | bytes 98312 | tf_op jit(solution)/shard_map/ppermute | solution.py:17
  14.5 3.7 %collective-permute-start.5 = (f32[376,256]{1,0:T(8,128)S(1)}, f32[376,256]{1,0:T(8,128)S(1)}, u32[]{:S(2)}, u32[]{:S(2)}) collective-permute-start(f32[376,256]{1,0:T(8,128)S(1)} %get-tuple-element.32), channel_id=1, source_target_pairs={{1,2},{2,1},{5,6},{6,5},{9,10},{10,9},{13,14},{14,13},{17,18},{18,... | collective-permute-start | bytes 1155080 | tf_op jit(solution)/shard_map/ppermute | solution.py:17
  15.2 4.3 %collective-permute-start.4 = (f32[376,256]{1,0:T(8,128)S(1)}, f32[376,256]{1,0:T(8,128)S(1)}, u32[]{:S(2)}, u32[]{:S(2)}) collective-permute-start(f32[376,256]{1,0:T(8,128)S(1)} %get-tuple-element.33), channel_id=1, source_target_pairs={{0,1},{1,0},{2,3},{3,2},{4,5},{5,4},{6,7},{7,6},{8,9},{9,8},{10,11... | collective-permute-start | bytes 1155080 | tf_op jit(solution)/shard_map/ppermute | solution.py:17

commit v9 on v8

--- a/solution.py
+++ b/solution.py
@@ -61,6 +61,7 @@
 WIDE = 2 * REACH
 LANES = 128
 SUBLANES = 8
+SHARE = LANES // 4
 VMEM_BYTES = 40 * 1024 * 1024
 KEPT = 210
 
@@ -306,7 +307,9 @@
                 totals[2] += other * own_pred[x, pl.ds(base, SUBLANES), half]
                 totals[3] += other
     totals = [jnp.sum(jnp.sum(v, 0, keepdims=True), 1, keepdims=True) for v in totals]
-    packed = jnp.broadcast_to(jnp.concatenate(totals * 2, 0), (SUBLANES, LANES))
+    packed = jnp.zeros((SUBLANES, LANES), jnp.float32)
+    for i, total in enumerate(totals):
+        packed = jnp.where(lane // SHARE == i, total, packed)
     for i in range(sums.shape[0] // SUBLANES):
         sums[i * SUBLANES : (i + 1) * SUBLANES, :] = packed
     for copy in sum(copies, []):
@@ -317,8 +320,11 @@
     total = jnp.zeros((SUBLANES, LANES), jnp.float32)
     for i in range(got.shape[0] // SUBLANES):
         total += got[i * SUBLANES : (i + 1) * SUBLANES, :]
-    total = total + pltpu.roll(total, 4, 0)
-    intersection_pred, mass_pred, intersection_mask, mass_mask = (total[i : i + 1] + 1.0 for i in range(4))
+    total = jnp.sum(total, 0, keepdims=True)
+    share = lax.broadcasted_iota(jnp.int32, (1, LANES), 1) // SHARE
+    intersection_pred, mass_pred, intersection_mask, mass_mask = (
+        jnp.sum(jnp.where(share == i, total, 0.0), 1, keepdims=True) * (1.0 / SHARE) + 1.0 for i in range(4)
+    )
     precision = intersection_pred / mass_pred
     sensitivity = intersection_mask / mass_mask
     paired = precision + sensitivity
@@ -329,7 +335,7 @@
     coef_mass = -coef_intersection * precision
     coef_cross = cells * slope_sens / mass_mask
     a, b, c = (
-        jnp.broadcast_to(jnp.concatenate([v, v], 1), (gradient.shape[1], 2 * LANES))
+        jnp.broadcast_to(v, (gradient.shape[1], 2 * LANES))
         for v in (coef_intersection, coef_mass, coef_cross)
     )
     for x in range(gradient.shape[0]):
@@ -366,7 +372,7 @@
     smem = pl.BlockSpec(memory_space=pltpu.SMEM)
     results, sums = pl.pallas_call(
         lambda *refs: skeleton_kernel(rows, cols, *refs),
-        out_shape=[jax.ShapeDtypeStruct((KEPT, rows, cols, depth), jnp.float32), jax.ShapeDtypeStruct((gx * gy * 4, LANES), jnp.float32)],
+        out_shape=[jax.ShapeDtypeStruct((KEPT, rows, cols, depth), jnp.float32), jax.ShapeDtypeStruct((gx * gy, LANES), jnp.float32)],
         in_specs=[vmem] * 5,
         out_specs=[pl.BlockSpec(memory_space=pltpu.HBM), vmem],
         scratch_shapes=scratch,

time: 47.8 us -> 47.7 us (level)
  no operation moved by 1% of the time
where the time goes in v9:
time: 47.7 us; the launch traced here: 47.4 us
  blocking collectives  17 us (36%)
  starting transfers between devices  10.9 us (23%)
  Pallas kernels  10.9 us (23%)
  waiting for transfers between devices  6.31 us (13%)
  other arithmetic  1.22 us (3%)
  between operations  0.85 us (2%)
    all_to_all x1, blocking collectives, local(): got = lax.all_to_all(sums, ('gx', 'gy'), 0, 0, tiled=True)  17 us
    ppermute x6, starting transfers between devices, moved(): return lax.ppermute(block, axis, pairs)  10.9 us
    pallas_call x1, Pallas kernels, local(): pl.pallas_call(lambda *refs: skeleton_kernel(rows, cols, *refs), out_shap...  9.04 us
    ppermute x6, waiting for transfers between devices, moved(): return lax.ppermute(block, axis, pairs)  6.31 us
    pallas_call x1, Pallas kernels, local(): pl.pallas_call(lambda *refs: combine_kernel(float(gx * rows * gy * cols *...  1.82 us
    add x1, other arithmetic, local(): jnp.pad(prediction, ((0, rows), none, none))  0.99 us
  transfers between devices with their start and end apart: 6, of which 2 were waited for; matrix products, arithmetic and copies ran while one was open for 0% of the time, Pallas kernels for 0%

profile of v9, /device:TPU:0, one launch (start us, length us, event | category | flops | bytes accessed | tf_op | source)
XLA Modules:
  0.0 47.4 jit_solution(17140179515147657917)
XLA Ops:
  0.6 1.0 %convert_add_fusion = f32[16,16,256]{2,1,0:T(8,128)S(1)} fusion(s32[8,16,256]{2,1,0:T(8,128)} %param.3, f32[8,16,256]{2,1,0:T(8,128)} %param.2), kind=kLoop, calls=%fused_computation.4 | loop fusion | flops 131072 | bytes 524288 | tf_op jit(solution)/shard_map/add | solution.py:349
  1.7 3.0 %collective-permute-start = (f32[13,16,256]{2,1,0:T(8,128)S(1)}, f32[13,16,256]{2,1,0:T(8,128)S(1)}, u32[]{:S(2)}, u32[]{:S(2)}) collective-permute-start(f32[13,16,256]{2,1,0:T(8,128)S(1)} %get-tuple-element.16), channel_id=1, source_target_pairs={{0,4},{4,0},{8,12},{12,8},{16,20},{20,16},{24,28},{28,24},{1,5},{5... | collective-permute-start | bytes 638984 | tf_op jit(solution)/shard_map/ppermute | solution.py:17
  4.8 0.7 %collective-permute-start.1 = (f32[13,16,256]{2,1,0:T(8,128)S(1)}, f32[13,16,256]{2,1,0:T(8,128)S(1)}, u32[]{:S(2)}, u32[]{:S(2)}) collective-permute-start(f32[13,16,256]{2,1,0:T(8,128)S(1)} %get-tuple-element.17), channel_id=1, source_target_pairs={{4,8},{8,4},{12,16},{16,12},{20,24},{24,20},{5,9},{9,5},{13,17},{1... | collective-permute-start | bytes 638984 | tf_op jit(solution)/shard_map/ppermute | solution.py:17
  5.4 2.9 %collective-permute-start.2 = (f32[2,16,256]{2,1,0:T(8,128)S(1)}, f32[2,16,256]{2,1,0:T(8,128)S(1)}, u32[]{:S(2)}, u32[]{:S(2)}) collective-permute-start(f32[2,16,256]{2,1,0:T(8,128)S(1)} %get-tuple-element.18), channel_id=1, source_target_pairs={{0,8},{4,12},{8,0},{12,4},{16,24},{20,28},{24,16},{28,20},{1,9},{5... | collective-permute-start | bytes 98312 | tf_op jit(solution)/shard_map/ppermute | solution.py:17
  8.3 0.7 %collective-permute-start.3 = (f32[2,16,256]{2,1,0:T(8,128)S(1)}, f32[2,16,256]{2,1,0:T(8,128)S(1)}, u32[]{:S(2)}, u32[]{:S(2)}) collective-permute-start(f32[2,16,256]{2,1,0:T(8,128)S(1)} %get-tuple-element.19), channel_id=1, source_target_pairs={{8,16},{12,20},{16,8},{20,12},{9,17},{13,21},{17,9},{21,13},{10,18... | collective-permute-start | bytes 98312 | tf_op jit(solution)/shard_map/ppermute | solution.py:17
  9.0 5.0 %collective-permute-done.2 = f32[2,16,256]{2,1,0:T(8,128)S(1)} collective-permute-done((f32[2,16,256]{2,1,0:T(8,128)S(1)}, f32[2,16,256]{2,1,0:T(8,128)S(1)}, u32[]{:S(2)}, u32[]{:S(2)}) %collective-permute-start.2) | collective-permute-done | bytes 32800 | tf_op jit(solution)/shard_map/ppermute | solution.py:17
  13.9 0.0 collective-permute-done.3
  13.9 0.0 collective-permute-done
  13.9 0.0 collective-permute-done.1
  14.2 0.1 fusion.2
  14.4 0.1 fusion.1
  14.5 0.7 %collective-permute-start.5 = (f32[376,256]{1,0:T(8,128)S(1)}, f32[376,256]{1,0:T(8,128)S(1)}, u32[]{:S(2)}, u32[]{:S(2)}) collective-permute-start(f32[376,256]{1,0:T(8,128)S(1)} %get-tuple-element.32), channel_id=1, source_target_pairs={{1,2},{2,1},{5,6},{6,5},{9,10},{10,9},{13,14},{14,13},{17,18},{18,... | collective-permute-start | bytes 1155080 | tf_op jit(solution)/shard_map/ppermute | solution.py:17
  15.2 3.0 %collective-permute-start.4 = (f32[376,256]{1,0:T(8,128)S(1)}, f32[376,256]{1,0:T(8,128)S(1)}, u32[]{:S(2)}, u32[]{:S(2)}) collective-permute-start(f32[376,256]{1,0:T(8,128)S(1)} %get-tuple-element.33), channel_id=1, source_target_pairs={{0,1},{1,0},{2,3},{3,2},{4,5},{5,4},{6,7},{7,6},{8,9},{9,8},{10,11... | collective-permute-start | bytes 1155080 | tf_op jit(solution)/shard_map/ppermute | solution.py:17
  18.2 0.0 collective-permute-done.5
  18.2 1.3 %collective-permute-done.4 = f32[376,256]{1,0:T(8,128)S(1)} collective-permute-done((f32[376,256]{1,0:T(8,128)S(1)}, f32[376,256]{1,0:T(8,128)S(1)}, u32[]{:S(2)}, u32[]{:S(2)}) %collective-permute-start.4) | collective-permute-done | bytes 385056 | tf_op jit(solution)/shard_map/ppermute | solution.py:17
  19.5 0.1 broadcast_select_fusion
  19.6 9.0 %skeleton.1 = (f32[210,8,16,256]{3,2,1,0:T(8,128)}, f32[32,128]{1,0:T(8,128)S(1)}) custom-call(f32[8,16,256]{2,1,0:T(8,128)S(1)} %slice.59.refs_0_, f32[28,16,256]{2,1,0:T(8,128)S(1)} %select_dynamic-update-slice_fusion.refs_1_, f32[18,16,256]{2,1,0:T(8,128)S(1)} %pad_maximum_fusion.refs_2_, f32[376,256]{1,0:T(8,128)S(1)} %get-tuple-element.31.refs_3_, ...), custom_call_target="tpu_custom_call" | custom-call | tf_op jit(solution)/shard_map/skeleton/pallas_call | solution.py:373
  28.6 17.0 %all_to_all.11 = f32[32,1,128]{2,1,0:T(1,128)} all-to-all(f32[32,1,128]{2,1,0:T(1,128)S(1)} %bitcast.5), channel_id=1, replica_groups=mesh['gx'=8,'gy'=4] {'gx','gy'}, dimensions={0} | all-to-all | bytes 32768 | tf_op jit(solution)/shard_map/all_to_all | solution.py:382
  45.6 1.8 %combine.1 = (f32[8,16,256]{2,1,0:T(8,128)}, f32[1]{0:T(128)}) custom-call(f32[32,128]{1,0:T(8,128)} %bitcast.6, f32[210,8,16,256]{3,2,1,0:T(8,128)} %get-tuple-element.27.refs_1_), custom_call_target="tpu_custom_call" | custom-call | tf_op jit(solution)/shard_map/combine/pallas_call | solution.py:383
  (18 shorter events, 0.3 us)
Async XLA Ops:
  1.7 12.2 %collective-permute-start = (f32[13,16,256]{2,1,0:T(8,128)S(1)}, f32[13,16,256]{2,1,0:T(8,128)S(1)}, u32[]{:S(2)}, u32[]{:S(2)}) collective-permute-start(f32[13,16,256]{2,1,0:T(8,128)S(1)} %get-tuple-element.16), channel_id=1, source_target_pairs={{0,4},{4,0},{8,12},{12,8},{16,20},{20,16},{24,28},{28,24},{1,5},{5... | collective-permute-start | bytes 638984 | tf_op jit(solution)/shard_map/ppermute | solution.py:17
  4.8 9.2 %collective-permute-start.1 = (f32[13,16,256]{2,1,0:T(8,128)S(1)}, f32[13,16,256]{2,1,0:T(8,128)S(1)}, u32[]{:S(2)}, u32[]{:S(2)}) collective-permute-start(f32[13,16,256]{2,1,0:T(8,128)S(1)} %get-tuple-element.17), channel_id=1, source_target_pairs={{4,8},{8,4},{12,16},{16,12},{20,24},{24,20},{5,9},{9,5},{13,17},{1... | collective-permute-start | bytes 638984 | tf_op jit(solution)/shard_map/ppermute | solution.py:17
  5.4 8.5 %collective-permute-start.2 = (f32[2,16,256]{2,1,0:T(8,128)S(1)}, f32[2,16,256]{2,1,0:T(8,128)S(1)}, u32[]{:S(2)}, u32[]{:S(2)}) collective-permute-start(f32[2,16,256]{2,1,0:T(8,128)S(1)} %get-tuple-element.18), channel_id=1, source_target_pairs={{0,8},{4,12},{8,0},{12,4},{16,24},{20,28},{24,16},{28,20},{1,9},{5... | collective-permute-start | bytes 98312 | tf_op jit(solution)/shard_map/ppermute | solution.py:17
  8.3 5.6 %collective-permute-start.3 = (f32[2,16,256]{2,1,0:T(8,128)S(1)}, f32[2,16,256]{2,1,0:T(8,128)S(1)}, u32[]{:S(2)}, u32[]{:S(2)}) collective-permute-start(f32[2,16,256]{2,1,0:T(8,128)S(1)} %get-tuple-element.19), channel_id=1, source_target_pairs={{8,16},{12,20},{16,8},{20,12},{9,17},{13,21},{17,9},{21,13},{10,18... | collective-permute-start | bytes 98312 | tf_op jit(solution)/shard_map/ppermute | solution.py:17
  14.5 3.7 %collective-permute-start.5 = (f32[376,256]{1,0:T(8,128)S(1)}, f32[376,256]{1,0:T(8,128)S(1)}, u32[]{:S(2)}, u32[]{:S(2)}) collective-permute-start(f32[376,256]{1,0:T(8,128)S(1)} %get-tuple-element.32), channel_id=1, source_target_pairs={{1,2},{2,1},{5,6},{6,5},{9,10},{10,9},{13,14},{14,13},{17,18},{18,... | collective-permute-start | bytes 1155080 | tf_op jit(solution)/shard_map/ppermute | solution.py:17
  15.2 4.3 %collective-permute-start.4 = (f32[376,256]{1,0:T(8,128)S(1)}, f32[376,256]{1,0:T(8,128)S(1)}, u32[]{:S(2)}, u32[]{:S(2)}) collective-permute-start(f32[376,256]{1,0:T(8,128)S(1)} %get-tuple-element.33), channel_id=1, source_target_pairs={{0,1},{1,0},{2,3},{3,2},{4,5},{5,4},{6,7},{7,6},{8,9},{9,8},{10,11... | collective-permute-start | bytes 1155080 | tf_op jit(solution)/shard_map/ppermute | solution.py:17
